TPU v7x, 32 devices: a whole 2x2x4 slice. The times are simulated.
32 devices in a mesh: dp: 4 (over y, x), blk: 8 (over z, core).
Axes of the slice: x: 2, y: 2, z: 4, core: 2. Of those that a mesh axis runs over, the one named last changes fastest.
Arguments:
- tokens: bfloat16 [7168, 2048], P(('dp', 'blk')), may hold values from -6 to 6
- cotangent: bfloat16 [7168, 2048], P(('dp', 'blk')), may hold values from -6 to 6
- document_length_list: int32 [4, 3], P('dp'), may hold values from 1 to 1790, as said below
- attention_norm_gain: float32 [2048], replicated, may hold values from 0.5 to 1.5
- feedforward_norm_gain: float32 [2048], replicated, may hold values from 0.5 to 1.5
- frozen_query_key_value: bfloat16 [3, 2048, 2048], P(None, None, 'blk'), may hold values from -0.125 to 0.125
- query_key_value_downmap: float32 [3, 2048, 16], replicated, may hold values from -0.125 to 0.125
- query_key_value_upmap: float32 [3, 16, 2048], replicated, may hold values from -0.3 to 0.3
- query_key_value_norm: float32 [3, 2048], replicated, may hold values from 0.8 to 2
- frozen_output_weight: bfloat16 [2048, 2048], P(None, 'blk'), may hold values from -0.125 to 0.125
- output_adapter_downmap: float32 [2048, 16], replicated, may hold values from -0.125 to 0.125
- output_adapter_upmap: float32 [16, 2048], replicated, may hold values from -0.3 to 0.3
- output_column_norm: float32 [2048], replicated, may hold values from 3 to 12
- frozen_gate_up_weight: bfloat16 [2, 2048, 5632], P(None, None, 'blk'), may hold values from -0.125 to 0.125
- gate_up_adapter_downmap: float32 [2, 2048, 16], replicated, may hold values from -0.125 to 0.125
- gate_up_adapter_upmap: float32 [2, 16, 5632], replicated, may hold values from -0.3 to 0.3
- gate_up_column_norm: float32 [2, 5632], replicated, may hold values from 0.8 to 2
- frozen_down_weight: bfloat16 [5632, 2048], P(None, 'blk'), may hold values from -0.078125 to 0.078125
- down_adapter_downmap: float32 [5632, 16], replicated, may hold values from -0.078125 to 0.078125
- down_adapter_upmap: float32 [16, 2048], replicated, may hold values from -0.3 to 0.3
- down_column_norm: float32 [2048], replicated, may hold values from 1 to 3
Outputs:
- result: bfloat16 [7168, 2048], P(('dp', 'blk'))
- grad_input: float32 [7168, 2048], P(('dp', 'blk'))
- grad_gain_attn: float32 [2048], replicated
- grad_gain_ffn: float32 [2048], replicated
- grad_a_qkv: float32 [3, 2048, 16], replicated
- grad_b_qkv: float32 [3, 16, 2048], replicated
- grad_mag_qkv: float32 [3, 2048], replicated
- grad_a_out: float32 [2048, 16], replicated
- grad_b_out: float32 [16, 2048], replicated
- grad_mag_out: float32 [2048], replicated
- grad_a_gu: float32 [2, 2048, 16], replicated
- grad_b_gu: float32 [2, 16, 5632], replicated
- grad_mag_gu: float32 [2, 5632], replicated
- grad_a_down: float32 [5632, 16], replicated
- grad_b_down: float32 [16, 2048], replicated
- grad_mag_down: float32 [2048], replicated
Inputs may be any that keep to these rules, and one draw needn't show every extreme that they name: `document_length_list`: each row lists the lengths of the 3 documents packed in order into one slot of 1792 positions; a row sums to at most 1792, and the positions after its documents are padding.
All inputs are finite; a program needn't handle non-finite values.
Results may differ from a plain program's by a relative error of at most 0.03.
Values may be sent and summed in bfloat16 or wider, within the bound.
No kernel may reach another device: no remote copies, remote signals or barrier semaphores. Data moves between devices by JAX's collectives and lax.ppermute only.
A program may use at most 448 MiB of HBM per device.

v0:
```python
import jax
import jax.numpy as jnp
from jax import lax
from jax.sharding import PartitionSpec as P

MODEL_WIDTH = 2048
HEADS = 16
ADAPTER_RANK = 16
ALPHA = 32
HDIM = 128


norm_eps = 1e-05
column_eps = 1e-06
rope_base = 10000.0
far_negative = -1e30


def shifted(array, axis, by):
    peers = lax.axis_size(axis)
    pairs = [(i, i + by) for i in range(peers) if 0 <= i + by < peers]
    return lax.ppermute(array, axis, pairs)


def shifted_2(block, axis, distance):
    devices = range(lax.axis_size(axis))
    route = [((i - distance) % len(devices), i) for i in devices]
    return lax.ppermute(block, axis, route)


def layout(lens_row, first, count):
    places = first + jnp.arange(count, dtype=jnp.int32)
    ends = jnp.cumsum(lens_row, dtype=jnp.int32)
    after = (places[:, None] >= ends[None, :]).astype(jnp.int32)
    segment = jnp.sum(after, axis=1, dtype=jnp.int32)
    begins = jnp.sum(after * lens_row[None, :], axis=1, dtype=jnp.int32)
    offset = (places - begins).astype(jnp.float32)
    return (places, segment, offset, places < ends[-1])


def angles(offset):
    half = HDIM // 2
    freq = rope_base ** (-(jnp.arange(half, dtype=jnp.float32) * 2.0 / HDIM))
    turn = offset[:, None] * freq[None, :]
    return (jnp.cos(turn)[:, None, :], jnp.sin(turn)[:, None, :])


def rotate(values, cosine, sine):
    count = values.shape[0]
    split = values.reshape(count, HEADS, HDIM)
    half = HDIM // 2
    first, second = (split[..., :half], split[..., half:])
    turned = jnp.concatenate(
        [first * cosine - second * sine, second * cosine + first * sine], axis=2
    )
    return turned.reshape(count, MODEL_WIDTH)


def unrotate(gradient_tuple, cosine, sine):
    count = gradient_tuple.shape[0]
    split = gradient_tuple.reshape(count, HEADS, HDIM)
    half = HDIM // 2
    first, second = (split[..., :half], split[..., half:])
    turned = jnp.concatenate(
        [first * cosine + second * sine, second * cosine - first * sine], axis=2
    )
    return turned.reshape(count, MODEL_WIDTH)


def normalize(values, gain):
    inverse = lax.rsqrt(jnp.mean(values * values, axis=-1, keepdims=True) + norm_eps)
    return (values * inverse * gain, inverse)


def normalize_back(values, inverse, gain, gradient_tuple):
    unit_columns = values * inverse
    scaled = gradient_tuple * gain
    d_values = inverse * (
        scaled - unit_columns * jnp.mean(scaled * unit_columns, axis=-1, keepdims=True)
    )
    return (d_values, jnp.sum(gradient_tuple * unit_columns, axis=0))


def combine_block(layer_block, lowrank_adapter, start_offset):
    adapter_downmap, adapter_upmap, column_magnitude = lowrank_adapter
    column_width = layer_block.shape[2]
    upmap_portion = lax.dynamic_slice_in_dim(adapter_upmap, start_offset, column_width, 2)
    magnitude_portion = lax.dynamic_slice_in_dim(column_magnitude, start_offset, column_width, 1)
    adapter_scale = ALPHA / ADAPTER_RANK
    unit_direction = layer_block.astype(jnp.float32) + adapter_scale * jnp.einsum(
        "xjf,xfa->xja", adapter_downmap, upmap_portion, precision=lax.Precision.HIGHEST
    )
    column_norms = jnp.sqrt(jnp.sum(unit_direction * unit_direction, axis=1) + column_eps)
    combined_weight = (unit_direction * (magnitude_portion / column_norms)[:, None, :]).astype(
        jnp.bfloat16
    )
    return (unit_direction, column_norms, magnitude_portion, upmap_portion, combined_weight)


def apply_section(input_rows, token_section, lowrank_adapter, unit_columns):
    section_width = token_section.shape[2]
    block_width = min(unit_columns, section_width)
    blocks = section_width // block_width

    def apply_one(block_number):
        layer_block = lax.dynamic_slice_in_dim(
            token_section, block_number * block_width, block_width, 2
        )
        combined_weight = combine_block(layer_block, lowrank_adapter, block_number * block_width)[4]
        return jnp.einsum(
            "ti,kiw->ktw", input_rows, combined_weight, preferred_element_type=jnp.float32
        )

    outputs = lax.map(apply_one, jnp.arange(blocks, dtype=jnp.int32))
    joined = jnp.moveaxis(outputs, 0, 2).reshape(
        outputs.shape[1], outputs.shape[2], blocks * block_width
    )
    return joined


def reverse_block(
    running_state, input_rows, gradient_tuple, layer_block, lowrank_adapter, start_offset
):
    d_inputs, grad_a, grad_b, grad_m = running_state
    adapter_downmap = lowrank_adapter[0]
    unit_direction, column_norms, magnitude_portion, upmap_portion, combined_weight = combine_block(
        layer_block, lowrank_adapter, start_offset
    )
    column_width = layer_block.shape[2]
    adapter_scale = ALPHA / ADAPTER_RANK
    g_part = lax.dynamic_slice_in_dim(gradient_tuple, start_offset, column_width, 2)
    d_inputs = d_inputs + jnp.einsum(
        "ktw,kiw->ti", g_part, combined_weight, preferred_element_type=jnp.float32
    )
    outer = jnp.einsum("ti,ktw->kiw", input_rows, g_part, preferred_element_type=jnp.float32)
    m_grad = jnp.sum(outer * unit_direction, axis=1) / column_norms
    direction_gradient = (magnitude_portion / column_norms)[:, None, :] * (
        outer - unit_direction * (m_grad / column_norms)[:, None, :]
    )
    grad_a = grad_a + adapter_scale * jnp.einsum(
        "kiw,krw->kir", direction_gradient, upmap_portion, precision=lax.Precision.HIGHEST
    )
    b_grad = adapter_scale * jnp.einsum(
        "btn,btz->bnz", adapter_downmap, direction_gradient, precision=lax.Precision.HIGHEST
    )
    grad_b = lax.dynamic_update_slice_in_dim(grad_b, b_grad, start_offset, 2)
    grad_m = lax.dynamic_update_slice_in_dim(grad_m, m_grad, start_offset, 1)
    return (d_inputs, grad_a, grad_b, grad_m)


def reverse_section(
    running_state, input_rows, gradient_tuple, token_section, lowrank_adapter, unit_columns
):
    section_width = token_section.shape[2]
    block_width = min(unit_columns, section_width)
    blocks = section_width // block_width

    def reverse_one(block_number, loop_state):
        layer_block = lax.dynamic_slice_in_dim(
            token_section, block_number * block_width, block_width, 2
        )
        return reverse_block(
            loop_state,
            input_rows,
            gradient_tuple,
            layer_block,
            lowrank_adapter,
            block_number * block_width,
        )

    running_state = lax.fori_loop(0, blocks, reverse_one, running_state)
    return running_state


def initial_state(input_rows, lowrank_adapter):
    adapter_downmap, adapter_upmap, column_magnitude = lowrank_adapter
    return (
        jnp.zeros((input_rows.shape[0], adapter_downmap.shape[1]), jnp.float32),
        jnp.zeros_like(adapter_downmap),
        jnp.zeros_like(adapter_upmap),
        jnp.zeros_like(column_magnitude),
    )


def apply_projection(input_rows, frozen_matrix, lowrank_adapter):
    unit_columns = frozen_matrix.shape[2]
    return apply_section(
        input_rows,
        lax.all_gather(frozen_matrix, "blk", axis=2, tiled=True),
        lowrank_adapter,
        unit_columns,
    )


def projection_reverse(input_rows, gradient_tuple, frozen_matrix, lowrank_adapter):
    unit_columns = frozen_matrix.shape[2]
    return reverse_section(
        initial_state(input_rows, lowrank_adapter),
        input_rows,
        gradient_tuple,
        lax.all_gather(frozen_matrix, "blk", axis=2, tiled=True),
        lowrank_adapter,
        unit_columns,
    )


def head_scores(queries, keys):
    return jnp.einsum(
        "qhd,khd->hqk",
        queries.reshape(queries.shape[0], HEADS, HDIM),
        keys.reshape(keys.shape[0], HEADS, HDIM),
        preferred_element_type=jnp.float32,
    ) * HDIM ** (-0.5)


def per_device(
    tokens,
    cotangent,
    document_length_list,
    attention_norm_gain,
    feedforward_norm_gain,
    frozen_query_key_value,
    query_key_value_downmap,
    query_key_value_upmap,
    query_key_value_norm,
    frozen_output_weight,
    output_adapter_downmap,
    output_adapter_upmap,
    output_column_norm,
    frozen_gate_up_weight,
    gate_up_adapter_downmap,
    gate_up_adapter_upmap,
    gate_up_column_norm,
    frozen_down_weight,
    down_adapter_downmap,
    down_adapter_upmap,
    down_column_norm,
):
    length = tokens.shape[0]
    lens_row = document_length_list[0]
    place_index = lax.axis_index("blk")
    places, segment, offset, valid = layout(lens_row, place_index * length, length)
    cosine, sine = angles(offset)
    frozen_matrices = (
        frozen_query_key_value,
        frozen_output_weight.reshape(
            1, frozen_output_weight.shape[0], frozen_output_weight.shape[1]
        ),
        frozen_gate_up_weight,
        frozen_down_weight.reshape(1, frozen_down_weight.shape[0], frozen_down_weight.shape[1]),
    )
    lowrank_adapters = (
        (query_key_value_downmap, query_key_value_upmap, query_key_value_norm),
        (output_adapter_downmap[None], output_adapter_upmap[None], output_column_norm[None]),
        (gate_up_adapter_downmap, gate_up_adapter_upmap, gate_up_column_norm),
        (down_adapter_downmap[None], down_adapter_upmap[None], down_column_norm[None]),
    )

    def receiver_use(block_number, input_rows):
        return apply_projection(
            input_rows, frozen_matrices[block_number], lowrank_adapters[block_number]
        )

    def backward_use(block_number, input_rows, gradient_tuple):
        return projection_reverse(
            input_rows,
            gradient_tuple,
            frozen_matrices[block_number],
            lowrank_adapters[block_number],
        )

    def forward_use(block_number, input_rows):
        return receiver_use(block_number, input_rows)

    x_full = tokens.astype(jnp.float32)
    normed_one, inverse_one = normalize(x_full, attention_norm_gain)
    h_one = normed_one.astype(jnp.bfloat16)
    triple = forward_use(0, h_one)
    queries = rotate(triple[0], cosine, sine).astype(jnp.bfloat16)
    keys = rotate(triple[1], cosine, sine).astype(jnp.bfloat16)
    values = triple[2].astype(jnp.bfloat16)

    def allowed_for(start_offset, count):
        key_places, key_segment, key_offset, key_valid = layout(lens_row, start_offset, count)
        return (
            (key_segment[None, :] == segment[:, None]) & (key_places[None, :] <= places[:, None])
        )[None]

    token_section = lax.all_gather(keys, "blk", axis=0, tiled=True)
    highest = jnp.full((HEADS, length), far_negative, jnp.float32)
    allowed = allowed_for(jnp.int32(0), token_section.shape[0])
    scores = jnp.where(allowed, head_scores(queries, token_section), far_negative)
    new_high = jnp.maximum(highest, jnp.max(scores, axis=2))
    total = jnp.sum(jnp.where(allowed, jnp.exp(scores - new_high[:, :, None]), 0.0), axis=2)
    highest, total = (new_high, total)
    lse = highest + jnp.log(total)
    key_piece = lax.all_gather(keys, "blk", axis=0, tiled=True)
    value_piece = lax.all_gather(values, "blk", axis=0, tiled=True)
    allowed = allowed_for(jnp.int32(0), key_piece.shape[0])
    weights = jnp.where(
        allowed, jnp.exp(head_scores(queries, key_piece) - lse[:, :, None]), 0.0
    ).astype(jnp.bfloat16)
    mixed = jnp.einsum(
        "hqk,khd->qhd",
        weights,
        value_piece.reshape(value_piece.shape[0], HEADS, HDIM),
        preferred_element_type=jnp.float32,
    )
    mixed_full = mixed.reshape(length, MODEL_WIDTH)
    attended = mixed_full.astype(jnp.bfloat16)
    residual = x_full + forward_use(1, attended)[0]
    normed_two, inverse_two = normalize(residual, feedforward_norm_gain)
    h_two = normed_two.astype(jnp.bfloat16)
    pair = forward_use(2, h_two)
    gate, upward = (pair[0], pair[1])
    act = (jax.nn.silu(gate) * upward).astype(jnp.bfloat16)
    final = residual + forward_use(3, act)[0]
    result = final.astype(jnp.bfloat16)
    d_final = cotangent.astype(jnp.float32) * valid.astype(jnp.float32)[:, None]
    d_act, grad_a_down, grad_b_down, grad_m_down = backward_use(
        3, act, d_final.astype(jnp.bfloat16)[None]
    )
    sigmoid_gate = jax.nn.sigmoid(gate)
    d_gate = d_act * upward * sigmoid_gate * (1.0 + gate * (1.0 - sigmoid_gate))
    d_upward = d_act * gate * sigmoid_gate
    dh_two, grad_a_gu, grad_b_gu, grad_m_gu = backward_use(
        2, h_two, jnp.stack([d_gate, d_upward]).astype(jnp.bfloat16)
    )
    d_norm_two, grad_g_ffn = normalize_back(residual, inverse_two, feedforward_norm_gain, dh_two)
    d_residual = d_final + d_norm_two
    d_attended, grad_a_out, grad_b_out, grad_m_out = backward_use(
        1, attended, d_residual.astype(jnp.bfloat16)[None]
    )
    d_mixed = d_attended.astype(jnp.bfloat16)
    mixed_heads = d_mixed.reshape(length, HEADS, HDIM)
    delta = jnp.sum(
        mixed_heads.astype(jnp.float32) * mixed_full.reshape(length, HEADS, HDIM), axis=2
    ).T
    query_heads = queries.reshape(length, HEADS, HDIM)
    zeros_rows = jnp.zeros((length, MODEL_WIDTH), jnp.float32)
    members = lax.axis_size("blk")

    def visit_step(step, loop_state):
        key_block, value_block, grad_keys, grad_values, grad_queries = loop_state
        source = (place_index - step) % members
        allowed = allowed_for(source * length, length)
        key_heads = key_block.reshape(length, HEADS, HDIM)
        probs = jnp.where(allowed, jnp.exp(head_scores(queries, key_block) - lse[:, :, None]), 0.0)
        probs_low = probs.astype(jnp.bfloat16)
        grad_values = grad_values + jnp.einsum(
            "hqk,qhd->khd", probs_low, mixed_heads, preferred_element_type=jnp.float32
        ).reshape(length, MODEL_WIDTH)
        d_probs = jnp.einsum(
            "qhd,khd->hqk",
            mixed_heads,
            value_block.reshape(length, HEADS, HDIM),
            preferred_element_type=jnp.float32,
        )
        d_scores = jnp.where(allowed, probs * (d_probs - delta[:, :, None]), 0.0).astype(
            jnp.bfloat16
        )
        grad_queries = grad_queries + jnp.einsum(
            "hqk,khd->qhd", d_scores, key_heads, preferred_element_type=jnp.float32
        ).reshape(length, MODEL_WIDTH) * HDIM ** (-0.5)
        grad_keys = grad_keys + jnp.einsum(
            "hqk,qhd->khd", d_scores, query_heads, preferred_element_type=jnp.float32
        ).reshape(length, MODEL_WIDTH) * HDIM ** (-0.5)
        key_block, value_block = shifted((key_block, value_block), "blk", 1)
        grad_keys, grad_values = (
            shifted_2(grad_keys.astype(jnp.bfloat16), "blk", 1).astype(grad_keys.dtype),
            shifted_2(grad_values.astype(jnp.bfloat16), "blk", 1).astype(grad_values.dtype),
        )
        return (key_block, value_block, grad_keys, grad_values, grad_queries)

    visited = lax.fori_loop(
        0, members, visit_step, (keys, values, zeros_rows, zeros_rows, zeros_rows)
    )
    grad_keys, grad_values, grad_queries = (visited[2], visited[3], visited[4])
    g_qkv = jnp.stack(
        [unrotate(grad_queries, cosine, sine), unrotate(grad_keys, cosine, sine), grad_values]
    ).astype(jnp.bfloat16)
    dh_one, grad_a_qkv, grad_b_qkv, grad_m_qkv = backward_use(0, h_one, g_qkv)
    d_norm_one, grad_g_attn = normalize_back(x_full, inverse_one, attention_norm_gain, dh_one)
    grad_input = d_residual + d_norm_one
    summed = lax.psum(
        (
            grad_g_attn,
            grad_g_ffn,
            grad_a_qkv,
            grad_b_qkv,
            grad_m_qkv,
            grad_a_out[0],
            grad_b_out[0],
            grad_m_out[0],
            grad_a_gu,
            grad_b_gu,
            grad_m_gu,
            grad_a_down[0],
            grad_b_down[0],
            grad_m_down[0],
        ),
        ("dp", "blk"),
    )
    return (result, grad_input) + tuple(summed)


def solution(mesh):
    in_specs = (
        P(("dp", "blk"), None),
        P(("dp", "blk"), None),
        P("dp", None),
        P(),
        P(),
        P(None, None, "blk"),
        P(),
        P(),
        P(),
        P(None, "blk"),
        P(),
        P(),
        P(),
        P(None, None, "blk"),
        P(),
        P(),
        P(),
        P(None, "blk"),
        P(),
        P(),
        P(),
    )
    out_specs = (
        P(("dp", "blk"), None),
        P(("dp", "blk"), None),
        P(),
        P(),
        P(),
        P(),
        P(),
        P(),
        P(),
        P(),
        P(),
        P(),
        P(),
        P(),
        P(),
        P(),
    )
    return jax.shard_map(
        per_device, mesh=mesh, in_specs=in_specs, out_specs=out_specs, check_vma=False
    )
```

profile of v0, /device:TPU:0, one launch (start us, length us, event | category | flops | bytes accessed | tf_op | source)
XLA Modules:
  0.0 3162.5 jit_solution(16929286264982317534)
XLA Ops:
  14.2 220.5 %all-gather.9.cloned.1.call-done = bf16[3,2048,2048]{1,2,0:T(8,128)(2,1)} async-done(((bf16[3,2048,256]{1,2,0:T(8,128)(2,1)}), bf16[3,2048,2048]{1,2,0:T(8,128)(2,1)}) %all-gather.9.cloned.1.call-update) | async-done | bytes 25165840 | tf_op jit(solution)/shard_map/all_gather | solution.py:189
  234.7 113.0 %while.144 = (s32[]{:T(128)}, f32[8,3,224,256]{3,2,1,0:T(8,128)}, s32[8]{0:T(128)S(1)}, bf16[3,2048,2048]{1,2,0:T(8,128)(2,1)}, f32[3,16,2048]{2,1,0:T(8,128)}, ...) while((s32[]{:T(128)}, f32[8,3,224,256]{3,2,1,0:T(8,128)}, ...), condition=%wide.region_3.4_spmd, body=%wide.region_1.3_spmd.sunk | while | flops 1022362368 | bytes 20939448 | solution.py:114
  389.3 56.4 %all-gather.13.cloned.1.call-done = bf16[1792,2048]{1,0:T(8,128)(2,1)} async-done(((bf16[224,2048]{1,0:T(8,128)(2,1)}), bf16[1792,2048]{1,0:T(8,128)(2,1)}) %all-gather.13.cloned.1.call-update) | async-done | bytes 7340048 | tf_op jit(solution)/shard_map/all_gather | solution.py:297
  456.3 63.1 %all-gather.11.cloned.1.call-done = bf16[1792,2048]{1,0:T(8,128)(2,1)} async-done(((bf16[224,2048]{1,0:T(8,128)(2,1)}), bf16[1792,2048]{1,0:T(8,128)(2,1)}) %all-gather.11.cloned.1.call-update) | async-done | bytes 7340048 | tf_op jit(solution)/shard_map/all_gather | solution.py:298
  572.5 29.0 all-gather.17.cloned.1.call-done
  602.9 53.7 %while.145 = (s32[]{:T(128)}, f32[8,1,224,256]{3,2,1,0:T(8,128)}, s32[8]{0:T(128)S(1)}, bf16[1,2048,2048]{1,2,0:T(8,128)(2,1)}, f32[1,16,2048]{2,1,0:T(8,128)}, ...) while((s32[]{:T(128)}, f32[8,1,224,256]{3,2,1,0:T(8,128)}, ...), condition=%wide.region_12.13_spmd, body=%wide.region_10.12_spmd.sunk | while | flops 339214592 | bytes 6546099 | solution.py:114
  660.5 333.0 %all-gather.15.cloned.1.call-done = bf16[2,2048,5632]{1,2,0:T(8,128)(2,1)} async-done(((bf16[2,2048,704]{1,2,0:T(8,128)(2,1)}), bf16[2,2048,5632]{1,2,0:T(8,128)(2,1)}) %all-gather.15.cloned.1.call-update) | async-done | bytes 46137360 | tf_op jit(solution)/shard_map/all_gather | solution.py:189
  993.5 172.8 %while.146 = (s32[]{:T(128)}, f32[8,2,224,704]{3,2,1,0:T(8,128)}, s32[8]{0:T(128)S(1)}, bf16[2,2048,5632]{1,2,0:T(8,128)(2,1)}, f32[2,16,5632]{2,1,0:T(8,128)}, ...) while((s32[]{:T(128)}, f32[8,2,224,704]{3,2,1,0:T(8,128)}, ...), condition=%wide.region_16.17_spmd, body=%wide.region_14.16_spmd.sunk | while | flops 1874331008 | bytes 37287096 | solution.py:114
  1208.0 253.7 %while.148 = (s32[]{:T(128)}, f32[224,5632]{1,0:T(8,128)}, f32[1,5632,16]{1,2,0:T(8,128)}, f32[1,16,2048]{2,1,0:T(8,128)}, f32[1,2048]{1,0:T(1,128)S(1)}, /*inde...) while((s32[]{:T(128)}, f32[224,5632]{1,0:T(8,128)}, ...), condition=%wide.region_23.24_spmd.clone, body=%wide.region_20.23_spmd.clone.sunk | while | flops 2146743040 | bytes 134022464 | solution.py:171
  1473.0 465.9 %while.149 = (s32[]{:T(128)}, f32[224,2048]{1,0:T(8,128)S(1)}, f32[2,2048,16]{1,2,0:T(8,128)S(1)}, f32[2,16,5632]{2,1,0:T(8,128)}, f32[2,5632]{1,0:T(2,128)S(1)}...) while((s32[]{:T(128)}, f32[224,2048]{1,0:T(8,128)S(1)}, ...), condition=%wide.region_27.28_spmd.clone, body=%wide.region_24.27_spmd.clone.sunk | while | flops 4289030144 | bytes 151744240 | solution.py:171
  1476.5 18.0 fusion.374
  1495.3 15.3 fusion.378
  1534.6 18.0 fusion.374
  1593.0 18.0 fusion.374
  1651.0 18.0 fusion.374
  1709.5 18.0 fusion.374
  1767.5 18.0 fusion.374
  1825.9 18.0 fusion.374
  1883.9 18.0 fusion.374
  1902.7 15.3 fusion.378
  1945.6 88.7 %while.147 = (s32[]{:T(128)}, f32[8,1,224,256]{3,2,1,0:T(8,128)}, s32[8]{0:T(128)S(1)}, bf16[1,5632,2048]{1,2,0:T(8,128)(2,1)}, f32[1,16,2048]{2,1,0:T(8,128)}, ...) while((s32[]{:T(128)}, f32[8,1,224,256]{3,2,1,0:T(8,128)}, ...), condition=%wide.region_19.20_spmd, body=%wide.region_17.19_spmd.sunk | while | flops 932839680 | bytes 17556148 | solution.py:114
  2040.8 112.3 %while.150 = (s32[]{:T(128)}, f32[224,2048]{1,0:T(8,128)}, f32[1,2048,16]{1,2,0:T(8,128)S(1)}, f32[1,16,2048]{2,1,0:T(8,128)S(1)}, f32[1,2048]{1,0:T(1,128)S(1)}...) while((s32[]{:T(128)}, f32[224,2048]{1,0:T(8,128)}, ...), condition=%wide.region_32.33_spmd.clone, body=%wide.region_29.32_spmd.clone.sunk | while | flops 780636928 | bytes 46302508 | solution.py:171
  2157.2 401.7 %while.151 = (s32[]{:T(128)}, bf16[224,2048]{1,0:T(8,128)(2,1)}, bf16[224,2048]{1,0:T(8,128)(2,1)}, f32[224,2048]{1,0:T(8,128)}, f32[224,2048]{1,0:T(8,128)}, /*...) while((s32[]{:T(128)}, bf16[224,2048]{1,0:T(8,128)(2,1)}, ...), condition=%wide.region_37.38_spmd.clone, body=%wide.region_35.37_spmd.clone.sunk | while | flops 1042093248 | bytes 105485000 | solution.py:375
  2250.2 22.1 collective-permute-start.2
  2303.4 22.1 collective-permute-start.2
  2356.6 22.1 collective-permute-start.2
  2409.7 22.1 collective-permute-start.2
  2462.9 22.1 collective-permute-start.2
  2516.1 22.1 collective-permute-start.2
  2575.0 266.7 %while.152 = (s32[]{:T(128)}, f32[224,2048]{1,0:T(8,128)S(1)}, f32[3,2048,16]{1,2,0:T(8,128)S(1)}, f32[3,16,2048]{2,1,0:T(8,128)}, f32[3,2048]{1,0:T(4,128)}, /*...) while((s32[]{:T(128)}, f32[224,2048]{1,0:T(8,128)S(1)}, ...), condition=%wide.region_41.42_spmd.clone, body=%wide.region_38.41_spmd.clone.sunk | while | flops 2340075776 | bytes 136014128 | solution.py:171
  2848.3 142.8 %all-reduce.5.cloned.1.call-done = (f32[2048]{0:T(1024)}, f32[2048]{0:T(1024)}, f32[3,2048]{1,0:T(4,128)}, f32[2048]{0:T(1024)}, f32[2,5632]{1,0:T(2,128)}, /*index=5*/f32[2048]{0:T(1024)}) async-done(((f32[2048]{0:T(1024)}, f32[2048]{0:T(1024)}, f32[3,2048]{1,0:T(4,128)}, f32[2048]{0:T(1024)}, f32[2,5632]{1,0:T(2,128)}, /*index=5*/f32[2048]{0:T(1024)}), (f32[2048]{0:T(1024)}, f32[2048]{0:T(1024)}, ...) | async-done | bytes 102416 | tf_op jit(solution)/shard_map/psum | solution.py:385
  2991.1 146.9 %all-reduce.7.cloned.1.call-done = (f32[3,2048,16]{1,2,0:T(8,128)}, f32[3,16,2048]{2,1,0:T(8,128)}, f32[2048,16]{0,1:T(8,128)}, f32[16,2048]{1,0:T(8,128)}, f32[...) async-done(((f32[3,2048,16]{1,2,0:T(8,128)}, f32[3,16,2048]{2,1,0:T(8,128)}, f32[2048,16]{0,1:T(8,128)}, ...) | async-done | bytes 2523152 | tf_op jit(solution)/shard_map/psum | solution.py:385
  (1101 shorter events, 1821.7 us)
Async XLA Ops:
  7.2 227.5 %all-gather.9.cloned.1.call-start = ((), (), s32[]{:S(2)}) async-start(), calls=%async_computation | async-start | bytes 28311552 | tf_op jit(solution)/shard_map/all_gather | solution.py:189
  12.0 433.7 %all-gather.13.cloned.1.call-start = ((), (), s32[]{:S(2)}) async-start(), calls=%async_computation.2 | async-start | bytes 8257536 | tf_op jit(solution)/shard_map/all_gather | solution.py:297
  373.9 145.4 %all-gather.11.cloned.1.call-start = ((), (), s32[]{:S(2)}) async-start(), calls=%async_computation.1 | async-start | bytes 8257536 | tf_op jit(solution)/shard_map/all_gather | solution.py:298
  376.8 224.7 %all-gather.17.cloned.1.call-start = ((), (), s32[]{:S(2)}) async-start(), calls=%async_computation.4 | async-start | bytes 9437184 | tf_op jit(solution)/shard_map/all_gather | solution.py:189
  378.3 615.2 %all-gather.15.cloned.1.call-start = ((), (), s32[]{:S(2)}) async-start(), calls=%async_computation.3 | async-start | bytes 51904512 | tf_op jit(solution)/shard_map/all_gather | solution.py:189
  378.9 828.5 %all-gather.19.cloned.1.call-start = ((), (), s32[]{:S(2)}) async-start(), calls=%async_computation.5 | async-start | bytes 25952256 | tf_op jit(solution)/shard_map/all_gather | solution.py:189
  383.7 2607.4 %all-reduce.5.cloned.1.call-start = ((), (), s32[]{:S(2)}) async-start(), calls=%async_computation.6 | async-start | bytes 221184 | tf_op jit(solution)/shard_map/psum | solution.py:385
  2168.2 14.9 collective-permute-start.2
  2171.3 21.7 collective-permute-start.3
  2171.3 24.4 collective-permute-start
  2174.1 21.5 collective-permute-start.1
  2206.3 26.7 collective-permute-start.2
  2224.5 15.1 collective-permute-start
  2250.2 36.0 %collective-permute-start.2 = (bf16[224,2048]{1,0:T(8,128)(2,1)}, bf16[224,2048]{1,0:T(8,128)(2,1)}, u32[]{:S(2)}, u32[]{:S(2)}) collective-permute-start(bf16[224,2048]{1,0:T(8,128)(2,1)} %fusion.406), channel_id=1, source_target_pairs={{7,0},{0,1},{1,2},{2,3},{3,4},{4,5},{5,6},{6,7},{15,8},{8,9},{9,10... | collective-permute-start | bytes 2752520 | tf_op jit(solution)/shard_map/while/body/eval_jaxpr/ppermute | solution.py:28
  2275.2 14.9 collective-permute-start.3
  2277.7 15.1 collective-permute-start
  2303.4 36.0 %collective-permute-start.2 = (bf16[224,2048]{1,0:T(8,128)(2,1)}, bf16[224,2048]{1,0:T(8,128)(2,1)}, u32[]{:S(2)}, u32[]{:S(2)}) collective-permute-start(bf16[224,2048]{1,0:T(8,128)(2,1)} %fusion.406), channel_id=1, source_target_pairs={{7,0},{0,1},{1,2},{2,3},{3,4},{4,5},{5,6},{6,7},{15,8},{8,9},{9,10... | collective-permute-start | bytes 2752520 | tf_op jit(solution)/shard_map/while/body/eval_jaxpr/ppermute | solution.py:28
  2328.4 14.9 collective-permute-start.3
  2330.9 15.1 collective-permute-start
  2356.6 36.0 %collective-permute-start.2 = (bf16[224,2048]{1,0:T(8,128)(2,1)}, bf16[224,2048]{1,0:T(8,128)(2,1)}, u32[]{:S(2)}, u32[]{:S(2)}) collective-permute-start(bf16[224,2048]{1,0:T(8,128)(2,1)} %fusion.406), channel_id=1, source_target_pairs={{7,0},{0,1},{1,2},{2,3},{3,4},{4,5},{5,6},{6,7},{15,8},{8,9},{9,10... | collective-permute-start | bytes 2752520 | tf_op jit(solution)/shard_map/while/body/eval_jaxpr/ppermute | solution.py:28
  2381.6 14.9 collective-permute-start.3
  2384.0 15.1 collective-permute-start
  2409.7 36.0 %collective-permute-start.2 = (bf16[224,2048]{1,0:T(8,128)(2,1)}, bf16[224,2048]{1,0:T(8,128)(2,1)}, u32[]{:S(2)}, u32[]{:S(2)}) collective-permute-start(bf16[224,2048]{1,0:T(8,128)(2,1)} %fusion.406), channel_id=1, source_target_pairs={{7,0},{0,1},{1,2},{2,3},{3,4},{4,5},{5,6},{6,7},{15,8},{8,9},{9,10... | collective-permute-start | bytes 2752520 | tf_op jit(solution)/shard_map/while/body/eval_jaxpr/ppermute | solution.py:28
  2434.8 14.9 collective-permute-start.3
  2437.2 15.1 collective-permute-start
  2462.9 36.0 %collective-permute-start.2 = (bf16[224,2048]{1,0:T(8,128)(2,1)}, bf16[224,2048]{1,0:T(8,128)(2,1)}, u32[]{:S(2)}, u32[]{:S(2)}) collective-permute-start(bf16[224,2048]{1,0:T(8,128)(2,1)} %fusion.406), channel_id=1, source_target_pairs={{7,0},{0,1},{1,2},{2,3},{3,4},{4,5},{5,6},{6,7},{15,8},{8,9},{9,10... | collective-permute-start | bytes 2752520 | tf_op jit(solution)/shard_map/while/body/eval_jaxpr/ppermute | solution.py:28
  2488.0 14.9 collective-permute-start.3
  2490.4 15.1 collective-permute-start
  2516.1 36.0 %collective-permute-start.2 = (bf16[224,2048]{1,0:T(8,128)(2,1)}, bf16[224,2048]{1,0:T(8,128)(2,1)}, u32[]{:S(2)}, u32[]{:S(2)}) collective-permute-start(bf16[224,2048]{1,0:T(8,128)(2,1)} %fusion.406), channel_id=1, source_target_pairs={{7,0},{0,1},{1,2},{2,3},{3,4},{4,5},{5,6},{6,7},{15,8},{8,9},{9,10... | collective-permute-start | bytes 2752520 | tf_op jit(solution)/shard_map/while/body/eval_jaxpr/ppermute | solution.py:28
  2541.2 14.9 collective-permute-start.3
  2543.6 15.1 collective-permute-start
  2844.3 293.8 %all-reduce.7.cloned.1.call-start = ((), (), s32[]{:S(2)}) async-start(), calls=%async_computation.7 | async-start | bytes 5046272 | tf_op jit(solution)/shard_map/psum | solution.py:385
  (221 other events, 5010.1 us)
Sparse Core Ops, SparseCore 0:
  12.1 222.5 all-gather.8
  374.1 71.5 all-gather.12
  447.3 71.9 all-gather.10
  520.8 80.6 all-gather.16
  603.0 390.5 all-gather.14
  995.0 200.8 all-gather.18
  2844.4 146.6 all-reduce.4
  2998.7 139.3 all-reduce.6
where the time goes:
time: 3180 us; the launch traced here: 3160 us
  matrix products  1460 us (46%)
  waiting for transfers between devices  1010 us (32%)
  local copies, waits for them, and re-layouts  246 us (8%)
  starting transfers between devices  215 us (7%)
  other arithmetic  191 us (6%)
    all_gather x4, waiting for transfers between devices, apply_projection(): lax.all_gather(frozen_matrix, 'blk', axis=2, tiled=True)  582 us
    dot_general x64, matrix products, combine_block(): jnp.einsum('xjf,xfa->xja', adapter_downmap, upmap_portion, precision=lax....  566 us
    psum x2, waiting for transfers between devices, per_device(): lax.psum((grad_g_attn, grad_g_ffn, grad_a_qkv, grad_b_qkv, grad_m_qkv, gr...  290 us
    dot_general x32, matrix products, reverse_block(): jnp.einsum('kiw,krw->kir', direction_gradient, upmap_portion, precision=l...  261 us
    dot_general x32, matrix products, reverse_block(): jnp.einsum('btn,btz->bnz', adapter_downmap, direction_gradient, precision...  235 us
    ppermute x16, starting transfers between devices, shifted_2(): return lax.ppermute(block, axis, route)  163 us
    dot_general x32, matrix products, reverse_block(): jnp.einsum('ktw,kiw->ti', g_part, combined_weight, preferred_element_type...  131 us
    dot_general x32, matrix products, apply_one(): jnp.einsum('ti,kiw->ktw', input_rows, combined_weight, preferred_element_...  110 us
  transfers between devices with their start and end apart: 40, of which 16 were waited for; matrix products, arithmetic and copies ran while one was open for 13% of the time, Pallas kernels for 0%

commit v1 on v0

v1 whole, which is shorter than its diff:
```python
import functools

import jax
import jax.numpy as jnp
from jax import lax
from jax.experimental import pallas as pl
from jax.experimental.pallas import tpu as pltpu
from jax.sharding import PartitionSpec as P

MODEL_WIDTH = 2048
HEADS = 16
ADAPTER_RANK = 16
ALPHA = 32
HDIM = 128
TILE = 256
QUAD = 4

norm_eps = 1e-05
column_eps = 1e-06
rope_base = 10000.0
far_negative = -1e30
adapter_scale = ALPHA / ADAPTER_RANK
bf16 = jnp.bfloat16
f32 = jnp.float32
NT = (((1,), (1,)), ((), ()))
TN = (((0,), (0,)), ((), ()))
NN = (((1,), (0,)), ((), ()))


def dot(a, b, dims=NN):
    return lax.dot_general(a, b, dims, preferred_element_type=f32)


def after(array, *earlier):
    return lax.optimization_barrier((array, *earlier))[0]


def blank(shape, dtype):
    return pl.pallas_call(
        lambda out: None,
        out_shape=jax.ShapeDtypeStruct(shape, dtype),
        out_specs=pl.BlockSpec(memory_space=pl.ANY),
        name="blank",
    )()


def swap(array, axis, bit):
    return lax.ppermute(array, axis, [(i, i ^ bit) for i in range(lax.axis_size(axis))])


def axis_sum(array, axis):
    bit = 1
    while bit < lax.axis_size(axis):
        array = array + swap(array, axis, bit)
        bit *= 2
    return array


def begins_of(lens_row, count):
    places = jnp.arange(count, dtype=jnp.int32)
    ends = jnp.cumsum(lens_row, dtype=jnp.int32)
    after = (places[:, None] >= ends[None, :]).astype(jnp.int32)
    return places, jnp.sum(after * lens_row[None, :], axis=1, dtype=jnp.int32), ends[-1]


def split_three(a):
    one = lax.reduce_precision(a, 8, 7)
    rest = a - one
    two = lax.reduce_precision(rest, 8, 7)
    return one.astype(bf16), two.astype(bf16), (rest - two).astype(bf16)


def parts_of(a, b):
    a1, a2, a3 = split_three(a * adapter_scale)
    b1, b2, b3 = split_three(b)
    return (
        jnp.concatenate([a1, a1, a2, a1, a2, a3], axis=-2),
        jnp.concatenate([b1, b2, b1, b3, b2, b1], axis=-2),
    )


def merge_kernel(w_ref, a_ref, b_ref, m_ref, out_ref, n_ref, v_ref):
    rows = w_ref.shape[1]

    def add(i, acc):
        at = pl.ds(pl.multiple_of(i * TILE, TILE), TILE)
        v = w_ref[0, at, :].astype(f32) + dot(a_ref[0, :, at], b_ref[0], TN)
        v_ref[at, :] = v
        return acc + jnp.sum(v * v, axis=0, keepdims=True)

    total = lax.fori_loop(0, rows // TILE, add, jnp.zeros(m_ref.shape, f32), unroll=2)
    norms = jnp.sqrt(total + column_eps)
    n_ref[...] = norms
    s = m_ref[...] / norms

    def put(i, carry):
        at = pl.ds(pl.multiple_of(i * TILE, TILE), TILE)
        out_ref[at, :] = (v_ref[at, :] * s).astype(bf16)
        return carry

    lax.fori_loop(0, rows // TILE, put, 0, unroll=2)


def merge(w, a, b, m):
    k, rows, cols = w.shape
    a_cat, b_cat = parts_of(a, b)
    wide = a_cat.shape[1]
    place = lambda i, h: (0, h * k + i)
    return pl.pallas_call(
        merge_kernel,
        grid=(k, cols // HDIM),
        in_specs=[
            pl.BlockSpec((1, rows, HDIM), lambda i, h: (i, 0, h)),
            pl.BlockSpec((1, wide, rows), lambda i, h: (i, 0, 0)),
            pl.BlockSpec((1, wide, HDIM), lambda i, h: (i, 0, h)),
            pl.BlockSpec((1, HDIM), place),
        ],
        out_specs=[pl.BlockSpec((rows, HDIM), place), pl.BlockSpec((1, HDIM), place)],
        out_shape=[
            jax.ShapeDtypeStruct((rows, k * cols), bf16),
            jax.ShapeDtypeStruct((1, k * cols), f32),
        ],
        scratch_shapes=[pltpu.VMEM((rows, HDIM), f32)],
        compiler_params=pltpu.CompilerParams(vmem_limit_bytes=48 * 2**20),
        cost_estimate=pl.CostEstimate(
            flops=2 * k * rows * cols * wide, bytes_accessed=4 * k * rows * cols, transcendentals=0
        ),
        name="merge",
    )(w, a_cat, b_cat, m)


def merge_rows_kernel(w_ref, a_ref, b_ref, m_ref, out_ref, n_ref):
    out_ref = out_ref.at[0]
    v = w_ref[0].astype(f32) + dot(b_ref[0], a_ref[0], TN)
    norms = jnp.sqrt(jnp.sum(v * v, axis=1, keepdims=True) + column_eps)
    n_ref[0] = norms
    out_ref[0] = (v * (m_ref[0] / norms)).astype(bf16)


def merge_rows(w, a, b, m, mates):
    k, cols, rows = w.shape
    a_cat, b_cat = parts_of(a, b)
    wide = a_cat.shape[1]
    return pl.pallas_call(
        merge_rows_kernel,
        grid=(k,),
        in_specs=[
            pl.BlockSpec((1, cols, rows), lambda i: (i, 0, 0)),
            pl.BlockSpec((1, wide, rows), lambda i: (i, 0, 0)),
            pl.BlockSpec((1, wide, cols), lambda i: (i, 0, 0)),
            pl.BlockSpec((1, cols, 1), lambda i: (i, 0, 0)),
        ],
        out_specs=[
            pl.BlockSpec((1, 1, cols, rows), lambda i: (0, i, 0, 0)),
            pl.BlockSpec((1, cols, 1), lambda i: (i, 0, 0)),
        ],
        out_shape=[
            jax.ShapeDtypeStruct((mates, k, cols, rows), bf16),
            jax.ShapeDtypeStruct((k, cols, 1), f32),
        ],
        compiler_params=pltpu.CompilerParams(vmem_limit_bytes=56 * 2**20),
        cost_estimate=pl.CostEstimate(
            flops=2 * k * rows * cols * wide, bytes_accessed=4 * k * rows * cols, transcendentals=0
        ),
        name="merge_rows",
    )(w, a_cat, b_cat, m)


def turned(u, cosine, sine):
    return u * cosine + pltpu.roll(u, HDIM // 2, 1) * sine


def forward_kernel(
    pre, cosine, sine, begin, q_out, k_out, v_out, att_out, mixed_t, lse_out, v_t
):
    count = pre.shape[0]
    scale = HDIM**-0.5
    for i in range(count // TILE):
        at = pl.ds(i * TILE, TILE)
        cos, sin = cosine[at, :], sine[at, :]
        q_out[at, :] = turned(pre[at, :HDIM], cos, sin).astype(bf16)
        k_out[at, :] = turned(pre[at, HDIM : 2 * HDIM], cos, sin).astype(bf16)
        v = pre[at, 2 * HDIM :]
        v_out[at, :] = v.astype(bf16)
        v_t[:, at] = v.T.astype(bf16)
    for i in range(count // TILE):
        rows = pl.ds(i * TILE, TILE)
        q = q_out[rows, :]
        start = begin[:, rows]

        def visit(j, state, diagonal):
            top, total, mixed = state
            keys = pl.ds(pl.multiple_of(j * TILE, TILE), TILE)
            s = dot(k_out[keys, :], q, NT) * scale
            place = j * TILE + lax.broadcasted_iota(jnp.int32, (TILE, TILE), 0)
            allowed = place >= start
            if diagonal:
                mine = i * TILE + lax.broadcasted_iota(jnp.int32, (TILE, TILE), 1)
                allowed = allowed & (place <= mine)
            s = jnp.where(allowed, s, far_negative)
            high = jnp.maximum(top, jnp.max(s, axis=0, keepdims=True))
            keep = jnp.exp(top - high)
            p = jnp.where(allowed, jnp.exp(s - high), 0.0)
            total = total * keep + jnp.sum(p, axis=0, keepdims=True)
            mixed = mixed * keep + dot(v_t[:, keys], p.astype(bf16))
            return high, total, mixed

        state = (
            jnp.full((1, TILE), far_negative, f32),
            jnp.zeros((1, TILE), f32),
            jnp.zeros((HDIM, TILE), f32),
        )
        state = visit(i, state, True)
        for j in range(i):
            state = visit(j, state, False)
        top, total, mixed = state
        mixed = mixed / total
        mixed_t[:, rows] = mixed
        att_out[rows, :] = mixed.T.astype(bf16)
        lse_out[0, :, rows] = top + jnp.log(total)


def backward_kernel(
    q_ref, k_ref, v_ref, pre, cosine, sine, begin, grad_att, mixed_t, lse,
    g_out, gm_out, dk, dv, k_t,
):
    count = q_ref.shape[0]
    scale = HDIM**-0.5
    dk[...] = jnp.zeros_like(dk)
    dv[...] = jnp.zeros_like(dv)
    for i in range(count // TILE):
        at = pl.ds(i * TILE, TILE)
        k_t[:, at] = k_ref[at, :].astype(f32).T.astype(bf16)
    gm_q = jnp.zeros((1, HDIM), f32)
    for i in range(count // TILE):
        rows = pl.ds(i * TILE, TILE)
        q = q_ref[rows, :]
        d_mixed = grad_att[rows, :]
        delta = jnp.sum(d_mixed.astype(f32).T * mixed_t[:, rows], axis=0, keepdims=True)
        start = begin[:, rows]
        high = lse[0, :, rows]
        dq_t = jnp.zeros((HDIM, TILE), f32)
        for j in range(i + 1):
            keys = pl.ds(j * TILE, TILE)
            s = dot(k_ref[keys, :], q, NT) * scale
            place = j * TILE + lax.broadcasted_iota(jnp.int32, (TILE, TILE), 0)
            allowed = place >= start
            if j == i:
                mine = i * TILE + lax.broadcasted_iota(jnp.int32, (TILE, TILE), 1)
                allowed = allowed & (place <= mine)
            p = jnp.where(allowed, jnp.exp(s - high), 0.0)
            dp = dot(v_ref[keys, :], d_mixed, NT)
            ds = (p * (dp - delta)).astype(bf16)
            dv[keys, :] += dot(p.astype(bf16), d_mixed)
            dk[keys, :] += dot(ds, q)
            dq_t = dq_t + dot(k_t[:, keys], ds)
        gq = turned(dq_t.T * scale, cosine[rows, :], -sine[rows, :]).astype(bf16)
        g_out[rows, :HDIM] = gq
        gm_q = gm_q + jnp.sum(gq.astype(f32) * pre[rows, :HDIM], axis=0, keepdims=True)
    gm_k = jnp.zeros((1, HDIM), f32)
    gm_v = jnp.zeros((1, HDIM), f32)
    for i in range(count // TILE):
        at = pl.ds(i * TILE, TILE)
        gk = turned(dk[at, :] * scale, cosine[at, :], -sine[at, :]).astype(bf16)
        g_out[at, HDIM : 2 * HDIM] = gk
        gm_k = gm_k + jnp.sum(gk.astype(f32) * pre[at, HDIM : 2 * HDIM], axis=0, keepdims=True)
        gv = dv[at, :].astype(bf16)
        g_out[at, 2 * HDIM :] = gv
        gm_v = gm_v + jnp.sum(gv.astype(f32) * pre[at, 2 * HDIM :], axis=0, keepdims=True)
    gm_out[0:1, :HDIM] = gm_q
    gm_out[0:1, HDIM : 2 * HDIM] = gm_k
    gm_out[0:1, 2 * HDIM :] = gm_v


def attention_forward(triple, cosine, sine, begin):
    count, width = triple.shape[0], triple.shape[1] // 3
    heads = width // HDIM
    whole = lambda h: (0, 0)
    head = lambda h: (0, h)
    tall = lambda at: pl.BlockSpec((count, HDIM), at)
    return pl.pallas_call(
        forward_kernel,
        grid=(heads,),
        in_specs=[
            pl.BlockSpec((count, 3 * HDIM), head),
            tall(whole),
            tall(whole),
            pl.BlockSpec((1, count), whole),
        ],
        out_specs=[
            tall(head),
            tall(head),
            tall(head),
            tall(head),
            pl.BlockSpec((HDIM, count), lambda h: (h, 0)),
            pl.BlockSpec((1, 1, count), lambda h: (h, 0, 0)),
        ],
        out_shape=[jax.ShapeDtypeStruct((count, width), bf16)] * 4
        + [
            jax.ShapeDtypeStruct((width, count), f32),
            jax.ShapeDtypeStruct((heads, 1, count), f32),
        ],
        scratch_shapes=[pltpu.VMEM((HDIM, count), bf16)],
        compiler_params=pltpu.CompilerParams(vmem_limit_bytes=48 * 2**20),
        cost_estimate=pl.CostEstimate(
            flops=2 * count * count * width, bytes_accessed=30 * count * width, transcendentals=0
        ),
        name="attend",
    )(triple, cosine, sine, begin)


def attention_backward(q, k, v, triple, cosine, sine, begin, grad_att, mixed_t, lse):
    count, width = q.shape
    heads = width // HDIM
    whole = lambda h: (0, 0)
    head = lambda h: (0, h)
    tall = lambda at: pl.BlockSpec((count, HDIM), at)
    return pl.pallas_call(
        backward_kernel,
        grid=(heads,),
        in_specs=[
            tall(head),
            tall(head),
            tall(head),
            pl.BlockSpec((count, 3 * HDIM), head),
            tall(whole),
            tall(whole),
            pl.BlockSpec((1, count), whole),
            tall(head),
            pl.BlockSpec((HDIM, count), lambda h: (h, 0)),
            pl.BlockSpec((1, 1, count), lambda h: (h, 0, 0)),
        ],
        out_specs=[pl.BlockSpec((count, 3 * HDIM), head), pl.BlockSpec((8, 3 * HDIM), head)],
        out_shape=[
            jax.ShapeDtypeStruct((count, 3 * width), bf16),
            jax.ShapeDtypeStruct((8, 3 * width), f32),
        ],
        scratch_shapes=[
            pltpu.VMEM((count, HDIM), f32),
            pltpu.VMEM((count, HDIM), f32),
            pltpu.VMEM((HDIM, count), bf16),
        ],
        compiler_params=pltpu.CompilerParams(vmem_limit_bytes=48 * 2**20),
        cost_estimate=pl.CostEstimate(
            flops=5 * count * count * width, bytes_accessed=40 * count * width, transcendentals=0
        ),
        name="attend_back",
    )(q, k, v, triple, cosine, sine, begin, grad_att, mixed_t, lse)


def feed_kernel(gu_ref, down_ref, h_ref, d_ref, acts_out, g_out, gm_out):
    h = h_ref[...]
    gate = dot(gu_ref[0, 0], h, NT)
    upward = dot(gu_ref[0, 1], h, NT)
    d_act = dot(down_ref[...], d_ref[...], NT)
    sigmoid_gate = jax.nn.sigmoid(gate)
    silu = gate * sigmoid_gate
    acts_out[...] = (silu * upward).astype(bf16)
    d_gate = (d_act * upward * sigmoid_gate * (1.0 + gate * (1.0 - sigmoid_gate))).astype(bf16)
    d_upward = (d_act * silu).astype(bf16)
    g_out[0, 0] = d_gate
    g_out[0, 1] = d_upward
    gm_out[0, 0] = jnp.sum(d_gate.astype(f32) * gate, axis=1, keepdims=True)
    gm_out[0, 1] = jnp.sum(d_upward.astype(f32) * upward, axis=1, keepdims=True)


def feed_forward(gu, down, h, d, mates):
    rows, width = h.shape
    hidden = down.shape[0] // mates
    unit = hidden // max(1, hidden // 176)
    steps = hidden // unit
    flat = lambda k, j: (k * steps + j, 0)
    deep = lambda k, j: (k, 0, j, 0)
    whole = lambda k, j: (0, 0)
    acts, g, gm = pl.pallas_call(
        feed_kernel,
        grid=(mates, steps),
        in_specs=[
            pl.BlockSpec((1, 2, unit, width), deep),
            pl.BlockSpec((unit, width), flat),
            pl.BlockSpec((rows, width), whole),
            pl.BlockSpec((rows, width), whole),
        ],
        out_specs=[
            pl.BlockSpec((unit, rows), flat),
            pl.BlockSpec((1, 2, unit, rows), deep),
            pl.BlockSpec((1, 2, unit, 1), deep),
        ],
        out_shape=[
            jax.ShapeDtypeStruct((mates * hidden, rows), bf16),
            jax.ShapeDtypeStruct((mates, 2, hidden, rows), bf16),
            jax.ShapeDtypeStruct((mates, 2, hidden, 1), f32),
        ],
        compiler_params=pltpu.CompilerParams(vmem_limit_bytes=48 * 2**20),
        cost_estimate=pl.CostEstimate(
            flops=6 * mates * hidden * rows * width,
            bytes_accessed=6 * mates * hidden * width + 4 * rows * width,
            transcendentals=0,
        ),
        name="feed_forward",
    )(gu.reshape(mates, 2, hidden, width), down, h, d)
    return acts, g.reshape(2 * mates * hidden, rows), gm


def normalize(values, gain):
    inverse = lax.rsqrt(jnp.mean(values * values, axis=-1, keepdims=True) + norm_eps)
    return (values * inverse * gain, inverse)


def normalize_back(values, inverse, gain, grad):
    unit = values * inverse
    scaled = grad * gain
    return inverse * (scaled - unit * jnp.mean(scaled * unit, axis=-1, keepdims=True))


def quad_gather(block):
    pair = jnp.concatenate([block, swap(block, "blk", 2)], axis=0)
    return jnp.concatenate([pair, swap(pair, "blk", 1)], axis=0)


def quad_halve(parts):
    half = parts.shape[0] // 2
    return parts[:half].astype(f32) + swap(parts[half:], "blk", 1).astype(f32)


def quad_finish(mine):
    half = mine.shape[0] // 2
    return mine[:half] + swap(mine[half:].astype(bf16), "blk", 2).astype(f32)


def step_chips(array, first, last, by):
    pairs = [(2 * i + c, 2 * (i + by) + c) for i in range(first, last + 1) for c in range(2)]
    return lax.ppermute(array, "blk", pairs)


def core_scatter(parts):
    chips = lax.axis_size("blk") // 2
    core = lax.axis_index("blk") % 2
    parts = parts.reshape(chips, 2, parts.shape[0] // (2 * chips), parts.shape[1])
    take = lambda c: lax.dynamic_index_in_dim(parts, c, 1, keepdims=False)
    return (take(core).astype(f32) + swap(take(1 - core), "blk", 1).astype(f32)).astype(bf16)


def chips_step(total, t, state):
    chips = total.shape[0]
    chip = lax.axis_index("blk") // 2
    pick = lambda c: lax.dynamic_index_in_dim(
        total, jnp.clip(c, 0, chips - 1), 0, keepdims=False
    )
    up, down = pick(chips - t + chip), pick(t - chips + chip)
    if t > 1:
        up = (up.astype(f32) + state[0].astype(f32)).astype(bf16)
        down = (down.astype(f32) + state[1].astype(f32)).astype(bf16)
    up, down = after((up, down))
    return step_chips(up, 0, t - 1, 1), step_chips(down, chips - t, chips - 1, -1)


def chips_end(total, state):
    chip = lax.axis_index("blk") // 2
    own = lax.dynamic_index_in_dim(total, chip, 0, keepdims=False)
    return own.astype(f32) + state[0].astype(f32) + state[1].astype(f32)


def dp_start(piece):
    half = piece.shape[0] // 2
    return piece[None, :half], piece[None, half:]


def dp_steps(state, first=None, last=None):
    bits = [1 << i for i in range(lax.axis_size("dp").bit_length() - 1)]
    one, two = state
    for step in range(len(bits))[first:last]:
        one = jnp.concatenate([one, swap(one, "dp", bits[step])], axis=0)
        two = jnp.concatenate([two, swap(two, "dp", bits[::-1][step])], axis=0)
    return one, two


def dp_places():
    groups = lax.axis_size("dp")
    bits = groups.bit_length() - 1
    who = jnp.arange(groups, dtype=jnp.int32) ^ lax.axis_index("dp")
    turned = sum(((who >> i) & 1) << (bits - 1 - i) for i in range(bits))
    return jnp.stack([who, turned]).astype(jnp.int32)


def lay_kernel(places, one, two, into, out):
    place = out.at[0, 0] if len(out.shape) == 5 else out.at[0, 0, 0]
    place[0] = one[0]
    place[1] = two[0]


def dp_lay(state, into, at):
    one, two = state
    groups, half, width = one.shape
    shape = into.shape
    if isinstance(at, tuple):
        split = into.reshape(shape[0], shape[1], groups, 2, half, width)
        block = (1, 1, 1, 2, half, width)
        where = lambda c, places: (at[0], at[1], c, 0, 0, 0)
        second = jnp.zeros((1, groups), jnp.int32)
    else:
        split = into.reshape(groups, 2, 2, half, width)
        block = (1, 1, 2, half, width)
        where = lambda c, places: (c, places[2, c], 0, 0, 0)
        second = jnp.full((1, groups), at, jnp.int32)
    out = pl.pallas_call(
        lay_kernel,
        grid_spec=pltpu.PrefetchScalarGridSpec(
            num_scalar_prefetch=1,
            grid=(groups,),
            in_specs=[
                pl.BlockSpec((1, half, width), lambda c, places: (places[0, c], 0, 0)),
                pl.BlockSpec((1, half, width), lambda c, places: (places[1, c], 0, 0)),
                pl.BlockSpec(memory_space=pl.ANY),
            ],
            out_specs=pl.BlockSpec(block, where),
        ),
        out_shape=jax.ShapeDtypeStruct(split.shape, into.dtype),
        input_output_aliases={3: 0},
        name="lay",
    )(jnp.concatenate([dp_places(), second]), one, two, split)
    return out.reshape(shape)


def total_sum(buffer, between):
    stages = [("blk", 2, 1), ("dp", lax.axis_size("dp"), 1), ("blk", lax.axis_size("blk") // 2, 2)]
    for number, (axis, ways, unit) in enumerate(stages):
        part = buffer.shape[1] // ways
        mine = (lax.axis_index(axis) // unit) % ways
        cut = lambda d: lax.dynamic_slice_in_dim(buffer, (mine ^ d) * part, part, 1)
        arrived = [swap(cut(d), axis, d * unit) for d in range(1, ways)]
        buffer = between(functools.reduce(jnp.add, arrived, cut(0)), number)
    for number, (axis, ways, unit) in enumerate(stages[::-1]):
        part = buffer.shape[1]
        mine = (lax.axis_index(axis) // unit) % ways
        whole = blank((buffer.shape[0], ways * part), f32)
        for d in range(ways):
            piece = swap(buffer, axis, d * unit) if d else buffer
            whole = lax.dynamic_update_slice_in_dim(whole, piece, (mine ^ d) * part, 1)
        buffer = between(whole, 3 + number)
    return buffer


def sum_all(tables, vectors, between):
    devices = lax.axis_size("dp") * lax.axis_size("blk")
    flat = jnp.concatenate(vectors)
    extra = -flat.shape[0] % 1024
    flat = jnp.pad(flat, (0, extra)).reshape(8, -1)
    joined = jnp.concatenate(
        [t[i * 8 : (i + 1) * 8] for t in tables for i in range(2)] + [flat], axis=1
    )
    width = joined.shape[1]
    joined = jnp.pad(joined, ((0, 0), (0, -width % (128 * devices))))
    joined = total_sum(joined, between)
    out, at = [], 0
    for t in tables:
        size = t.shape[1]
        out.append(
            jnp.concatenate([joined[:, at : at + size], joined[:, at + size : at + 2 * size]], axis=0)
        )
        at += 2 * size
    flat = joined[:, at:width].reshape(-1)
    vecs, at = [], 0
    for v in vectors:
        vecs.append(flat[at : at + v.shape[0]])
        at += v.shape[0]
    return out, vecs


def per_device(
    tokens,
    cotangent,
    document_length_list,
    attention_norm_gain,
    feedforward_norm_gain,
    frozen_query_key_value,
    query_key_value_downmap,
    query_key_value_upmap,
    query_key_value_norm,
    frozen_output_weight,
    output_adapter_downmap,
    output_adapter_upmap,
    output_column_norm,
    frozen_gate_up_weight,
    gate_up_adapter_downmap,
    gate_up_adapter_upmap,
    gate_up_column_norm,
    frozen_down_weight,
    down_adapter_downmap,
    down_adapter_upmap,
    down_column_norm,
):
    length = tokens.shape[0]
    members, groups = lax.axis_size("blk"), lax.axis_size("dp")
    me, line = lax.axis_index("blk"), lax.axis_index("dp")
    count = length * members
    mates = members // QUAD
    wide = frozen_output_weight.shape[1]
    heads = wide // HDIM
    hidden = frozen_gate_up_weight.shape[2]
    lens_row = document_length_list[0]
    rank = ADAPTER_RANK
    flip = lambda a: jnp.swapaxes(a, -1, -2)

    def home(array, axis, width, who=None):
        return lax.dynamic_slice_in_dim(array, (me if who is None else who) * width, width, axis)

    def by_head(array):
        split = array.reshape(3, array.shape[1], heads, HDIM)
        return jnp.transpose(split, (1, 2, 0, 3)).reshape(array.shape[1], 3 * wide)

    def by_three(array):
        split = array.reshape(array.shape[0], heads, 3, HDIM)
        return jnp.transpose(split, (2, 0, 1, 3)).reshape(3, array.shape[0], wide)

    x_full = tokens.astype(f32)
    normed_one, inverse_one = normalize(x_full, attention_norm_gain)
    h_one = normed_one.astype(bf16)
    h_all = lax.all_gather(h_one, "blk", axis=0, tiled=True)

    w_out, n_out = merge(
        after(frozen_output_weight, h_one)[None],
        flip(output_adapter_downmap)[None],
        home(output_adapter_upmap, 1, wide)[None],
        home(output_column_norm, 0, wide)[None],
    )
    gu, n_gu = merge_rows(
        flip(frozen_gate_up_weight),
        flip(gate_up_adapter_downmap),
        home(gate_up_adapter_upmap, 2, hidden),
        home(gate_up_column_norm, 1, hidden)[:, :, None],
        mates,
    )
    b_qkv = home(query_key_value_upmap, 2, wide)
    m_qkv = by_head(home(query_key_value_norm, 1, wide)[:, None, :])
    w_qkv, n_qkv = merge(frozen_query_key_value, flip(query_key_value_downmap), b_qkv, m_qkv)
    w_down, n_down = merge(
        frozen_down_weight[None],
        flip(down_adapter_downmap)[None],
        home(down_adapter_upmap, 1, wide)[None],
        home(down_column_norm, 0, wide)[None],
    )
    places, begins, end = begins_of(lens_row, count)
    half = HDIM // 2
    freq = rope_base ** (-(jnp.arange(half, dtype=f32) * 2.0 / HDIM))
    angle = (places - begins).astype(f32)[:, None] * freq[None, :]
    cosine, sine = jnp.cos(angle), jnp.sin(angle)
    cosine = jnp.concatenate([cosine, cosine], axis=1)
    sine = jnp.concatenate([-sine, sine], axis=1)
    begin = begins[None, :]
    valid = (me * length + jnp.arange(length, dtype=jnp.int32)) < end
    d_final = cotangent.astype(f32) * valid.astype(f32)[:, None]
    d_final_low = d_final.astype(bf16)

    def spread_rows(chunks):
        got = lax.all_to_all(chunks, "blk", 0, 0, tiled=True)
        return jnp.transpose(got, (1, 0, 2)).reshape(chunks.shape[1], members * wide)

    def spread_rows(chunks):
        got = lax.all_to_all(chunks, "blk", 0, 0, tiled=True)
        return jnp.transpose(got, (1, 0, 2)).reshape(chunks.shape[1], members * wide)

    w_out, gu = after((w_out, gu), w_qkv, w_down, cosine, sine)
    piece = MODEL_WIDTH // (2 * groups)
    core = me % 2
    pair = lax.dynamic_slice_in_dim(w_out, 2 * line * piece, 2 * piece, 0)
    pair = pair.reshape(1, 2, piece, wide)
    mine = spread_rows(jnp.tile(pair, (members // 2, 1, 1, 1)).reshape(members, piece, wide))
    mine = dp_steps(dp_start(mine), 0, 1)
    piece = mates * hidden // groups
    per_shard = groups // mates
    turn = line // per_shard
    shards = lax.dynamic_slice_in_dim(
        after(w_down, w_out).reshape(mates, QUAD, hidden, wide),
        (line % per_shard) * piece,
        piece,
        2,
    )
    chosen = jnp.stack(
        [
            functools.reduce(
                lambda rest, k: jnp.where(turn == k, shards[q ^ k], rest),
                range(1, mates),
                shards[q],
            )
            for q in range(mates)
        ]
    ).reshape(members, piece, wide)
    own = jnp.concatenate([n_out[0], n_gu[0, :, 0], n_gu[1, :, 0], n_down[0]])
    own = jnp.pad(own, (0, -own.shape[0] % wide)).reshape(-1, wide)
    own_high = lax.reduce_precision(own, 8, 7)
    riders = jnp.concatenate([own_high, own - own_high], axis=0).astype(bf16)
    extra = -riders.shape[0] % 16
    riders = jnp.pad(riders, ((0, extra), (0, 0)))
    riders = jnp.broadcast_to(riders[None], (members, *riders.shape))
    rows_down = spread_rows(jnp.concatenate([chosen, riders], axis=1))
    norm_rows = rows_down[piece:].astype(f32)
    norms = norm_rows[: own.shape[0]] + norm_rows[own.shape[0] : 2 * own.shape[0]]
    norms = jnp.transpose(norms.reshape(own.shape[0], members, wide), (1, 0, 2))
    norms = norms.reshape(members, own.shape[0] * wide)
    rows_down = rows_down[:piece]
    piece_gu = hidden // groups
    gu_part = lax.dynamic_slice(
        gu, (0, 0, line * piece_gu, 0), (1, 2, piece_gu, MODEL_WIDTH)
    ).reshape(2, piece_gu, MODEL_WIDTH)
    gate_part = after(gu_part[0], rows_down)
    gate_parts = [swap(gate_part, "blk", QUAD * k) for k in range(1, mates)]
    h_all, d_final_low, mine, rows_down = after((h_all, d_final_low, mine, rows_down), cosine)

    mine = dp_steps(mine, 1, None)
    d_final_pair = jnp.concatenate([d_final_low, swap(d_final_low, "blk", 2)], axis=0)
    down_rows = lax.all_gather(rows_down, "dp", axis=0, tiled=True)
    triple = dot(h_all, w_qkv)
    q, k, v, attended_heads, mixed_t, lse = attention_forward(triple, cosine, sine, begin)


    attended_heads = after(attended_heads, mine, gate_parts, d_final_pair)
    one, two, d_final_pair, gate_parts = after(
        (*mine, d_final_pair, gate_parts), attended_heads
    )
    over = swap(one, "blk", 1), swap(two, "blk", 1)
    up_part = after(gu_part[1], attended_heads)
    up_parts = [swap(up_part, "blk", QUAD * k) for k in range(1, mates)]
    gate_states = [dp_steps(dp_start(g)) for g in gate_parts]
    out_full = blank((groups, 2, MODEL_WIDTH // (2 * groups), MODEL_WIDTH), bf16)
    out_full = dp_lay((one, two), out_full, core)
    out_full = dp_lay(over, out_full, 1 - core).reshape(MODEL_WIDTH, MODEL_WIDTH)
    attended = lax.all_to_all(
        attended_heads.reshape(members, length, wide), "blk", 0, 0, tiled=True
    )
    a_low = flip(query_key_value_downmap).astype(bf16).reshape(3 * rank, MODEL_WIDTH)
    h_all_late = after(h_all, attended_heads)
    xa_qkv = dot(a_low, h_all_late, NT).astype(bf16)
    aw_qkv = dot(a_low, w_qkv)
    attended = after(
        attended, xa_qkv, aw_qkv, out_full, gate_states, up_parts, down_rows
    )

    attended = jnp.transpose(attended, (1, 0, 2)).reshape(length, MODEL_WIDTH)
    a_out_low = flip(output_adapter_downmap).astype(bf16)
    y_out = dot(jnp.concatenate([attended, a_out_low], axis=0), out_full)
    y_out, aw_out = y_out[:length], y_out[length:]
    residual = x_full + y_out
    normed_two, inverse_two = normalize(residual, feedforward_norm_gain)
    h_two = normed_two.astype(bf16)
    up_parts = after(up_parts, attended)
    up_states = [dp_steps(dp_start(g), 0, 1) for g in up_parts]
    h_two = after(h_two, up_states)

    attended_late = after(attended, h_two)
    xa_out = dot(a_out_low, attended_late, NT).astype(bf16)
    gate_states = after(gate_states, h_two)
    up_states = [dp_steps(after(state, h_two), 1, None) for state in up_states]
    d_final_pair = after(d_final_pair, h_two)
    d_final_all = jnp.concatenate([d_final_pair, swap(d_final_pair, "blk", 1)], axis=0)
    for k_ in range(1, mates):
        gu = dp_lay(gate_states[k_ - 1], gu, (k_, 0))
        gu = dp_lay(up_states[k_ - 1], gu, (k_, 1))
    gu = gu.reshape(mates * 2 * hidden, MODEL_WIDTH)
    a_gu_low = flip(gate_up_adapter_downmap).astype(bf16).reshape(2 * rank, MODEL_WIDTH)
    norms_out = norms[:, :wide].reshape(-1)
    norms_down = norms[:, wide + 2 * hidden : 2 * wide + 2 * hidden].reshape(-1)

    h_two_all = after(quad_gather(h_two), xa_out, gu, down_rows)
    acts, g_gu, gm_gu = feed_forward(gu, down_rows, h_two_all, d_final_all, mates)
    dh_parts = dot(g_gu, gu, TN).astype(bf16)
    dh_half = quad_halve(dh_parts)
    dh_two = quad_finish(dh_half)

    acts_late, down_late, h_two_late, gu_late = after(
        (acts, down_rows, h_two_all, gu), dh_half
    )
    y_parts = dot(acts_late, down_late, TN).astype(bf16)
    a_down_low = flip(down_adapter_downmap).astype(bf16)
    order = [me ^ (QUAD * k_) for k_ in range(mates)]
    low = jnp.concatenate([home(a_down_low, 1, hidden, who) for who in order], axis=1)
    xa_down = dot(low, acts_late).astype(bf16)
    aw_down = dot(low, down_late)
    xa_gu = dot(a_gu_low, h_two_late, NT).astype(bf16)
    aw_gu = dot(a_gu_low, gu_late, NT)
    dh_two = after(dh_two, y_parts, xa_down, aw_down, xa_gu, aw_gu)

    d_norm_two = normalize_back(residual, inverse_two, feedforward_norm_gain, dh_two)
    d_residual = d_final + d_norm_two
    g_out = d_residual.astype(bf16)
    d_attended = dot(g_out, out_full, NT).astype(bf16)
    d_parts = jnp.transpose(d_attended.reshape(length, members, wide), (1, 0, 2))
    d_heads = lax.all_to_all(d_parts, "blk", 0, 0, tiled=True).reshape(count, wide)

    y_down = quad_finish(quad_halve(after(y_parts, d_parts)))
    result = (residual + y_down).astype(bf16)
    g_late, h_two_late, gu_late, gm_gu = after((g_gu, h_two_all, gu, gm_gu), d_parts)

    def joined(pick):
        return jnp.concatenate([pick(who, i) for who in order for i in range(2)], axis=-1)

    m_gu = joined(lambda who, i: home(gate_up_column_norm[i], 0, hidden, who))
    n_gu_all = joined(
        lambda who, i: lax.dynamic_slice(norms, (who, wide + i * hidden), (1, hidden))[0]
    )
    b_gu = joined(lambda who, i: home(gate_up_adapter_upmap[i], 1, hidden, who))
    s_gu = m_gu / n_gu_all
    gm_gu = gm_gu.reshape(-1) / m_gu
    row = lax.broadcasted_iota(jnp.int32, (2 * rank, b_gu.shape[1]), 0) // rank
    column = (lax.broadcasted_iota(jnp.int32, (2 * rank, b_gu.shape[1]), 1) // hidden) % 2
    own_gu = row == column
    spread = jnp.where(own_gu, jnp.tile(b_gu, (2, 1)), 0.0)
    p_gu = dot((spread * s_gu).astype(bf16), g_late).astype(bf16)
    tilt = (spread * (gm_gu / n_gu_all)).astype(bf16)
    ga_gu = adapter_scale * (dot(p_gu, h_two_late) - dot(tilt, gu_late))
    gb_gu = adapter_scale * (dot(xa_gu, g_late, NT) * s_gu - aw_gu * (gm_gu / n_gu_all))
    gb_gu = jnp.sum(jnp.where(own_gu, gb_gu, 0.0).reshape(2, rank, -1), axis=0)
    d_heads = after(d_heads, ga_gu, gb_gu)

    g_three, gm_heads = attention_backward(
        q, k, v, triple, cosine, sine, begin, d_heads, mixed_t, lse
    )
    g_three = after(g_three, y_down)
    dh_parts = dot(g_three, w_qkv, NT).astype(bf16)
    total = core_scatter(dh_parts)
    acts_late, d_final_late, y_down, dh_late, unit_two, g_out, out_late = after(
        (acts, d_final_all, y_down, dh_two, residual * inverse_two, g_out, out_full), total
    )
    grad_g_ffn = jnp.sum(dh_late * unit_two, axis=0)
    gm_down = jnp.sum(d_final_low.astype(f32) * y_down, axis=0) / down_column_norm
    gm_quad = gm_down + swap(gm_down, "blk", 1)
    gm_quad = gm_quad + swap(gm_quad, "blk", 2)
    s_down = down_column_norm / norms_down
    p_down = dot((down_adapter_upmap * s_down).astype(bf16), d_final_late, NT).astype(bf16)
    tilt_down = (down_adapter_upmap * (gm_quad / norms_down)).astype(bf16)
    ga_down = adapter_scale * (dot(p_down, acts_late, NT) - dot(tilt_down, down_rows, NT))
    gb_down = adapter_scale * (
        dot(xa_down, d_final_late) * s_down - aw_down * (gm_quad / norms_down)
    )
    gm_out = jnp.sum(g_out.astype(f32) * y_out, axis=0) / output_column_norm
    s_out = output_column_norm / norms_out
    p_out = dot((output_adapter_upmap * s_out).astype(bf16), g_out, NT).astype(bf16)
    tilt_out = (output_adapter_upmap * (gm_out / norms_out)).astype(bf16)
    ga_out = adapter_scale * (dot(p_out, attended) - dot(tilt_out, out_late, NT))
    gb_out = adapter_scale * (dot(xa_out, g_out) * s_out - aw_out * (gm_out / norms_out))

    state = chips_step(total, 1, None)
    state = after(state, ga_down, gb_down, ga_out, gb_out, grad_g_ffn)
    g_three, gm_heads, h_all_late = after((g_three, gm_heads, h_all), state)
    chips = members // 2

    gm = gm_heads[0:1] / m_qkv
    s_qkv = m_qkv / n_qkv
    row = lax.broadcasted_iota(jnp.int32, (3 * rank, 3 * wide), 0) // rank
    column = (lax.broadcasted_iota(jnp.int32, (3 * rank, 3 * wide), 1) // HDIM) % 3
    own_block = row == column
    spread = jnp.where(own_block, jnp.tile(by_head(b_qkv), (3, 1)), 0.0)
    p = dot((spread * s_qkv).astype(bf16), g_three, NT).astype(bf16)
    tilt = (spread * (gm / n_qkv)).astype(bf16)
    grad_a = adapter_scale * (dot(p, h_all_late) - dot(tilt, w_qkv, NT))
    grad_b = adapter_scale * (dot(xa_qkv, g_three) * s_qkv - aw_qkv * (gm / n_qkv))
    grad_b = jnp.sum(jnp.where(own_block, grad_b, 0.0).reshape(3, rank, 3 * wide), axis=0)
    grad_b = by_three(grad_b)
    grad_m = by_three(gm)[:, 0]
    grad_g_attn = (
        jnp.sum(dh_parts.astype(f32) * h_all_late.astype(f32), axis=0) / attention_norm_gain
    )


    for t in range(2, chips - 1):
        state = chips_step(total, t, state)
        state = after(state, grad_a, grad_b, grad_g_attn)
    grad_a, grad_b, grad_m, ga_gu, gb_gu = after((grad_a, grad_b, grad_m, ga_gu, gb_gu), state)
    ends = {}

    def between(buffer, stage):
        if stage == 1:
            ends[0] = after(chips_step(total, chips - 1, state), buffer)
            buffer = after(buffer, ends[0])
        return buffer

    def placed(array, total, k_, i):
        part = array[..., (2 * k_ + i) * hidden : (2 * k_ + i + 1) * hidden]
        return lax.dynamic_update_slice_in_dim(total, part, order[k_] * hidden, array.ndim - 1)

    units = members * hidden
    all_b, all_m = [], []
    for i in range(2):
        tall, thin = jnp.zeros((rank, units), f32), jnp.zeros((units,), f32)
        for k_ in range(mates):
            tall, thin = placed(gb_gu, tall, k_, i), placed(gm_gu, thin, k_, i)
        all_b.append(tall)
        all_m.append(thin)
    all_a = jnp.zeros((rank, units), f32)
    for k_ in range(mates):
        all_a = lax.dynamic_update_slice_in_dim(
            all_a, ga_down[:, k_ * hidden : (k_ + 1) * hidden], order[k_] * hidden, 1
        )
    empty = jnp.zeros((rank, MODEL_WIDTH), f32)
    tables, vectors = sum_all(
        [grad_a[i * rank : (i + 1) * rank] for i in range(3)]
        + [lax.dynamic_update_slice_in_dim(empty, grad_b[i], me * wide, 1) for i in range(3)]
        + [ga_out, gb_out, ga_gu[:rank], ga_gu[rank:], gb_down]
        + [*all_b, all_a],
        [grad_g_attn, grad_g_ffn, gm_out, gm_down]
        + [lax.dynamic_update_slice_in_dim(empty[0], grad_m[i], me * wide, 0) for i in range(3)]
        + all_m,
        between,
    )
    d_norm_one = normalize_back(x_full, inverse_one, attention_norm_gain, chips_end(total, ends[0]))
    grad_input = d_residual + d_norm_one
    a_out, b_out, a_gate, a_up, b_down, b_gate, b_up, a_down = tables[6:]
    return (
        result,
        grad_input,
        vectors[0],
        vectors[1],
        flip(jnp.stack(tables[:3])),
        jnp.stack(tables[3:6]),
        jnp.stack(vectors[4:7]),
        flip(a_out),
        b_out,
        vectors[2],
        flip(jnp.stack([a_gate, a_up])),
        jnp.stack([b_gate, b_up]),
        jnp.stack(vectors[7:]),
        flip(a_down),
        b_down,
        vectors[3],
    )


def solution(mesh):
    rows, none = P(("dp", "blk"), None), P()
    in_specs = (
        rows,
        rows,
        P("dp", None),
        none,
        none,
        P(None, None, "blk"),
        none,
        none,
        none,
        P(None, "blk"),
        none,
        none,
        none,
        P(None, None, "blk"),
        none,
        none,
        none,
        P(None, "blk"),
        none,
        none,
        none,
    )
    out_specs = (rows, rows) + (none,) * 14
    return jax.shard_map(
        per_device, mesh=mesh, in_specs=in_specs, out_specs=out_specs, check_vma=False
    )
```

time: 3180 us -> 776 us (0.24)
  matrix products: 1460 us -> 121 us
  waiting for transfers between devices: 1010 us -> 194 us
  starting transfers between devices: 215 us -> 82.8 us
  local copies, waits for them, and re-layouts: 246 us -> 118 us
  Pallas kernels: 0 us -> 119 us
  other arithmetic: 191 us -> 113 us
    dot_general x266 -> x22, matrix products: 1460 us -> 121 us  [dot(): return lax.dot_general(a, b, dims, preferred_element_type=f32)]
    all_gather x6 -> x2, waiting for transfers between devices: 702 us -> 0.01 us  [the longest x1 0.01 us: per_device(): h_all = lax.all_gather(h_one, 'blk', axis=0, tiled=True)]
    psum x2 -> x0, waiting for transfers between devices: 290 us -> none  [per_device(): lax.psum((grad_g_attn, grad_g_ffn, grad_a_qkv, grad_b_qkv, grad_m_qkv, gr...]
    ppermute x32 -> x47, starting transfers between devices: 214 us -> 61.9 us  [the longest x41 37.8 us: swap(): lax.ppermute(array, axis, [(i, i ^ bit) for i in range(lax.axis_size(axis...]
    ppermute x32 -> x47, waiting for transfers between devices: 15.5 us -> 142 us  [the longest x41 114 us: swap(): lax.ppermute(array, axis, [(i, i ^ bit) for i in range(lax.axis_size(axis...]
    pallas_call x0 -> x15, Pallas kernels: none -> 119 us  [the longest x1 35 us: feed_forward(): pl.pallas_call(feed_kernel, grid=(mates, steps), in_specs=[pl.BlockSpec((...]
    while x304 -> x0, local copies, waits for them, and re-layouts: 77.7 us -> none
    all_to_all x0 -> x4, waiting for transfers between devices: none -> 51.8 us  [the longest x2 51.8 us: spread_rows(): got = lax.all_to_all(chunks, 'blk', 0, 0, tiled=True)]
  transfers between devices with their start and end apart: 40 -> 53, of which waited for: 16 -> 26; matrix products, arithmetic and copies ran while one was open for 13% -> 26% of each run, Pallas kernels for 0% -> 11%
where the time goes in v1:
time: 776 us; the launch traced here: 764 us
  waiting for transfers between devices  194 us (25%)
  matrix products  121 us (16%)
  Pallas kernels  119 us (15%)
  local copies, waits for them, and re-layouts  118 us (15%)
  other arithmetic  113 us (15%)
  starting transfers between devices  82.8 us (11%)
  between operations  16.3 us (2%)
    dot_general x22, matrix products, dot(): return lax.dot_general(a, b, dims, preferred_element_type=f32)  121 us
    ppermute x41, waiting for transfers between devices, swap(): lax.ppermute(array, axis, [(i, i ^ bit) for i in range(lax.axis_size(axis...  114 us
    all_to_all x2, waiting for transfers between devices, spread_rows(): got = lax.all_to_all(chunks, 'blk', 0, 0, tiled=True)  51.8 us
    unnamed x296, local copies, waits for them, and re-layouts  40.9 us
    ppermute x41, starting transfers between devices, swap(): lax.ppermute(array, axis, [(i, i ^ bit) for i in range(lax.axis_size(axis...  37.8 us
    pallas_call x1, Pallas kernels, feed_forward(): pl.pallas_call(feed_kernel, grid=(mates, steps), in_specs=[pl.BlockSpec((...  35 us
    ppermute x6, waiting for transfers between devices, step_chips(): return lax.ppermute(array, 'blk', pairs)  28 us
    ppermute x6, starting transfers between devices, step_chips(): return lax.ppermute(array, 'blk', pairs)  24.1 us
  transfers between devices with their start and end apart: 53, of which 26 were waited for; matrix products, arithmetic and copies ran while one was open for 26% of the time, Pallas kernels for 11%

profile of v1, /device:TPU:0, one launch (start us, length us, event | category | flops | bytes accessed | tf_op | source)
XLA Modules:
  0.0 764.0 jit_solution(10688900647673055380)
XLA Ops:
  20.0 7.5 merge.5
  29.4 7.9 %merge.4 = (bf16[2048,768]{1,0:T(8,128)(2,1)S(1)}, f32[1,768]{1,0:T(1,128)S(1)}) custom-call(bf16[3,2048,256]{2,1,0:T(8,128)(2,1)} %w_ref.1, bf16[3,96,2048]{2,1,0:T(8,128)(2,1)S(1)} %fusion.49.a_ref, bf16[3,96,256]{2,1,0:T(8,128)(2,1)S(1)} %constant_dynamic-update-slice_fusion.29.b_ref, f32[1,768]{1,0:T(1,128)S(1)} %reshape.413.m_ref), custom_call_target="tpu_custom_call" | custom-call | flops 301989888 | bytes 6291456 | tf_op jit(solution)/shard_map/merge/pallas_call | solution.py:109
  39.0 7.4 merge_rows.1
  54.4 6.3 all-to-all-start
  65.2 43.2 %all-to-all-done = bf16[8,256,256]{2,1,0:T(8,128)(2,1)} async-done(((bf16[8,256,256]{2,1,0:T(8,128)(2,1)}), bf16[8,256,256]{2,1,0:T(8,128)(2,1)}, u32[]{:S(2)}, u32[]{:S(2)}) %all-to-all-start) | async-done | bytes 1048608 | tf_op jit(solution)/shard_map/all_to_all | solution.py:660
  140.4 8.7 %all-to-all-done.1 = bf16[8,368,256]{2,1,0:T(8,128)(2,1)} async-done(((bf16[8,368,256]{2,1,0:T(8,128)(2,1)}), bf16[8,368,256]{2,1,0:T(8,128)(2,1)}, u32[]{:S(2)}, u32[]{:S(2)}) %all-to-all-start.1) | async-done | bytes 1507360 | tf_op jit(solution)/shard_map/all_to_all | solution.py:660
  156.2 10.0 %fusion.122.pre = f32[1792,768]{1,0:T(8,128)} fusion(bf16[1792,2048]{1,0:T(8,128)(2,1)} %all-gather.3.cloned.1.call-done, bf16[2048,768]{1,0:T(8,128)(2,1)S(1)} %get-tuple-element.105), kind=kOutput, calls=%fused_computation.447 | convolution fusion | flops 5637144576 | bytes 15990784 | tf_op jit(solution)/shard_map/dot_general | solution.py:31
  170.0 20.6 %attend.1 = (bf16[1792,256]{1,0:T(8,128)(2,1)S(1)}, bf16[1792,256]{1,0:T(8,128)(2,1)S(1)}, bf16[1792,256]{1,0:T(8,128)(2,1)S(1)}, bf16[1792,256]{1,0:T(8,128)(2,...) custom-call(f32[1792,768]{1,0:T(8,128)} %fusion.122.pre, f32[1792,128]{1,0:T(8,128)S(1)} %copy-done.4, ...), custom_call_target="tpu_custom_call" | custom-call | flops 1644167168 | bytes 13762560 | tf_op jit(solution)/shard_map/attend/pallas_call | solution.py:281
  194.2 9.9 %collective-permute-done.3 = bf16[2,128,2048]{2,1,0:T(8,128)(2,1)S(1)} collective-permute-done((bf16[2,128,2048]{2,1,0:T(8,128)(2,1)S(1)}, bf16[2,128,2048]{2,1,0:T(8,128)(2,1)S(1)}, u32[]{:S(2)}, u32[]{:S(2)}) %collective-permute-start.3) | collective-permute-done | bytes 1048608 | tf_op jit(solution)/shard_map/ppermute | solution.py:48
  216.3 9.5 %collective-permute-done.10 = bf16[1,88,2048]{2,1,0:T(8,128)(2,1)} collective-permute-done((bf16[1,88,2048]{2,1,0:T(8,128)(2,1)}, bf16[1,88,2048]{2,1,0:T(8,128)(2,1)}, u32[]{:S(2)}, u32[]{:S(2)}) %collective-permute-start.10) | collective-permute-done | bytes 360480 | tf_op jit(solution)/shard_map/ppermute | solution.py:48
  241.7 12.2 %collective-permute-done.11 = bf16[2,88,2048]{2,1,0:T(8,128)(2,1)} collective-permute-done((bf16[2,88,2048]{2,1,0:T(8,128)(2,1)}, bf16[2,88,2048]{2,1,0:T(8,128)(2,1)}, u32[]{:S(2)}, u32[]{:S(2)}) %collective-permute-start.11) | collective-permute-done | bytes 720928 | tf_op jit(solution)/shard_map/ppermute | solution.py:48
  264.5 6.5 collective-permute-done.12
  283.9 6.2 collective-permute-done.14
  294.2 18.7 %collective-permute-done.17 = bf16[224,2048]{1,0:T(8,128)(2,1)S(1)} collective-permute-done((bf16[224,2048]{1,0:T(8,128)(2,1)S(1)}, bf16[224,2048]{1,0:T(8,128)(2,1)S(1)}, u32[]{:S(2)}, u32[]{:S(2)}) %collective-permute-start.17) | collective-permute-done | bytes 917536 | tf_op jit(solution)/shard_map/ppermute | solution.py:48
  339.4 35.0 %feed_forward.1 = (bf16[1408,896]{1,0:T(8,128)(2,1)S(1)}, bf16[2,2,704,896]{3,2,1,0:T(8,128)(2,1)}, f32[2,2,704,1]{3,2,1,0:T(8,128)S(1)}) custom-call(bf16[2,2,704,2048]{3,2,1,0:T(8,128)(2,1)} %bitcast.388, bf16[1408,2048]{1,0:T(8,128)(2,1)} %all-gather.5.cloned.1.call-done.down_ref, bf16[896,2048]{1,0:T(8,128)(2,1)} %pad_maximum_fusion.h_ref, ...), custom_call_target="tpu_custom_call" | custom-call | flops 15502147584 | bytes 24641536 | tf_op jit(solution)/shard_map/feed_forward/pallas_call | solution.py:375
  374.4 16.5 %convolution_convert_fusion.1 = bf16[896,2048]{1,0:T(8,128)(2,1)S(1)} fusion(bf16[2816,896]{1,0:T(8,128)(2,1)} %bitcast.404, bf16[2816,2048]{1,0:T(8,128)(2,1)} %bitcast.389), kind=kOutput, calls=%fused_computation.8 | convolution fusion | flops 10336600064 | bytes 20250624 | tf_op jit(solution)/shard_map/dot_general | solution.py:31
  404.7 8.5 %convolution_convert_fusion.2 = bf16[896,2048]{1,0:T(8,128)(2,1)S(1)} fusion(bf16[1408,896]{1,0:T(8,128)(2,1)S(1)} %copy-done.3, bf16[1408,2048]{1,0:T(8,128)(2,1)} %all-gather.5.cloned.1.call-done.down_ref), kind=kOutput, calls=%fused_computation.9 | convolution fusion | flops 5169217536 | bytes 11960320 | tf_op jit(solution)/shard_map/dot_general | solution.py:31
  419.7 7.0 collective-permute-done.21
  455.1 7.1 fusion.3
  462.3 6.1 fusion.33
  476.7 7.1 fusion.8
  489.7 17.8 %attend_back.1 = (bf16[1792,768]{1,0:T(8,128)(2,1)}, f32[8,768]{1,0:T(8,128)S(1)}) custom-call(bf16[1792,256]{1,0:T(8,128)(2,1)S(1)} %copy-done.16, bf16[1792,256]{1,0:T(8,128)(2,1)S(1)} %copy-done.18, bf16[1792,256]{1,0:T(8,128)(2,1)S(1)} %copy-done.20, f32[1792,768]{1,0:T(8,128)} %fusion.122.pre, f32[1792,128]{1,0:T(8,128)S(1)} %copy-done.5, ...), custom_call_target="tpu_custom_call" | custom-call | flops 4110417920 | bytes 18350080 | tf_op jit(solution)/shard_map/attend_back/pallas_call | solution.py:318
  511.0 6.3 convolution_convert_fusion
  528.1 7.0 fusion
  551.8 6.5 fusion.14
  558.6 8.0 %collective-permute-done.28 = f32[2048]{0:T(1024)S(1)} collective-permute-done((f32[2048]{0:T(1024)S(1)}, f32[2048]{0:T(1024)S(1)}, u32[]{:S(2)}, u32[]{:S(2)}) %collective-permute-start.28) | collective-permute-done | bytes 8224 | tf_op jit(solution)/shard_map/ppermute | solution.py:48
  585.0 8.2 %multiply_reduce_fusion = f32[2048]{0:T(1024)S(1)} fusion(bf16[1792,2048]{1,0:T(8,128)(2,1)} %all-gather.3.cloned.1.call-done, bf16[1792,2048]{1,0:T(8,128)(2,1)} %copy-done.29), kind=kLoop, calls=%fused_computation | loop fusion | flops 14678016 | bytes 14688256 | tf_op jit(solution)/shard_map/reduce_sum | solution.py:861
  596.2 7.1 fusion.32
  617.0 6.9 fusion.29
  626.8 7.1 collective-permute-done.29
  668.9 10.8 %collective-permute-start.31 = (bf16[224,2048]{1,0:T(8,128)(2,1)S(1)}, bf16[224,2048]{1,0:T(8,128)(2,1)S(1)}, u32[]{:S(2)}, u32[]{:S(2)}) collective-permute-start(bf16[224,2048]{1,0:T(8,128)(2,1)S(1)} %get-tuple-element.178), channel_id=1, source_target_pairs={{0,2},{1,3},{2,4},{3,5},{4,6},{5,7},{8,10},{9,11},{10,12},{11,13},... | collective-permute-start | bytes 2752520 | tf_op jit(solution)/shard_map/ppermute | solution.py:433
  682.0 16.7 %collective-permute-done.31 = bf16[224,2048]{1,0:T(8,128)(2,1)S(1)} collective-permute-done((bf16[224,2048]{1,0:T(8,128)(2,1)S(1)}, bf16[224,2048]{1,0:T(8,128)(2,1)S(1)}, u32[]{:S(2)}, u32[]{:S(2)}) %collective-permute-start.31) | collective-permute-done | bytes 917536 | tf_op jit(solution)/shard_map/ppermute | solution.py:433
  (666 shorter events, 383.5 us)
Async XLA Ops:
  7.2 144.6 %all-gather.3.cloned.1.call-start = ((), (), s32[]{:S(2)}) async-start(), calls=%async_computation.4 | async-start | bytes 8257536 | tf_op jit(solution)/shard_map/all_gather | solution.py:619
  54.4 54.0 %all-to-all-start = ((bf16[8,256,256]{2,1,0:T(8,128)(2,1)}), bf16[8,256,256]{2,1,0:T(8,128)(2,1)}, u32[]{:S(2)}, u32[]{:S(2)}) async-start(bf16[8,256,256]{2,1,0:T(8,128)(2,1)} %bitcast.413), calls=%async_computation | async-start | bytes 2097152 | tf_op jit(solution)/shard_map/all_to_all | solution.py:660
  108.4 40.7 %all-to-all-start.1 = ((bf16[8,368,256]{2,1,0:T(8,128)(2,1)}), bf16[8,368,256]{2,1,0:T(8,128)(2,1)}, u32[]{:S(2)}, u32[]{:S(2)}) async-start(bf16[8,368,256]{2,1,0:T(8,128)(2,1)} %pad_maximum_fusion.2), calls=%async_computation.1 | async-start | bytes 3014656 | tf_op jit(solution)/shard_map/all_to_all | solution.py:660
  112.7 158.3 %all-gather.5.cloned.1.call-start = ((), (), s32[]{:S(2)}) async-start(), calls=%async_computation.5 | async-start | bytes 7208960 | tf_op jit(solution)/shard_map/all_gather | solution.py:712
  154.3 52.1 %collective-permute-start.4 = (bf16[176,2048]{1,0:T(8,128)(2,1)S(1)}, bf16[176,2048]{1,0:T(8,128)(2,1)S(1)}, u32[]{:S(2)}, u32[]{:S(2)}) collective-permute-start(bf16[176,2048]{1,0:T(8,128)(2,1)S(1)} %get-tuple-element.117), channel_id=1, source_target_pairs={{0,4},{1,5},{2,6},{3,7},{4,0},{5,1},{6,2},{7,3},{8,12},{9,13},{10,... | collective-permute-start | bytes 2162696 | tf_op jit(solution)/shard_map/ppermute | solution.py:48
  154.4 38.7 %collective-permute-start.5 = (bf16[224,2048]{1,0:T(8,128)(2,1)S(1)}, bf16[224,2048]{1,0:T(8,128)(2,1)S(1)}, u32[]{:S(2)}, u32[]{:S(2)}) collective-permute-start(bf16[224,2048]{1,0:T(8,128)(2,1)S(1)} %copy-done.48), channel_id=1, source_target_pairs={{0,2},{1,3},{2,0},{3,1},{4,6},{5,7},{6,4},{7,5},{8,10},{9,11},{10,... | collective-permute-start | bytes 2752520 | tf_op jit(solution)/shard_map/ppermute | solution.py:48
  166.2 37.9 %collective-permute-start.3 = (bf16[2,128,2048]{2,1,0:T(8,128)(2,1)S(1)}, bf16[2,128,2048]{2,1,0:T(8,128)(2,1)S(1)}, u32[]{:S(2)}, u32[]{:S(2)}) collective-permute-start(bf16[2,128,2048]{2,1,0:T(8,128)(2,1)S(1)} %copy-done.52), channel_id=1, source_target_pairs={{0,8},{8,0},{16,24},{24,16},{1,9},{9,1},{17,25},{25,17},{2,10},{10... | collective-permute-start | bytes 3145736 | tf_op jit(solution)/shard_map/ppermute | solution.py:48
  167.6 37.7 %collective-permute-start.2 = (bf16[2,128,2048]{2,1,0:T(8,128)(2,1)S(1)}, bf16[2,128,2048]{2,1,0:T(8,128)(2,1)S(1)}, u32[]{:S(2)}, u32[]{:S(2)}) collective-permute-start(bf16[2,128,2048]{2,1,0:T(8,128)(2,1)S(1)} %copy-done.51), channel_id=1, source_target_pairs={{0,16},{8,24},{16,0},{24,8},{1,17},{9,25},{17,1},{25,9},{2,18},{10... | collective-permute-start | bytes 3145736 | tf_op jit(solution)/shard_map/ppermute | solution.py:48
  207.3 18.4 %collective-permute-start.10 = (bf16[1,88,2048]{2,1,0:T(8,128)(2,1)}, bf16[1,88,2048]{2,1,0:T(8,128)(2,1)}, u32[]{:S(2)}, u32[]{:S(2)}) collective-permute-start(bf16[1,88,2048]{2,1,0:T(8,128)(2,1)} %get-tuple-element.266), channel_id=1, source_target_pairs={{0,16},{8,24},{16,0},{24,8},{1,17},{9,25},{17,1},{25,9},{2,18},{10... | collective-permute-start | bytes 1081352 | tf_op jit(solution)/shard_map/ppermute | solution.py:48
  208.7 20.4 %collective-permute-start.8 = (bf16[1,88,2048]{2,1,0:T(8,128)(2,1)}, bf16[1,88,2048]{2,1,0:T(8,128)(2,1)}, u32[]{:S(2)}, u32[]{:S(2)}) collective-permute-start(bf16[1,88,2048]{2,1,0:T(8,128)(2,1)} %get-tuple-element.267), channel_id=1, source_target_pairs={{0,8},{8,0},{16,24},{24,16},{1,9},{9,1},{17,25},{25,17},{2,10},{10... | collective-permute-start | bytes 1081352 | tf_op jit(solution)/shard_map/ppermute | solution.py:48
  209.3 49.7 %collective-permute-start.6 = (bf16[4,128,2048]{2,1,0:T(8,128)(2,1)}, bf16[4,128,2048]{2,1,0:T(8,128)(2,1)}, u32[]{:S(2)}, u32[]{:S(2)}) collective-permute-start(bf16[4,128,2048]{2,1,0:T(8,128)(2,1)} %constant_dynamic-update-slice_fusion.46.one), channel_id=1, source_target_pairs={{0,1},{1,0},{2,3},{3,2},{4,5},{5,4},{6,7},{7,6},{8,9},{9,8},{10,11... | collective-permute-start | bytes 6291464 | tf_op jit(solution)/shard_map/ppermute | solution.py:48
  209.3 49.7 %collective-permute-start.7 = (bf16[4,128,2048]{2,1,0:T(8,128)(2,1)}, bf16[4,128,2048]{2,1,0:T(8,128)(2,1)}, u32[]{:S(2)}, u32[]{:S(2)}) collective-permute-start(bf16[4,128,2048]{2,1,0:T(8,128)(2,1)} %constant_dynamic-update-slice_fusion.48.two), channel_id=1, source_target_pairs={{0,1},{1,0},{2,3},{3,2},{4,5},{5,4},{6,7},{7,6},{8,9},{9,8},{10,11... | collective-permute-start | bytes 6291464 | tf_op jit(solution)/shard_map/ppermute | solution.py:48
  211.1 59.9 %all-to-all-start.2 = ((bf16[8,224,256]{2,1,0:T(8,128)(2,1)}), bf16[8,224,256]{2,1,0:T(8,128)(2,1)}, u32[]{:S(2)}, u32[]{:S(2)}) async-start(bf16[8,224,256]{2,1,0:T(8,128)(2,1)} %bitcast.381), calls=%async_computation.2 | async-start | bytes 1835008 | tf_op jit(solution)/shard_map/all_to_all | solution.py:728
  227.7 26.1 %collective-permute-start.11 = (bf16[2,88,2048]{2,1,0:T(8,128)(2,1)}, bf16[2,88,2048]{2,1,0:T(8,128)(2,1)}, u32[]{:S(2)}, u32[]{:S(2)}) collective-permute-start(bf16[2,88,2048]{2,1,0:T(8,128)(2,1)} %pad_maximum_fusion.13), channel_id=1, source_target_pairs={{0,8},{8,0},{16,24},{24,16},{1,9},{9,1},{17,25},{25,17},{2,10},{10... | collective-permute-start | bytes 2162696 | tf_op jit(solution)/shard_map/ppermute | solution.py:48
  231.2 25.2 %collective-permute-start.9 = (bf16[2,88,2048]{2,1,0:T(8,128)(2,1)}, bf16[2,88,2048]{2,1,0:T(8,128)(2,1)}, u32[]{:S(2)}, u32[]{:S(2)}) collective-permute-start(bf16[2,88,2048]{2,1,0:T(8,128)(2,1)} %pad_maximum_fusion.12), channel_id=1, source_target_pairs={{0,16},{8,24},{16,0},{24,8},{1,17},{9,25},{17,1},{25,9},{2,18},{10... | collective-permute-start | bytes 2162696 | tf_op jit(solution)/shard_map/ppermute | solution.py:48
  233.2 37.8 %collective-permute-start.12 = (bf16[176,2048]{1,0:T(8,128)(2,1)}, bf16[176,2048]{1,0:T(8,128)(2,1)}, u32[]{:S(2)}, u32[]{:S(2)}) collective-permute-start(bf16[176,2048]{1,0:T(8,128)(2,1)} %get-tuple-element.123), channel_id=1, source_target_pairs={{0,4},{1,5},{2,6},{3,7},{4,0},{5,1},{6,2},{7,3},{8,12},{9,13},{10,... | collective-permute-start | bytes 2162696 | tf_op jit(solution)/shard_map/ppermute | solution.py:48
  292.3 20.7 %collective-permute-start.17 = (bf16[224,2048]{1,0:T(8,128)(2,1)S(1)}, bf16[224,2048]{1,0:T(8,128)(2,1)S(1)}, u32[]{:S(2)}, u32[]{:S(2)}) collective-permute-start(bf16[224,2048]{1,0:T(8,128)(2,1)S(1)} %get-tuple-element.127), channel_id=1, source_target_pairs={{0,2},{1,3},{2,0},{3,1},{4,6},{5,7},{6,4},{7,5},{8,10},{9,11},{10,... | collective-permute-start | bytes 2752520 | tf_op jit(solution)/shard_map/ppermute | solution.py:48
  292.3 40.9 %collective-permute-start.19 = (bf16[448,2048]{1,0:T(8,128)(2,1)}, bf16[448,2048]{1,0:T(8,128)(2,1)}, u32[]{:S(2)}, u32[]{:S(2)}) collective-permute-start(bf16[448,2048]{1,0:T(8,128)(2,1)} %constant_dynamic-update-slice_fusion.50), channel_id=1, source_target_pairs={{0,1},{1,0},{2,3},{3,2},{4,5},{5,4},{6,7},{7,6},{8,9},{9,8},{10,11... | collective-permute-start | bytes 5505032 | tf_op jit(solution)/shard_map/ppermute | solution.py:48
  292.3 31.0 %collective-permute-start.16 = (bf16[2,88,2048]{2,1,0:T(8,128)(2,1)}, bf16[2,88,2048]{2,1,0:T(8,128)(2,1)}, u32[]{:S(2)}, u32[]{:S(2)}) collective-permute-start(bf16[2,88,2048]{2,1,0:T(8,128)(2,1)} %pad_maximum_fusion.15), channel_id=1, source_target_pairs={{0,8},{8,0},{16,24},{24,16},{1,9},{9,1},{17,25},{25,17},{2,10},{10... | collective-permute-start | bytes 2162696 | tf_op jit(solution)/shard_map/ppermute | solution.py:48
  293.4 32.4 %collective-permute-start.15 = (bf16[2,88,2048]{2,1,0:T(8,128)(2,1)}, bf16[2,88,2048]{2,1,0:T(8,128)(2,1)}, u32[]{:S(2)}, u32[]{:S(2)}) collective-permute-start(bf16[2,88,2048]{2,1,0:T(8,128)(2,1)} %pad_maximum_fusion.14), channel_id=1, source_target_pairs={{0,16},{8,24},{16,0},{24,8},{1,17},{9,25},{17,1},{25,9},{2,18},{10... | collective-permute-start | bytes 2162696 | tf_op jit(solution)/shard_map/ppermute | solution.py:48
  314.5 21.8 %collective-permute-start.18 = (bf16[448,2048]{1,0:T(8,128)(2,1)}, bf16[448,2048]{1,0:T(8,128)(2,1)}, u32[]{:S(2)}, u32[]{:S(2)}) collective-permute-start(bf16[448,2048]{1,0:T(8,128)(2,1)} %pad_maximum_fusion.1), channel_id=1, source_target_pairs={{0,1},{1,0},{2,3},{3,2},{4,5},{5,4},{6,7},{7,6},{8,9},{9,8},{10,11... | collective-permute-start | bytes 5505032 | tf_op jit(solution)/shard_map/ppermute | solution.py:48
  404.4 22.3 %collective-permute-start.21 = (bf16[224,2048]{1,0:T(8,128)(2,1)S(1)}, bf16[224,2048]{1,0:T(8,128)(2,1)S(1)}, u32[]{:S(2)}, u32[]{:S(2)}) collective-permute-start(bf16[224,2048]{1,0:T(8,128)(2,1)S(1)} %slice.646), channel_id=1, source_target_pairs={{0,2},{1,3},{2,0},{3,1},{4,6},{5,7},{6,4},{7,5},{8,10},{9,11},{10,... | collective-permute-start | bytes 2752520 | tf_op jit(solution)/shard_map/ppermute | solution.py:48
  436.7 32.3 %collective-permute-start.22 = (bf16[448,2048]{1,0:T(8,128)(2,1)}, bf16[448,2048]{1,0:T(8,128)(2,1)}, u32[]{:S(2)}, u32[]{:S(2)}) collective-permute-start(bf16[448,2048]{1,0:T(8,128)(2,1)} %slice.403), channel_id=1, source_target_pairs={{0,1},{1,0},{2,3},{3,2},{4,5},{5,4},{6,7},{7,6},{8,9},{9,8},{10,11... | collective-permute-start | bytes 5505032 | tf_op jit(solution)/shard_map/ppermute | solution.py:48
  442.7 41.0 %all-to-all-start.3 = ((bf16[8,224,256]{2,1,0:T(8,128)(2,1)}), bf16[8,224,256]{2,1,0:T(8,128)(2,1)}, u32[]{:S(2)}, u32[]{:S(2)}) async-start(bf16[8,224,256]{2,1,0:T(8,128)(2,1)} %bitcast.414), calls=%async_computation.3 | async-start | bytes 1835008 | tf_op jit(solution)/shard_map/all_to_all | solution.py:788
  474.7 32.7 %collective-permute-start.23 = (bf16[224,2048]{1,0:T(8,128)(2,1)}, bf16[224,2048]{1,0:T(8,128)(2,1)}, u32[]{:S(2)}, u32[]{:S(2)}) collective-permute-start(bf16[224,2048]{1,0:T(8,128)(2,1)} %slice.645), channel_id=1, source_target_pairs={{0,2},{1,3},{2,0},{3,1},{4,6},{5,7},{6,4},{7,5},{8,10},{9,11},{10,... | collective-permute-start | bytes 2752520 | tf_op jit(solution)/shard_map/ppermute | solution.py:48
  544.1 40.9 %collective-permute-start.25 = (bf16[224,2048]{1,0:T(8,128)(2,1)}, bf16[224,2048]{1,0:T(8,128)(2,1)}, u32[]{:S(2)}, u32[]{:S(2)}) collective-permute-start(bf16[224,2048]{1,0:T(8,128)(2,1)} %get-tuple-element.156), channel_id=1, source_target_pairs={{0,2},{1,3},{8,10},{9,11},{16,18},{17,19},{24,26},{25,27}} | collective-permute-start | bytes 2752520 | tf_op jit(solution)/shard_map/ppermute | solution.py:433
  547.0 37.9 %collective-permute-start.26 = (bf16[224,2048]{1,0:T(8,128)(2,1)}, bf16[224,2048]{1,0:T(8,128)(2,1)}, u32[]{:S(2)}, u32[]{:S(2)}) collective-permute-start(bf16[224,2048]{1,0:T(8,128)(2,1)} %get-tuple-element.157), channel_id=1, source_target_pairs={{6,4},{7,5},{14,12},{15,13},{22,20},{23,21},{30,28},{31,29}} | collective-permute-start | bytes 2752520 | tf_op jit(solution)/shard_map/ppermute | solution.py:433
  609.7 24.2 %collective-permute-start.29 = (bf16[224,2048]{1,0:T(8,128)(2,1)}, bf16[224,2048]{1,0:T(8,128)(2,1)}, u32[]{:S(2)}, u32[]{:S(2)}) collective-permute-start(bf16[224,2048]{1,0:T(8,128)(2,1)} %get-tuple-element.168), channel_id=1, source_target_pairs={{0,2},{1,3},{2,4},{3,5},{8,10},{9,11},{10,12},{11,13},{16,18},{17,... | collective-permute-start | bytes 2752520 | tf_op jit(solution)/shard_map/ppermute | solution.py:433
  615.0 18.9 %collective-permute-start.30 = (bf16[224,2048]{1,0:T(8,128)(2,1)}, bf16[224,2048]{1,0:T(8,128)(2,1)}, u32[]{:S(2)}, u32[]{:S(2)}) collective-permute-start(bf16[224,2048]{1,0:T(8,128)(2,1)} %get-tuple-element.169), channel_id=1, source_target_pairs={{4,2},{5,3},{6,4},{7,5},{12,10},{13,11},{14,12},{15,13},{20,18},{2... | collective-permute-start | bytes 2752520 | tf_op jit(solution)/shard_map/ppermute | solution.py:433
  663.2 17.8 %collective-permute-start.34 = (f32[8,10752]{1,0:T(8,128)S(1)}, f32[8,10752]{1,0:T(8,128)S(1)}, u32[]{:S(2)}, u32[]{:S(2)}) collective-permute-start(f32[8,10752]{1,0:T(8,128)S(1)} %get-tuple-element.257), channel_id=1, source_target_pairs={{0,8},{8,0},{16,24},{24,16},{1,9},{9,1},{17,25},{25,17},{2,10},{10... | collective-permute-start | bytes 1032200 | tf_op jit(solution)/shard_map/ppermute | solution.py:48
  668.9 29.8 %collective-permute-start.31 = (bf16[224,2048]{1,0:T(8,128)(2,1)S(1)}, bf16[224,2048]{1,0:T(8,128)(2,1)S(1)}, u32[]{:S(2)}, u32[]{:S(2)}) collective-permute-start(bf16[224,2048]{1,0:T(8,128)(2,1)S(1)} %get-tuple-element.178), channel_id=1, source_target_pairs={{0,2},{1,3},{2,4},{3,5},{4,6},{5,7},{8,10},{9,11},{10,12},{11,13},... | collective-permute-start | bytes 2752520 | tf_op jit(solution)/shard_map/ppermute | solution.py:433
  679.7 23.2 %collective-permute-start.32 = (bf16[224,2048]{1,0:T(8,128)(2,1)S(1)}, bf16[224,2048]{1,0:T(8,128)(2,1)S(1)}, u32[]{:S(2)}, u32[]{:S(2)}) collective-permute-start(bf16[224,2048]{1,0:T(8,128)(2,1)S(1)} %get-tuple-element.179), channel_id=1, source_target_pairs={{2,0},{3,1},{4,2},{5,3},{6,4},{7,5},{10,8},{11,9},{12,10},{13,11},... | collective-permute-start | bytes 2752520 | tf_op jit(solution)/shard_map/ppermute | solution.py:433
  (146 other events, 1312.6 us)
Sparse Core Ops, SparseCore 0:
  11.4 98.3 all-gather.2
  152.0 95.7 all-gather.4

commit v2 on v1

--- a/solution.py
+++ b/solution.py
@@ -19,6 +19,7 @@
 column_eps = 1e-06
 rope_base = 10000.0
 far_negative = -1e30
+log2_e = 1.4426950408889634
 adapter_scale = ALPHA / ADAPTER_RANK
 bf16 = jnp.bfloat16
 f32 = jnp.float32
@@ -174,7 +175,7 @@
     pre, cosine, sine, begin, q_out, k_out, v_out, att_out, mixed_t, lse_out, v_t
 ):
     count = pre.shape[0]
-    scale = HDIM**-0.5
+    scale = HDIM**-0.5 * log2_e
     for i in range(count // TILE):
         at = pl.ds(i * TILE, TILE)
         cos, sin = cosine[at, :], sine[at, :]
@@ -199,8 +200,8 @@
                 allowed = allowed & (place <= mine)
             s = jnp.where(allowed, s, far_negative)
             high = jnp.maximum(top, jnp.max(s, axis=0, keepdims=True))
-            keep = jnp.exp(top - high)
-            p = jnp.where(allowed, jnp.exp(s - high), 0.0)
+            keep = jnp.exp2(top - high)
+            p = jnp.exp2(s - high)
             total = total * keep + jnp.sum(p, axis=0, keepdims=True)
             mixed = mixed * keep + dot(v_t[:, keys], p.astype(bf16))
             return high, total, mixed
@@ -217,7 +218,7 @@
         mixed = mixed / total
         mixed_t[:, rows] = mixed
         att_out[rows, :] = mixed.T.astype(bf16)
-        lse_out[0, :, rows] = top + jnp.log(total)
+        lse_out[0, :, rows] = top + jnp.log2(total)
 
 
 def backward_kernel(
@@ -242,13 +243,13 @@
         dq_t = jnp.zeros((HDIM, TILE), f32)
         for j in range(i + 1):
             keys = pl.ds(j * TILE, TILE)
-            s = dot(k_ref[keys, :], q, NT) * scale
+            s = dot(k_ref[keys, :], q, NT) * (scale * log2_e)
             place = j * TILE + lax.broadcasted_iota(jnp.int32, (TILE, TILE), 0)
             allowed = place >= start
             if j == i:
                 mine = i * TILE + lax.broadcasted_iota(jnp.int32, (TILE, TILE), 1)
                 allowed = allowed & (place <= mine)
-            p = jnp.where(allowed, jnp.exp(s - high), 0.0)
+            p = jnp.where(allowed, jnp.exp2(s - high), 0.0)
             dp = dot(v_ref[keys, :], d_mixed, NT)
             ds = (p * (dp - delta)).astype(bf16)
             dv[keys, :] += dot(p.astype(bf16), d_mixed)
@@ -367,7 +368,7 @@
 def feed_forward(gu, down, h, d, mates):
     rows, width = h.shape
     hidden = down.shape[0] // mates
-    unit = hidden // max(1, hidden // 176)
+    unit = hidden // max(1, hidden // 352)
     steps = hidden // unit
     flat = lambda k, j: (k * steps + j, 0)
     deep = lambda k, j: (k, 0, j, 0)
@@ -391,7 +392,7 @@
             jax.ShapeDtypeStruct((mates, 2, hidden, rows), bf16),
             jax.ShapeDtypeStruct((mates, 2, hidden, 1), f32),
         ],
-        compiler_params=pltpu.CompilerParams(vmem_limit_bytes=48 * 2**20),
+        compiler_params=pltpu.CompilerParams(vmem_limit_bytes=58 * 2**20),
         cost_estimate=pl.CostEstimate(
             flops=6 * mates * hidden * rows * width,
             bytes_accessed=6 * mates * hidden * width + 4 * rows * width,
@@ -402,6 +403,101 @@
     return acts, g.reshape(2 * mates * hidden, rows), gm
 
 
+def back_kernel(
+    core, g_ref, h_ref, w_ref, spread, s_ref, over_n, sums, m_ref, xa_ref, aw_ref,
+    own_out, other_out, ga_out, gb_out, gg_out, gm_out,
+):
+    step = pl.program_id(0)
+    length = own_out.shape[1]
+    g = g_ref[...]
+    h = h_ref[...]
+    s = s_ref[...]
+    dh = dot(g, w_ref[...], NT)
+    low = dh.astype(bf16)
+
+    @pl.when(core[0] == 0)
+    def _():
+        own_out[0] = low[:length]
+        other_out[0] = low[length:]
+
+    @pl.when(core[0] != 0)
+    def _():
+        own_out[0] = low[length:]
+        other_out[0] = low[:length]
+
+    p = dot((spread[...] * s).astype(bf16), g, NT).astype(bf16)
+    ga = dot(p, h)
+    gb = dot(xa_ref[...], g)
+    gg = jnp.sum(dh * h.astype(f32), axis=0, keepdims=True)
+
+    @pl.when(step == 0)
+    def _():
+        gm = sums[0:1, :] / m_ref[...]
+        gm_out[...] = gm
+        tilt = (spread[...] * (gm * over_n[...])).astype(bf16)
+        ga_out[...] = ga - dot(tilt, w_ref[...], NT)
+        gb_out[...] = gb * s - aw_ref[...] * (gm * over_n[...])
+        gg_out[...] = gg
+
+    @pl.when(step > 0)
+    def _():
+        ga_out[...] += ga
+        gb_out[...] += gb * s
+        gg_out[...] += gg
+
+
+def back_qkv(g, h, w, spread, m, n, sums, xa, aw):
+    chips = lax.axis_size("blk") // 2
+    core = (lax.axis_index("blk") % 2).astype(jnp.int32).reshape(1)
+    count, cols = g.shape
+    width = h.shape[1]
+    pair = count // chips
+    wide = spread.shape[0]
+    rows = lambda i, core: (i, 0)
+    whole = lambda i, core: (0, 0)
+    deep = lambda i, core: (i, 0, 0)
+    return pl.pallas_call(
+        back_kernel,
+        grid_spec=pltpu.PrefetchScalarGridSpec(
+            num_scalar_prefetch=1,
+            grid=(chips,),
+            in_specs=[
+                pl.BlockSpec((pair, cols), rows),
+                pl.BlockSpec((pair, width), rows),
+                pl.BlockSpec((width, cols), whole),
+                pl.BlockSpec((wide, cols), whole),
+                pl.BlockSpec((1, cols), whole),
+                pl.BlockSpec((1, cols), whole),
+                pl.BlockSpec((8, cols), whole),
+                pl.BlockSpec((1, cols), whole),
+                pl.BlockSpec((None, wide, pair), deep),
+                pl.BlockSpec((wide, cols), whole),
+            ],
+            out_specs=[
+                pl.BlockSpec((1, pair // 2, width), deep),
+                pl.BlockSpec((1, pair // 2, width), deep),
+                pl.BlockSpec((wide, width), whole),
+                pl.BlockSpec((wide, cols), whole),
+                pl.BlockSpec((1, width), whole),
+                pl.BlockSpec((1, cols), whole),
+            ],
+        ),
+        out_shape=[
+            jax.ShapeDtypeStruct((chips, pair // 2, width), bf16),
+            jax.ShapeDtypeStruct((chips, pair // 2, width), bf16),
+            jax.ShapeDtypeStruct((wide, width), f32),
+            jax.ShapeDtypeStruct((wide, cols), f32),
+            jax.ShapeDtypeStruct((1, width), f32),
+            jax.ShapeDtypeStruct((1, cols), f32),
+        ],
+        compiler_params=pltpu.CompilerParams(vmem_limit_bytes=56 * 2**20),
+        cost_estimate=pl.CostEstimate(
+            flops=3 * count * cols * width, bytes_accessed=8 * count * width, transcendentals=0
+        ),
+        name="back_qkv",
+    )(core, g, h, w, spread, m / n, 1.0 / n, sums, m, xa, aw)
+
+
 def normalize(values, gain):
     inverse = lax.rsqrt(jnp.mean(values * values, axis=-1, keepdims=True) + norm_eps)
     return (values * inverse * gain, inverse)
@@ -431,14 +527,6 @@
 def step_chips(array, first, last, by):
     pairs = [(2 * i + c, 2 * (i + by) + c) for i in range(first, last + 1) for c in range(2)]
     return lax.ppermute(array, "blk", pairs)
-
-
-def core_scatter(parts):
-    chips = lax.axis_size("blk") // 2
-    core = lax.axis_index("blk") % 2
-    parts = parts.reshape(chips, 2, parts.shape[0] // (2 * chips), parts.shape[1])
-    take = lambda c: lax.dynamic_index_in_dim(parts, c, 1, keepdims=False)
-    return (take(core).astype(f32) + swap(take(1 - core), "blk", 1).astype(f32)).astype(bf16)
 
 
 def chips_step(total, t, state):
@@ -475,12 +563,20 @@
     return one, two
 
 
+def dp_last(state):
+    bits = [1 << i for i in range(lax.axis_size("dp").bit_length() - 1)]
+    one, two = state
+    return jnp.concatenate(
+        [one, swap(one, "dp", bits[-1]), two, swap(two, "dp", bits[0])], axis=0
+    )
+
+
 def dp_places():
     groups = lax.axis_size("dp")
     bits = groups.bit_length() - 1
     who = jnp.arange(groups, dtype=jnp.int32) ^ lax.axis_index("dp")
     turned = sum(((who >> i) & 1) << (bits - 1 - i) for i in range(bits))
-    return jnp.stack([who, turned]).astype(jnp.int32)
+    return jnp.stack([who, turned + groups]).astype(jnp.int32)
 
 
 def lay_kernel(places, one, two, into, out):
@@ -490,8 +586,7 @@
 
 
 def dp_lay(state, into, at):
-    one, two = state
-    groups, half, width = one.shape
+    groups, half, width = state.shape[0] // 2, state.shape[1], state.shape[2]
     shape = into.shape
     if isinstance(at, tuple):
         split = into.reshape(shape[0], shape[1], groups, 2, half, width)
@@ -518,7 +613,7 @@
         out_shape=jax.ShapeDtypeStruct(split.shape, into.dtype),
         input_output_aliases={3: 0},
         name="lay",
-    )(jnp.concatenate([dp_places(), second]), one, two, split)
+    )(jnp.concatenate([dp_places(), second]), state, state, split)
     return out.reshape(shape)
 
 
@@ -541,30 +636,19 @@
     return buffer
 
 
-def sum_all(tables, vectors, between):
+def packed_up(tables, vectors):
     devices = lax.axis_size("dp") * lax.axis_size("blk")
-    flat = jnp.concatenate(vectors)
-    extra = -flat.shape[0] % 1024
-    flat = jnp.pad(flat, (0, extra)).reshape(8, -1)
-    joined = jnp.concatenate(
-        [t[i * 8 : (i + 1) * 8] for t in tables for i in range(2)] + [flat], axis=1
-    )
-    width = joined.shape[1]
-    joined = jnp.pad(joined, ((0, 0), (0, -width % (128 * devices))))
-    joined = total_sum(joined, between)
+    joined = jnp.concatenate([*tables, *[v.reshape(16, -1) for v in vectors]], axis=1)
+    return jnp.pad(joined, ((0, 0), (0, -joined.shape[1] % (128 * devices))))
+
+
+def unpacked(joined, tables, vectors):
     out, at = [], 0
-    for t in tables:
-        size = t.shape[1]
-        out.append(
-            jnp.concatenate([joined[:, at : at + size], joined[:, at + size : at + 2 * size]], axis=0)
-        )
-        at += 2 * size
-    flat = joined[:, at:width].reshape(-1)
-    vecs, at = [], 0
-    for v in vectors:
-        vecs.append(flat[at : at + v.shape[0]])
-        at += v.shape[0]
-    return out, vecs
+    for t in (*tables, *vectors):
+        size = t.size // 16
+        out.append(joined[:, at : at + size].reshape(t.shape))
+        at += size
+    return out[: len(tables)], out[len(tables) :]
 
 
 def per_device(
@@ -707,23 +791,20 @@
     gate_parts = [swap(gate_part, "blk", QUAD * k) for k in range(1, mates)]
     h_all, d_final_low, mine, rows_down = after((h_all, d_final_low, mine, rows_down), cosine)
 
-    mine = dp_steps(mine, 1, None)
-    d_final_pair = jnp.concatenate([d_final_low, swap(d_final_low, "blk", 2)], axis=0)
+    mine = dp_last(dp_steps(mine, 1, -1))
     down_rows = lax.all_gather(rows_down, "dp", axis=0, tiled=True)
     triple = dot(h_all, w_qkv)
     q, k, v, attended_heads, mixed_t, lse = attention_forward(triple, cosine, sine, begin)
 
 
-    attended_heads = after(attended_heads, mine, gate_parts, d_final_pair)
-    one, two, d_final_pair, gate_parts = after(
-        (*mine, d_final_pair, gate_parts), attended_heads
-    )
-    over = swap(one, "blk", 1), swap(two, "blk", 1)
+    attended_heads = after(attended_heads, mine, gate_parts)
+    mine, d_final_low, gate_parts = after((mine, d_final_low, gate_parts), attended_heads)
+    over = swap(mine, "blk", 1)
     up_part = after(gu_part[1], attended_heads)
     up_parts = [swap(up_part, "blk", QUAD * k) for k in range(1, mates)]
-    gate_states = [dp_steps(dp_start(g)) for g in gate_parts]
+    gate_states = [dp_steps(dp_start(g), 0, 1) for g in gate_parts]
     out_full = blank((groups, 2, MODEL_WIDTH // (2 * groups), MODEL_WIDTH), bf16)
-    out_full = dp_lay((one, two), out_full, core)
+    out_full = dp_lay(mine, out_full, core)
     out_full = dp_lay(over, out_full, 1 - core).reshape(MODEL_WIDTH, MODEL_WIDTH)
     attended = lax.all_to_all(
         attended_heads.reshape(members, length, wide), "blk", 0, 0, tiled=True
@@ -731,9 +812,15 @@
     a_low = flip(query_key_value_downmap).astype(bf16).reshape(3 * rank, MODEL_WIDTH)
     h_all_late = after(h_all, attended_heads)
     xa_qkv = dot(a_low, h_all_late, NT).astype(bf16)
+    chips = members // 2
+    xa_qkv = jnp.transpose(xa_qkv.reshape(3 * rank, chips, 2 * length), (1, 0, 2))
     aw_qkv = dot(a_low, w_qkv)
+    row = lax.broadcasted_iota(jnp.int32, (3 * rank, 3 * wide), 0) // rank
+    column = (lax.broadcasted_iota(jnp.int32, (3 * rank, 3 * wide), 1) // HDIM) % 3
+    own_block = row == column
+    spread_qkv = jnp.where(own_block, jnp.tile(by_head(b_qkv), (3, 1)), 0.0)
     attended = after(
-        attended, xa_qkv, aw_qkv, out_full, gate_states, up_parts, down_rows
+        attended, xa_qkv, aw_qkv, spread_qkv, out_full, gate_states, up_parts
     )
 
     attended = jnp.transpose(attended, (1, 0, 2)).reshape(length, MODEL_WIDTH)
@@ -743,14 +830,15 @@
     residual = x_full + y_out
     normed_two, inverse_two = normalize(residual, feedforward_norm_gain)
     h_two = normed_two.astype(bf16)
-    up_parts = after(up_parts, attended)
+    up_parts, d_final_low, gate_states = after((up_parts, d_final_low, gate_states), attended)
+    gate_states = [dp_last(dp_steps(state, 1, -1)) for state in gate_states]
+    d_final_pair = jnp.concatenate([d_final_low, swap(d_final_low, "blk", 2)], axis=0)
     up_states = [dp_steps(dp_start(g), 0, 1) for g in up_parts]
-    h_two = after(h_two, up_states)
+    h_two = after(h_two, up_states, d_final_pair)
 
     attended_late = after(attended, h_two)
     xa_out = dot(a_out_low, attended_late, NT).astype(bf16)
-    gate_states = after(gate_states, h_two)
-    up_states = [dp_steps(after(state, h_two), 1, None) for state in up_states]
+    up_states = [dp_last(dp_steps(after(state, h_two), 1, -1)) for state in up_states]
     d_final_pair = after(d_final_pair, h_two)
     d_final_all = jnp.concatenate([d_final_pair, swap(d_final_pair, "blk", 1)], axis=0)
     for k_ in range(1, mates):
@@ -807,104 +895,95 @@
     spread = jnp.where(own_gu, jnp.tile(b_gu, (2, 1)), 0.0)
     p_gu = dot((spread * s_gu).astype(bf16), g_late).astype(bf16)
     tilt = (spread * (gm_gu / n_gu_all)).astype(bf16)
-    ga_gu = adapter_scale * (dot(p_gu, h_two_late) - dot(tilt, gu_late))
     gb_gu = adapter_scale * (dot(xa_gu, g_late, NT) * s_gu - aw_gu * (gm_gu / n_gu_all))
     gb_gu = jnp.sum(jnp.where(own_gu, gb_gu, 0.0).reshape(2, rank, -1), axis=0)
-    d_heads = after(d_heads, ga_gu, gb_gu)
+    d_heads = after(d_heads, p_gu, tilt, gb_gu)
 
     g_three, gm_heads = attention_backward(
         q, k, v, triple, cosine, sine, begin, d_heads, mixed_t, lse
     )
-    g_three = after(g_three, y_down)
-    dh_parts = dot(g_three, w_qkv, NT).astype(bf16)
-    total = core_scatter(dh_parts)
-    acts_late, d_final_late, y_down, dh_late, unit_two, g_out, out_late = after(
-        (acts, d_final_all, y_down, dh_two, residual * inverse_two, g_out, out_full), total
+    gm_down = jnp.sum(d_final_low.astype(f32) * y_down, axis=0) / down_column_norm
+    g_three = after(g_three, gm_down)
+    own_rows, other_rows, grad_a, grad_b, grad_g_attn, gm = back_qkv(
+        g_three, h_all, w_qkv, spread_qkv, m_qkv, n_qkv, gm_heads, xa_qkv, aw_qkv
+    )
+    gm_quad = gm_down + swap(gm_down, "blk", 1)
+    total = (own_rows.astype(f32) + swap(other_rows, "blk", 1).astype(f32)).astype(bf16)
+    total, gm_quad = after((total, gm_quad))
+    state = chips_step(total, 1, None)
+    gm_quad = gm_quad + swap(gm_quad, "blk", 2)
+    acts_late, d_final_late, dh_late, unit_two, g_out, out_late = after(
+        (acts, d_final_all, dh_two, residual * inverse_two, g_out, out_full), gm_quad
     )
     grad_g_ffn = jnp.sum(dh_late * unit_two, axis=0)
-    gm_down = jnp.sum(d_final_low.astype(f32) * y_down, axis=0) / down_column_norm
-    gm_quad = gm_down + swap(gm_down, "blk", 1)
-    gm_quad = gm_quad + swap(gm_quad, "blk", 2)
-    s_down = down_column_norm / norms_down
-    p_down = dot((down_adapter_upmap * s_down).astype(bf16), d_final_late, NT).astype(bf16)
-    tilt_down = (down_adapter_upmap * (gm_quad / norms_down)).astype(bf16)
-    ga_down = adapter_scale * (dot(p_down, acts_late, NT) - dot(tilt_down, down_rows, NT))
-    gb_down = adapter_scale * (
-        dot(xa_down, d_final_late) * s_down - aw_down * (gm_quad / norms_down)
-    )
     gm_out = jnp.sum(g_out.astype(f32) * y_out, axis=0) / output_column_norm
     s_out = output_column_norm / norms_out
     p_out = dot((output_adapter_upmap * s_out).astype(bf16), g_out, NT).astype(bf16)
     tilt_out = (output_adapter_upmap * (gm_out / norms_out)).astype(bf16)
     ga_out = adapter_scale * (dot(p_out, attended) - dot(tilt_out, out_late, NT))
     gb_out = adapter_scale * (dot(xa_out, g_out) * s_out - aw_out * (gm_out / norms_out))
-
-    state = chips_step(total, 1, None)
-    state = after(state, ga_down, gb_down, ga_out, gb_out, grad_g_ffn)
-    g_three, gm_heads, h_all_late = after((g_three, gm_heads, h_all), state)
-    chips = members // 2
-
-    gm = gm_heads[0:1] / m_qkv
-    s_qkv = m_qkv / n_qkv
-    row = lax.broadcasted_iota(jnp.int32, (3 * rank, 3 * wide), 0) // rank
-    column = (lax.broadcasted_iota(jnp.int32, (3 * rank, 3 * wide), 1) // HDIM) % 3
-    own_block = row == column
-    spread = jnp.where(own_block, jnp.tile(by_head(b_qkv), (3, 1)), 0.0)
-    p = dot((spread * s_qkv).astype(bf16), g_three, NT).astype(bf16)
-    tilt = (spread * (gm / n_qkv)).astype(bf16)
-    grad_a = adapter_scale * (dot(p, h_all_late) - dot(tilt, w_qkv, NT))
-    grad_b = adapter_scale * (dot(xa_qkv, g_three) * s_qkv - aw_qkv * (gm / n_qkv))
+    s_down = down_column_norm / norms_down
+    p_down = dot((down_adapter_upmap * s_down).astype(bf16), d_final_late, NT).astype(bf16)
+    state = after(state, ga_out, gb_out, grad_g_ffn, p_down, gm_quad)
+
+    gm_quad, p_down, p_gu, tilt = after((gm_quad, p_down, p_gu, tilt), state)
+    ga_gu = adapter_scale * (dot(p_gu, h_two_late) - dot(tilt, gu_late))
+    tilt_down = (down_adapter_upmap * (gm_quad / norms_down)).astype(bf16)
+    ga_down = adapter_scale * (dot(p_down, acts_late, NT) - dot(tilt_down, down_rows, NT))
+    gb_down = adapter_scale * (
+        dot(xa_down, d_final_late) * s_down - aw_down * (gm_quad / norms_down)
+    )
+    room = -hidden % 128
+    place = jnp.stack(order)[:, None] == jnp.arange(members)[None, :]
+
+    def spread_shards(array):
+        array = jnp.pad(array, [(0, 0)] * (array.ndim - 1) + [(0, room)])
+        return sum(
+            jnp.where(place[k_][:, None], array[..., k_, None, :], 0.0) for k_ in range(mates)
+        )
+
+    gb_both = jnp.swapaxes(gb_gu.reshape(rank, mates, 2, hidden), 1, 2)
+    tall = jnp.stack([gb_both[:, 0], gb_both[:, 1], ga_down.reshape(rank, mates, hidden)])
+    tall = spread_shards(tall).reshape(3, rank, -1)
+    thin = spread_shards(jnp.swapaxes(gm_gu.reshape(mates, 2, hidden), 0, 1)).reshape(2, -1)
     grad_b = jnp.sum(jnp.where(own_block, grad_b, 0.0).reshape(3, rank, 3 * wide), axis=0)
-    grad_b = by_three(grad_b)
-    grad_m = by_three(gm)[:, 0]
-    grad_g_attn = (
-        jnp.sum(dh_parts.astype(f32) * h_all_late.astype(f32), axis=0) / attention_norm_gain
-    )
-
-
+    mine_only = jnp.arange(members)[:, None] == me
+    b_all = jnp.where(mine_only, by_three(adapter_scale * grad_b)[:, :, None, :], 0.0)
+    b_all = b_all.reshape(3, rank, MODEL_WIDTH)
+    m_all = jnp.where(mine_only, by_three(gm)[:, 0][:, None, :], 0.0).reshape(3, MODEL_WIDTH)
+    grad_g_attn = grad_g_attn[0] / attention_norm_gain
+    grad_a = adapter_scale * grad_a
+    tables = (
+        [grad_a[i * rank : (i + 1) * rank] for i in range(3)]
+        + [b_all[i] for i in range(3)]
+        + [ga_out, gb_out, ga_gu[:rank], ga_gu[rank:], gb_down]
+        + [tall[0], tall[1], tall[2]]
+    )
+    vectors = [grad_g_attn, grad_g_ffn, gm_out, gm_down, m_all[0], m_all[1], m_all[2]]
+    vectors += [thin[0], thin[1]]
+    packed = packed_up(tables, vectors)
     for t in range(2, chips - 1):
         state = chips_step(total, t, state)
-        state = after(state, grad_a, grad_b, grad_g_attn)
-    grad_a, grad_b, grad_m, ga_gu, gb_gu = after((grad_a, grad_b, grad_m, ga_gu, gb_gu), state)
+        state = after(state, packed)
+    packed = after(packed, state)
     ends = {}
 
     def between(buffer, stage):
-        if stage == 1:
+        if stage == 2:
             ends[0] = after(chips_step(total, chips - 1, state), buffer)
             buffer = after(buffer, ends[0])
         return buffer
 
-    def placed(array, total, k_, i):
-        part = array[..., (2 * k_ + i) * hidden : (2 * k_ + i + 1) * hidden]
-        return lax.dynamic_update_slice_in_dim(total, part, order[k_] * hidden, array.ndim - 1)
-
-    units = members * hidden
-    all_b, all_m = [], []
-    for i in range(2):
-        tall, thin = jnp.zeros((rank, units), f32), jnp.zeros((units,), f32)
-        for k_ in range(mates):
-            tall, thin = placed(gb_gu, tall, k_, i), placed(gm_gu, thin, k_, i)
-        all_b.append(tall)
-        all_m.append(thin)
-    all_a = jnp.zeros((rank, units), f32)
-    for k_ in range(mates):
-        all_a = lax.dynamic_update_slice_in_dim(
-            all_a, ga_down[:, k_ * hidden : (k_ + 1) * hidden], order[k_] * hidden, 1
-        )
-    empty = jnp.zeros((rank, MODEL_WIDTH), f32)
-    tables, vectors = sum_all(
-        [grad_a[i * rank : (i + 1) * rank] for i in range(3)]
-        + [lax.dynamic_update_slice_in_dim(empty, grad_b[i], me * wide, 1) for i in range(3)]
-        + [ga_out, gb_out, ga_gu[:rank], ga_gu[rank:], gb_down]
-        + [*all_b, all_a],
-        [grad_g_attn, grad_g_ffn, gm_out, gm_down]
-        + [lax.dynamic_update_slice_in_dim(empty[0], grad_m[i], me * wide, 0) for i in range(3)]
-        + all_m,
-        between,
-    )
-    d_norm_one = normalize_back(x_full, inverse_one, attention_norm_gain, chips_end(total, ends[0]))
+    tables, vectors = unpacked(total_sum(packed, between), tables, vectors)
+    d_norm_one = normalize_back(
+        x_full, inverse_one, attention_norm_gain, chips_end(total, ends[0])
+    )
     grad_input = d_residual + d_norm_one
-    a_out, b_out, a_gate, a_up, b_down, b_gate, b_up, a_down = tables[6:]
+    dense = lambda array: array.reshape(-1, members, hidden + room)[:, :, :hidden].reshape(
+        array.shape[:-1] + (members * hidden,)
+    )
+    a_out, b_out, a_gate, a_up, b_down = tables[6:11]
+    b_gate, b_up, a_down = [dense(t) for t in tables[11:]]
     return (
         result,
         grad_input,
@@ -918,7 +997,7 @@
         vectors[2],
         flip(jnp.stack([a_gate, a_up])),
         jnp.stack([b_gate, b_up]),
-        jnp.stack(vectors[7:]),
+        jnp.stack([dense(v) for v in vectors[7:]]),
         flip(a_down),
         b_down,
         vectors[3],

time: 776 us -> 681 us (0.88)
  local copies, waits for them, and re-layouts: 118 us -> 88.2 us
  other arithmetic: 113 us -> 85.7 us
  matrix products: 121 us -> 95.2 us
  waiting for transfers between devices: 194 us -> 170 us
  Pallas kernels: 119 us -> 130 us
    dot_general x22 -> x21, matrix products: 121 us -> 95.2 us  [dot(): return lax.dot_general(a, b, dims, preferred_element_type=f32)]
    pallas_call x0 -> x1, Pallas kernels: none -> 19.4 us  [back_qkv(): pl.pallas_call(back_kernel, grid_spec=pltpu.PrefetchScalarGridSpec(num_sc...]
    ppermute x6, waiting for transfers between devices: 28 us -> 10.9 us  [step_chips(): return lax.ppermute(array, 'blk', pairs)]
    ppermute x41 -> x40, waiting for transfers between devices: 114 us -> 104 us  [swap(): lax.ppermute(array, axis, [(i, i ^ bit) for i in range(lax.axis_size(axis...]
    dynamic_update_slice x15 -> x0, local copies, waits for them, and re-layouts: 9.82 us -> none  [the longest x7 4.04 us: placed(): lax.dynamic_update_slice_in_dim(total, part, order[k_] * hidden, array.nd...]
    pallas_call x1, Pallas kernels: 35 us -> 26.7 us  [feed_forward(): pl.pallas_call(feed_kernel, grid=(mates, steps), in_specs=[pl.BlockSpec((...]
    reduce_sum x1 -> x0, other arithmetic: 8.18 us -> none  [per_device(): jnp.sum(dh_parts.astype(f32) * h_all_late.astype(f32), axis=0)]
    unnamed x296 -> x277, local copies, waits for them, and re-layouts: 40.9 us -> 35.9 us
  transfers between devices with their start and end apart: 53 -> 52, of which waited for: 26 -> 18; matrix products, arithmetic and copies ran while one was open for 26% -> 28% of each run, Pallas kernels for 11% -> 15%
where the time goes in v2:
time: 681 us; the launch traced here: 671 us
  waiting for transfers between devices  170 us (25%)
  Pallas kernels  130 us (19%)
  matrix products  95.2 us (14%)
  local copies, waits for them, and re-layouts  88.2 us (13%)
  other arithmetic  85.7 us (13%)
  starting transfers between devices  85 us (12%)
  between operations  16.8 us (2%)
    ppermute x40, waiting for transfers between devices, swap(): lax.ppermute(array, axis, [(i, i ^ bit) for i in range(lax.axis_size(axis...  104 us
    dot_general x21, matrix products, dot(): return lax.dot_general(a, b, dims, preferred_element_type=f32)  95.2 us
    all_to_all x2, waiting for transfers between devices, spread_rows(): got = lax.all_to_all(chunks, 'blk', 0, 0, tiled=True)  54.2 us
    ppermute x40, starting transfers between devices, swap(): lax.ppermute(array, axis, [(i, i ^ bit) for i in range(lax.axis_size(axis...  40.8 us
    unnamed x277, local copies, waits for them, and re-layouts  35.9 us
    pallas_call x1, Pallas kernels, feed_forward(): pl.pallas_call(feed_kernel, grid=(mates, steps), in_specs=[pl.BlockSpec((...  26.7 us
    ppermute x6, starting transfers between devices, step_chips(): return lax.ppermute(array, 'blk', pairs)  25.1 us
    pallas_call x4, Pallas kernels, dp_lay(): pl.pallas_call(lay_kernel, grid_spec=pltpu.PrefetchScalarGridSpec(num_sca...  20.5 us
  transfers between devices with their start and end apart: 52, of which 18 were waited for; matrix products, arithmetic and copies ran while one was open for 28% of the time, Pallas kernels for 15%

profile of v2, /device:TPU:0, one launch (start us, length us, event | category | flops | bytes accessed | tf_op | source)
XLA Modules:
  0.0 670.7 jit_solution(16764772388858826574)
XLA Ops:
  18.4 7.4 %merge.5 = (bf16[5632,256]{1,0:T(8,128)(2,1)S(1)}, f32[1,256]{1,0:T(1,128)S(1)}) custom-call(bf16[1,5632,256]{2,1,0:T(8,128)(2,1)} %bitcast.453, bf16[1,96,5632]{2,1,0:T(8,128)(2,1)S(1)} %fusion.45.a_ref, bf16[1,96,256]{2,1,0:T(8,128)(2,1)S(1)} %constant_dynamic-update-slice_fusion.40.b_ref, f32[1,256]{1,0:T(1,128)S(1)} %bitcast.420), custom_call_target="tpu_custom_call" | custom-call | flops 276824064 | bytes 5767168 | tf_op jit(solution)/shard_map/merge/pallas_call | solution.py:110
  27.6 8.0 %merge.4 = (bf16[2048,768]{1,0:T(8,128)(2,1)S(1)}, f32[1,768]{1,0:T(1,128)S(1)}) custom-call(bf16[3,2048,256]{2,1,0:T(8,128)(2,1)} %w_ref.1, bf16[3,96,2048]{2,1,0:T(8,128)(2,1)S(1)} %fusion.43.a_ref, bf16[3,96,256]{2,1,0:T(8,128)(2,1)S(1)} %constant_dynamic-update-slice_fusion.29.b_ref, f32[1,768]{1,0:T(1,128)S(1)} %reshape.496.m_ref), custom_call_target="tpu_custom_call" | custom-call | flops 301989888 | bytes 6291456 | tf_op jit(solution)/shard_map/merge/pallas_call | solution.py:110
  38.8 7.4 %merge_rows.1 = (bf16[2,2,704,2048]{3,2,1,0:T(8,128)(2,1)}, f32[2,704,1]{2,1,0:T(8,128)}) custom-call(bf16[2,704,2048]{2,1,0:T(8,128)(2,1)} %bitcast.449, bf16[2,96,2048]{2,1,0:T(8,128)(2,1)} %copy-done.62, bf16[2,96,704]{2,1,0:T(8,128)(2,1)} %copy-done.69, f32[2,704,1]{2,1,0:T(8,128)} %copy.76.m_ref), custom_call_target="tpu_custom_call" | custom-call | flops 553648128 | bytes 11534336 | tf_op jit(solution)/shard_map/merge_rows/pallas_call | solution.py:145
  51.3 6.4 all-to-all-start
  62.3 45.4 %all-to-all-done = bf16[8,256,256]{2,1,0:T(8,128)(2,1)S(1)} async-done(((bf16[8,256,256]{2,1,0:T(8,128)(2,1)}), bf16[8,256,256]{2,1,0:T(8,128)(2,1)S(1)}, u32[]{:S(2)}, u32[]{:S(2)}) %all-to-all-start) | async-done | bytes 1048608 | tf_op jit(solution)/shard_map/all_to_all | solution.py:744
  128.4 7.8 %collective-permute-done = bf16[1,128,2048]{2,1,0:T(8,128)(2,1)} collective-permute-done((bf16[1,128,2048]{2,1,0:T(8,128)(2,1)}, bf16[1,128,2048]{2,1,0:T(8,128)(2,1)}, u32[]{:S(2)}, u32[]{:S(2)}) %collective-permute-start) | collective-permute-done | bytes 524320 | tf_op jit(solution)/shard_map/ppermute | solution.py:49
  139.6 8.9 %all-to-all-done.1 = bf16[8,368,256]{2,1,0:T(8,128)(2,1)} async-done(((bf16[8,368,256]{2,1,0:T(8,128)(2,1)}), bf16[8,368,256]{2,1,0:T(8,128)(2,1)}, u32[]{:S(2)}, u32[]{:S(2)}) %all-to-all-start.1) | async-done | bytes 1507360 | tf_op jit(solution)/shard_map/all_to_all | solution.py:744
  154.3 10.5 %fusion.112.pre = f32[1792,768]{1,0:T(8,128)} fusion(bf16[1792,2048]{1,0:T(8,128)(2,1)} %all-gather.3.cloned.1.call-done.h_ref, bf16[2048,768]{1,0:T(8,128)(2,1)} %copy-done.2), kind=kOutput, calls=%fused_computation.424 | convolution fusion | flops 5637144576 | bytes 15990784 | tf_op jit(solution)/shard_map/dot_general | solution.py:32
  164.9 20.3 %attend.1 = (bf16[1792,256]{1,0:T(8,128)(2,1)S(1)}, bf16[1792,256]{1,0:T(8,128)(2,1)S(1)}, bf16[1792,256]{1,0:T(8,128)(2,1)S(1)}, bf16[1792,256]{1,0:T(8,128)(2,...) custom-call(f32[1792,768]{1,0:T(8,128)} %fusion.112.pre, f32[1792,128]{1,0:T(8,128)S(1)} %pad_maximum_fusion.8.cosine, ...), custom_call_target="tpu_custom_call" | custom-call | flops 1644167168 | bytes 13762560 | tf_op jit(solution)/shard_map/attend/pallas_call | solution.py:282
  206.1 6.3 fusion.7
  213.3 5.4 lay.4.into
  222.8 5.4 lay.5
  228.2 24.6 %collective-permute-done.8 = bf16[176,2048]{1,0:T(8,128)(2,1)} collective-permute-done((bf16[176,2048]{1,0:T(8,128)(2,1)}, bf16[176,2048]{1,0:T(8,128)(2,1)}, u32[]{:S(2)}, u32[]{:S(2)}) %collective-permute-start.8) | collective-permute-done | bytes 720928 | tf_op jit(solution)/shard_map/ppermute | solution.py:49
  257.7 5.6 fusion.29
  266.7 8.4 %collective-permute-done.10 = bf16[1,88,2048]{2,1,0:T(8,128)(2,1)S(1)} collective-permute-done((bf16[1,88,2048]{2,1,0:T(8,128)(2,1)S(1)}, bf16[1,88,2048]{2,1,0:T(8,128)(2,1)S(1)}, u32[]{:S(2)}, u32[]{:S(2)}) %collective-permute-start.10) | collective-permute-done | bytes 360480 | tf_op jit(solution)/shard_map/ppermute | solution.py:49
  284.6 16.1 %collective-permute-done.16 = bf16[224,2048]{1,0:T(8,128)(2,1)S(1)} collective-permute-done((bf16[224,2048]{1,0:T(8,128)(2,1)S(1)}, bf16[224,2048]{1,0:T(8,128)(2,1)S(1)}, u32[]{:S(2)}, u32[]{:S(2)}) %collective-permute-start.16) | collective-permute-done | bytes 917536 | tf_op jit(solution)/shard_map/ppermute | solution.py:49
  327.7 26.7 %feed_forward.1 = (bf16[1408,896]{1,0:T(8,128)(2,1)}, bf16[2,2,704,896]{3,2,1,0:T(8,128)(2,1)}, f32[2,2,704,1]{3,2,1,0:T(8,128)}) custom-call(bf16[2,2,704,2048]{3,2,1,0:T(8,128)(2,1)} %bitcast.425, bf16[1408,2048]{1,0:T(8,128)(2,1)} %all-gather.5.cloned.1.call-done.down_ref, bf16[896,2048]{1,0:T(8,128)(2,1)} %pad_maximum_fusion.h_ref, ...), custom_call_target="tpu_custom_call" | custom-call | flops 15502147584 | bytes 24641536 | tf_op jit(solution)/shard_map/feed_forward/pallas_call | solution.py:376
  354.4 15.4 %convolution_convert_fusion = bf16[896,2048]{1,0:T(8,128)(2,1)S(1)} fusion(bf16[2816,896]{1,0:T(8,128)(2,1)} %bitcast.441, bf16[2816,2048]{1,0:T(8,128)(2,1)} %bitcast.426), kind=kOutput, calls=%fused_computation.4 | convolution fusion | flops 10336600064 | bytes 20250624 | tf_op jit(solution)/shard_map/dot_general | solution.py:32
  383.8 8.9 %convolution_convert_fusion.1 = bf16[896,2048]{1,0:T(8,128)(2,1)S(1)} fusion(bf16[1408,896]{1,0:T(8,128)(2,1)S(1)} %copy-done.38, bf16[1408,2048]{1,0:T(8,128)(2,1)} %all-gather.5.cloned.1.call-done.down_ref), kind=kOutput, calls=%fused_computation.5 | convolution fusion | flops 5169217536 | bytes 11960320 | tf_op jit(solution)/shard_map/dot_general | solution.py:32
  399.2 5.9 collective-permute-done.20
  421.9 7.0 %fusion.2 = f32[32,2816]{1,0:T(8,128)} fusion(bf16[2816,896]{1,0:T(8,128)(2,1)} %bitcast.442, bf16[896,2048]{1,0:T(8,128)(2,1)} %pad_maximum_fusion.h_ref, bf16[32,2048]{1,0:T(8,128)(2,1)S(1)} %bitcast.470, f32[32,2816]{1,0:T(8,128)S(1)} %convolution_bitcast_fusion, f32[2816]{0:T(1024)S(1)} %get-tuple-element.294, f32[2816]{0:T(1024)S(1)} %get-tuple-element.295, ...), kind=kOutput, calls=%fused_computation.9 | convolution fusion | flops 280662016 | bytes 9616416 | tf_op jit(solution)/shard_map/dot_general | solution.py:32
  448.6 17.7 %attend_back.1 = (bf16[1792,768]{1,0:T(8,128)(2,1)}, f32[8,768]{1,0:T(8,128)S(1)}) custom-call(bf16[1792,256]{1,0:T(8,128)(2,1)S(1)} %copy-done.7, bf16[1792,256]{1,0:T(8,128)(2,1)S(1)} %copy-done.9, bf16[1792,256]{1,0:T(8,128)(2,1)S(1)} %copy-done.11, f32[1792,768]{1,0:T(8,128)} %fusion.112.pre, f32[1792,128]{1,0:T(8,128)S(1)} %pad_maximum_fusion.8.cosine, ...), custom_call_target="tpu_custom_call" | custom-call | flops 4110417920 | bytes 18350080 | tf_op jit(solution)/shard_map/attend_back/pallas_call | solution.py:319
  469.3 19.4 %back_qkv.1 = (bf16[4,224,2048]{2,1,0:T(8,128)(2,1)}, bf16[4,224,2048]{2,1,0:T(8,128)(2,1)}, f32[48,2048]{1,0:T(8,128)}, f32[48,768]{1,0:T(8,128)}, f32[1,2048]{1,0:T(1,128)}, /*index=5*/f32[1,768]{1,0:T(1,128)}) custom-call(s32[1]{0:T(128)} %bitcast.130.core, bf16[1792,768]{1,0:T(8,128)(2,1)} %get-tuple-element.158.g_ref, ...), custom_call_target="tpu_custom_call" | custom-call | flops 8455716864 | bytes 29360128 | tf_op jit(solution)/shard_map/back_qkv/pallas_call | solution.py:459
  497.4 5.1 add_convert_fusion
  513.7 6.5 constant_dynamic-update-slice_fusion.69
  527.9 6.5 fusion.113
  547.6 5.3 collective-permute-start.28
  560.6 10.0 %collective-permute-done.28 = bf16[224,2048]{1,0:T(8,128)(2,1)} collective-permute-done((bf16[224,2048]{1,0:T(8,128)(2,1)S(1)}, bf16[224,2048]{1,0:T(8,128)(2,1)}, u32[]{:S(2)}, u32[]{:S(2)}) %collective-permute-start.28) | collective-permute-done | bytes 917536 | tf_op jit(solution)/shard_map/ppermute | solution.py:529
  583.9 10.3 %collective-permute-start.30 = (bf16[224,2048]{1,0:T(8,128)(2,1)}, bf16[224,2048]{1,0:T(8,128)(2,1)}, u32[]{:S(2)}, u32[]{:S(2)}) collective-permute-start(bf16[224,2048]{1,0:T(8,128)(2,1)} %get-tuple-element.190), channel_id=1, source_target_pairs={{0,2},{1,3},{2,4},{3,5},{4,6},{5,7},{8,10},{9,11},{10,12},{11,13},... | collective-permute-start | bytes 2752520 | tf_op jit(solution)/shard_map/ppermute | solution.py:529
  597.1 7.4 %collective-permute-start.36 = (f32[16,1408]{1,0:T(8,128)S(1)}, f32[16,1408]{1,0:T(8,128)S(1)}, u32[]{:S(2)}, u32[]{:S(2)}) collective-permute-start(f32[16,1408]{1,0:T(8,128)S(1)} %get-tuple-element.272), channel_id=1, source_target_pairs={{0,2},{1,3},{2,0},{3,1},{4,6},{5,7},{6,4},{7,5},{8,10},{9,11},{10,... | collective-permute-start | bytes 270344 | tf_op jit(solution)/shard_map/ppermute | solution.py:49
  606.1 16.3 %collective-permute-done.36 = f32[16,1408]{1,0:T(8,128)S(1)} collective-permute-done((f32[16,1408]{1,0:T(8,128)S(1)}, f32[16,1408]{1,0:T(8,128)S(1)}, u32[]{:S(2)}, u32[]{:S(2)}) %collective-permute-start.36) | collective-permute-done | bytes 90144 | tf_op jit(solution)/shard_map/ppermute | solution.py:49
  639.8 12.0 %collective-permute-done.42 = f32[16,5632]{1,0:T(8,128)S(1)} collective-permute-done((f32[16,5632]{1,0:T(8,128)S(1)}, f32[16,5632]{1,0:T(8,128)S(1)}, u32[]{:S(2)}, u32[]{:S(2)}) %collective-permute-start.42) | collective-permute-done | bytes 360480 | tf_op jit(solution)/shard_map/ppermute | solution.py:49
  (633 shorter events, 279.7 us)
Async XLA Ops:
  7.3 144.1 %all-gather.3.cloned.1.call-start = ((), (), s32[]{:S(2)}) async-start(), calls=%async_computation.4 | async-start | bytes 8257536 | tf_op jit(solution)/shard_map/all_gather | solution.py:703
  51.3 56.3 %all-to-all-start = ((bf16[8,256,256]{2,1,0:T(8,128)(2,1)}), bf16[8,256,256]{2,1,0:T(8,128)(2,1)S(1)}, u32[]{:S(2)}, u32[]{:S(2)}) async-start(bf16[8,256,256]{2,1,0:T(8,128)(2,1)} %bitcast.29), calls=%async_computation | async-start | bytes 2097152 | tf_op jit(solution)/shard_map/all_to_all | solution.py:744
  107.6 40.9 %all-to-all-start.1 = ((bf16[8,368,256]{2,1,0:T(8,128)(2,1)}), bf16[8,368,256]{2,1,0:T(8,128)(2,1)}, u32[]{:S(2)}, u32[]{:S(2)}) async-start(bf16[8,368,256]{2,1,0:T(8,128)(2,1)} %pad_maximum_fusion.4), calls=%async_computation.1 | async-start | bytes 3014656 | tf_op jit(solution)/shard_map/all_to_all | solution.py:744
  151.3 38.3 %collective-permute-start.4 = (bf16[176,2048]{1,0:T(8,128)(2,1)}, bf16[176,2048]{1,0:T(8,128)(2,1)}, u32[]{:S(2)}, u32[]{:S(2)}) collective-permute-start(bf16[176,2048]{1,0:T(8,128)(2,1)} %get-tuple-element.121), channel_id=1, source_target_pairs={{0,4},{1,5},{2,6},{3,7},{4,0},{5,1},{6,2},{7,3},{8,12},{9,13},{10,... | collective-permute-start | bytes 2162696 | tf_op jit(solution)/shard_map/ppermute | solution.py:49
  151.3 35.1 %collective-permute-start.2 = (bf16[2,128,2048]{2,1,0:T(8,128)(2,1)}, bf16[2,128,2048]{2,1,0:T(8,128)(2,1)S(1)}, u32[]{:S(2)}, u32[]{:S(2)}) collective-permute-start(bf16[2,128,2048]{2,1,0:T(8,128)(2,1)} %pad_maximum_fusion.6), channel_id=1, source_target_pairs={{0,16},{8,24},{16,0},{24,8},{1,17},{9,25},{17,1},{25,9},{2,18},{10... | collective-permute-start | bytes 3145736 | tf_op jit(solution)/shard_map/ppermute | solution.py:49
  152.8 35.7 %collective-permute-start.3 = (bf16[2,128,2048]{2,1,0:T(8,128)(2,1)S(1)}, bf16[2,128,2048]{2,1,0:T(8,128)(2,1)S(1)}, u32[]{:S(2)}, u32[]{:S(2)}) collective-permute-start(bf16[2,128,2048]{2,1,0:T(8,128)(2,1)S(1)} %pad_maximum_fusion.7), channel_id=1, source_target_pairs={{0,8},{8,0},{16,24},{24,16},{1,9},{9,1},{17,25},{25,17},{2,10},{10... | collective-permute-start | bytes 3145736 | tf_op jit(solution)/shard_map/ppermute | solution.py:49
  189.7 33.2 %collective-permute-start.5 = (bf16[8,128,2048]{2,1,0:T(8,128)(2,1)}, bf16[8,128,2048]{2,1,0:T(8,128)(2,1)}, u32[]{:S(2)}, u32[]{:S(2)}) collective-permute-start(bf16[8,128,2048]{2,1,0:T(8,128)(2,1)} %constant_dynamic-update-slice_fusion.46.one.two), channel_id=1, source_target_pairs={{0,1},{1,0},{2,3},{3,2},{4,5},{5,4},{6,7},{7,6},{8,9},{9,8},{10,11... | collective-permute-start | bytes 12582920 | tf_op jit(solution)/shard_map/ppermute | solution.py:49
  193.7 59.1 %all-to-all-start.2 = ((bf16[8,224,256]{2,1,0:T(8,128)(2,1)}), bf16[8,224,256]{2,1,0:T(8,128)(2,1)S(1)}, u32[]{:S(2)}, u32[]{:S(2)}) async-start(bf16[8,224,256]{2,1,0:T(8,128)(2,1)} %bitcast.37), calls=%async_computation.2 | async-start | bytes 1835008 | tf_op jit(solution)/shard_map/all_to_all | solution.py:809
  198.1 129.6 %all-gather.5.cloned.1.call-start = ((), (), s32[]{:S(2)}) async-start(), calls=%async_computation.5 | async-start | bytes 7208960 | tf_op jit(solution)/shard_map/all_gather | solution.py:795
  203.2 49.7 %collective-permute-start.8 = (bf16[176,2048]{1,0:T(8,128)(2,1)}, bf16[176,2048]{1,0:T(8,128)(2,1)}, u32[]{:S(2)}, u32[]{:S(2)}) collective-permute-start(bf16[176,2048]{1,0:T(8,128)(2,1)} %get-tuple-element.127), channel_id=1, source_target_pairs={{0,4},{1,5},{2,6},{3,7},{4,0},{5,1},{6,2},{7,3},{8,12},{9,13},{10,... | collective-permute-start | bytes 2162696 | tf_op jit(solution)/shard_map/ppermute | solution.py:49
  257.1 18.9 %collective-permute-start.9 = (bf16[1,88,2048]{2,1,0:T(8,128)(2,1)S(1)}, bf16[1,88,2048]{2,1,0:T(8,128)(2,1)S(1)}, u32[]{:S(2)}, u32[]{:S(2)}) collective-permute-start(bf16[1,88,2048]{2,1,0:T(8,128)(2,1)S(1)} %get-tuple-element.264), channel_id=1, source_target_pairs={{0,8},{8,0},{16,24},{24,16},{1,9},{9,1},{17,25},{25,17},{2,10},{10... | collective-permute-start | bytes 1081352 | tf_op jit(solution)/shard_map/ppermute | solution.py:49
  257.7 21.5 %collective-permute-start.11 = (bf16[224,2048]{1,0:T(8,128)(2,1)}, bf16[224,2048]{1,0:T(8,128)(2,1)S(1)}, u32[]{:S(2)}, u32[]{:S(2)}) collective-permute-start(bf16[224,2048]{1,0:T(8,128)(2,1)} %fusion.27), channel_id=1, source_target_pairs={{0,2},{1,3},{2,0},{3,1},{4,6},{5,7},{6,4},{7,5},{8,10},{9,11},{10,... | collective-permute-start | bytes 2752520 | tf_op jit(solution)/shard_map/ppermute | solution.py:49
  280.3 20.4 %collective-permute-start.16 = (bf16[224,2048]{1,0:T(8,128)(2,1)S(1)}, bf16[224,2048]{1,0:T(8,128)(2,1)S(1)}, u32[]{:S(2)}, u32[]{:S(2)}) collective-permute-start(bf16[224,2048]{1,0:T(8,128)(2,1)S(1)} %get-tuple-element.132), channel_id=1, source_target_pairs={{0,2},{1,3},{2,0},{3,1},{4,6},{5,7},{6,4},{7,5},{8,10},{9,11},{10,... | collective-permute-start | bytes 2752520 | tf_op jit(solution)/shard_map/ppermute | solution.py:49
  280.6 21.5 %collective-permute-start.14 = (bf16[2,88,2048]{2,1,0:T(8,128)(2,1)S(1)}, bf16[2,88,2048]{2,1,0:T(8,128)(2,1)S(1)}, u32[]{:S(2)}, u32[]{:S(2)}) collective-permute-start(bf16[2,88,2048]{2,1,0:T(8,128)(2,1)S(1)} %copy-done.55), channel_id=1, source_target_pairs={{0,16},{8,24},{16,0},{24,8},{1,17},{9,25},{17,1},{25,9},{2,18},{10... | collective-permute-start | bytes 2162696 | tf_op jit(solution)/shard_map/ppermute | solution.py:49
  282.1 21.2 %collective-permute-start.15 = (bf16[2,88,2048]{2,1,0:T(8,128)(2,1)S(1)}, bf16[2,88,2048]{2,1,0:T(8,128)(2,1)S(1)}, u32[]{:S(2)}, u32[]{:S(2)}) collective-permute-start(bf16[2,88,2048]{2,1,0:T(8,128)(2,1)S(1)} %copy-done.54), channel_id=1, source_target_pairs={{0,8},{8,0},{16,24},{24,16},{1,9},{9,1},{17,25},{25,17},{2,10},{10... | collective-permute-start | bytes 2162696 | tf_op jit(solution)/shard_map/ppermute | solution.py:49
  283.6 29.3 %collective-permute-start.12 = (bf16[2,88,2048]{2,1,0:T(8,128)(2,1)}, bf16[2,88,2048]{2,1,0:T(8,128)(2,1)}, u32[]{:S(2)}, u32[]{:S(2)}) collective-permute-start(bf16[2,88,2048]{2,1,0:T(8,128)(2,1)} %pad_maximum_fusion.12), channel_id=1, source_target_pairs={{0,16},{8,24},{16,0},{24,8},{1,17},{9,25},{17,1},{25,9},{2,18},{10... | collective-permute-start | bytes 2162696 | tf_op jit(solution)/shard_map/ppermute | solution.py:49
  284.1 29.5 %collective-permute-start.13 = (bf16[2,88,2048]{2,1,0:T(8,128)(2,1)}, bf16[2,88,2048]{2,1,0:T(8,128)(2,1)}, u32[]{:S(2)}, u32[]{:S(2)}) collective-permute-start(bf16[2,88,2048]{2,1,0:T(8,128)(2,1)} %pad_maximum_fusion.13), channel_id=1, source_target_pairs={{0,8},{8,0},{16,24},{24,16},{1,9},{9,1},{17,25},{25,17},{2,10},{10... | collective-permute-start | bytes 2162696 | tf_op jit(solution)/shard_map/ppermute | solution.py:49
  300.7 20.8 %collective-permute-start.18 = (bf16[448,2048]{1,0:T(8,128)(2,1)}, bf16[448,2048]{1,0:T(8,128)(2,1)}, u32[]{:S(2)}, u32[]{:S(2)}) collective-permute-start(bf16[448,2048]{1,0:T(8,128)(2,1)} %constant_dynamic-update-slice_fusion.50), channel_id=1, source_target_pairs={{0,1},{1,0},{2,3},{3,2},{4,5},{5,4},{6,7},{7,6},{8,9},{9,8},{10,11... | collective-permute-start | bytes 5505032 | tf_op jit(solution)/shard_map/ppermute | solution.py:49
  302.1 22.4 %collective-permute-start.17 = (bf16[448,2048]{1,0:T(8,128)(2,1)}, bf16[448,2048]{1,0:T(8,128)(2,1)}, u32[]{:S(2)}, u32[]{:S(2)}) collective-permute-start(bf16[448,2048]{1,0:T(8,128)(2,1)} %pad_maximum_fusion.3), channel_id=1, source_target_pairs={{0,1},{1,0},{2,3},{3,2},{4,5},{5,4},{6,7},{7,6},{8,9},{9,8},{10,11... | collective-permute-start | bytes 5505032 | tf_op jit(solution)/shard_map/ppermute | solution.py:49
  382.3 22.8 %collective-permute-start.20 = (bf16[224,2048]{1,0:T(8,128)(2,1)S(1)}, bf16[224,2048]{1,0:T(8,128)(2,1)S(1)}, u32[]{:S(2)}, u32[]{:S(2)}) collective-permute-start(bf16[224,2048]{1,0:T(8,128)(2,1)S(1)} %slice.503), channel_id=1, source_target_pairs={{0,2},{1,3},{2,0},{3,1},{4,6},{5,7},{6,4},{7,5},{8,10},{9,11},{10,... | collective-permute-start | bytes 2752520 | tf_op jit(solution)/shard_map/ppermute | solution.py:49
  415.2 19.6 %collective-permute-start.21 = (bf16[448,2048]{1,0:T(8,128)(2,1)}, bf16[448,2048]{1,0:T(8,128)(2,1)}, u32[]{:S(2)}, u32[]{:S(2)}) collective-permute-start(bf16[448,2048]{1,0:T(8,128)(2,1)} %slice.308), channel_id=1, source_target_pairs={{0,1},{1,0},{2,3},{3,2},{4,5},{5,4},{6,7},{7,6},{8,9},{9,8},{10,11... | collective-permute-start | bytes 5505032 | tf_op jit(solution)/shard_map/ppermute | solution.py:49
  416.1 28.9 %all-to-all-start.3 = ((bf16[8,224,256]{2,1,0:T(8,128)(2,1)}), bf16[8,224,256]{2,1,0:T(8,128)(2,1)S(1)}, u32[]{:S(2)}, u32[]{:S(2)}) async-start(bf16[8,224,256]{2,1,0:T(8,128)(2,1)} %bitcast.451), calls=%async_computation.3 | async-start | bytes 1835008 | tf_op jit(solution)/shard_map/all_to_all | solution.py:876
  438.8 27.4 %collective-permute-start.22 = (bf16[224,2048]{1,0:T(8,128)(2,1)}, bf16[224,2048]{1,0:T(8,128)(2,1)}, u32[]{:S(2)}, u32[]{:S(2)}) collective-permute-start(bf16[224,2048]{1,0:T(8,128)(2,1)} %slice.502), channel_id=1, source_target_pairs={{0,2},{1,3},{2,0},{3,1},{4,6},{5,7},{6,4},{7,5},{8,10},{9,11},{10,... | collective-permute-start | bytes 2752520 | tf_op jit(solution)/shard_map/ppermute | solution.py:49
  469.2 28.2 %collective-permute-start.24 = (f32[2048]{0:T(1024)S(1)}, f32[2048]{0:T(1024)S(1)}, u32[]{:S(2)}, u32[]{:S(2)}) collective-permute-start(f32[2048]{0:T(1024)S(1)} %get-tuple-element.304), channel_id=1, source_target_pairs={{0,1},{1,0},{2,3},{3,2},{4,5},{5,4},{6,7},{7,6},{8,9},{9,8},{10,11... | collective-permute-start | bytes 24584 | tf_op jit(solution)/shard_map/ppermute | solution.py:49
  504.3 23.6 %collective-permute-start.25 = (bf16[224,2048]{1,0:T(8,128)(2,1)}, bf16[224,2048]{1,0:T(8,128)(2,1)}, u32[]{:S(2)}, u32[]{:S(2)}) collective-permute-start(bf16[224,2048]{1,0:T(8,128)(2,1)} %get-tuple-element.164), channel_id=1, source_target_pairs={{0,2},{1,3},{8,10},{9,11},{16,18},{17,19},{24,26},{25,27}} | collective-permute-start | bytes 2752520 | tf_op jit(solution)/shard_map/ppermute | solution.py:529
  508.9 18.9 %collective-permute-start.26 = (bf16[224,2048]{1,0:T(8,128)(2,1)}, bf16[224,2048]{1,0:T(8,128)(2,1)}, u32[]{:S(2)}, u32[]{:S(2)}) collective-permute-start(bf16[224,2048]{1,0:T(8,128)(2,1)} %get-tuple-element.165), channel_id=1, source_target_pairs={{6,4},{7,5},{14,12},{15,13},{22,20},{23,21},{30,28},{31,29}} | collective-permute-start | bytes 2752520 | tf_op jit(solution)/shard_map/ppermute | solution.py:529
  547.6 23.0 %collective-permute-start.28 = (bf16[224,2048]{1,0:T(8,128)(2,1)S(1)}, bf16[224,2048]{1,0:T(8,128)(2,1)}, u32[]{:S(2)}, u32[]{:S(2)}) collective-permute-start(bf16[224,2048]{1,0:T(8,128)(2,1)S(1)} %get-tuple-element.175), channel_id=1, source_target_pairs={{0,2},{1,3},{2,4},{3,5},{8,10},{9,11},{10,12},{11,13},{16,18},{17,... | collective-permute-start | bytes 2752520 | tf_op jit(solution)/shard_map/ppermute | solution.py:529
  577.0 18.7 %collective-permute-start.33 = (f32[16,5632]{1,0:T(8,128)S(1)}, f32[16,5632]{1,0:T(8,128)S(1)}, u32[]{:S(2)}, u32[]{:S(2)}) collective-permute-start(f32[16,5632]{1,0:T(8,128)S(1)} %get-tuple-element.253), channel_id=1, source_target_pairs={{0,8},{8,0},{16,24},{24,16},{1,9},{9,1},{17,25},{25,17},{2,10},{10... | collective-permute-start | bytes 1081352 | tf_op jit(solution)/shard_map/ppermute | solution.py:49
  583.9 41.3 %collective-permute-start.30 = (bf16[224,2048]{1,0:T(8,128)(2,1)}, bf16[224,2048]{1,0:T(8,128)(2,1)}, u32[]{:S(2)}, u32[]{:S(2)}) collective-permute-start(bf16[224,2048]{1,0:T(8,128)(2,1)} %get-tuple-element.190), channel_id=1, source_target_pairs={{0,2},{1,3},{2,4},{3,5},{4,6},{5,7},{8,10},{9,11},{10,12},{11,13},... | collective-permute-start | bytes 2752520 | tf_op jit(solution)/shard_map/ppermute | solution.py:529
  594.2 31.0 %collective-permute-start.31 = (bf16[224,2048]{1,0:T(8,128)(2,1)}, bf16[224,2048]{1,0:T(8,128)(2,1)}, u32[]{:S(2)}, u32[]{:S(2)}) collective-permute-start(bf16[224,2048]{1,0:T(8,128)(2,1)} %get-tuple-element.191), channel_id=1, source_target_pairs={{2,0},{3,1},{4,2},{5,3},{6,4},{7,5},{10,8},{11,9},{12,10},{13,11},... | collective-permute-start | bytes 2752520 | tf_op jit(solution)/shard_map/ppermute | solution.py:529
  597.1 25.3 %collective-permute-start.36 = (f32[16,1408]{1,0:T(8,128)S(1)}, f32[16,1408]{1,0:T(8,128)S(1)}, u32[]{:S(2)}, u32[]{:S(2)}) collective-permute-start(f32[16,1408]{1,0:T(8,128)S(1)} %get-tuple-element.272), channel_id=1, source_target_pairs={{0,2},{1,3},{2,0},{3,1},{4,6},{5,7},{6,4},{7,5},{8,10},{9,11},{10,... | collective-permute-start | bytes 270344 | tf_op jit(solution)/shard_map/ppermute | solution.py:49
  605.1 19.1 %collective-permute-start.37 = (f32[16,1408]{1,0:T(8,128)S(1)}, f32[16,1408]{1,0:T(8,128)}, u32[]{:S(2)}, u32[]{:S(2)}) collective-permute-start(f32[16,1408]{1,0:T(8,128)S(1)} %get-tuple-element.274), channel_id=1, source_target_pairs={{0,4},{1,5},{2,6},{3,7},{4,0},{5,1},{6,2},{7,3},{8,12},{9,13},{10,... | collective-permute-start | bytes 270344 | tf_op jit(solution)/shard_map/ppermute | solution.py:49
  (139 other events, 1596.8 us)
Sparse Core Ops, SparseCore 0:
  11.5 98.3 all-gather.2
  200.8 74.8 all-gather.4

commit v3 on v2

--- a/solution.py
+++ b/solution.py
@@ -964,14 +964,15 @@
     packed = packed_up(tables, vectors)
     for t in range(2, chips - 1):
         state = chips_step(total, t, state)
-        state = after(state, packed)
-    packed = after(packed, state)
     ends = {}
 
     def between(buffer, stage):
-        if stage == 2:
-            ends[0] = after(chips_step(total, chips - 1, state), buffer)
-            buffer = after(buffer, ends[0])
+        if stage == 0:
+            ends[1] = after(state, buffer)
+        if stage == 1:
+            buffer = after(buffer, ends[1])
+        if stage == 3:
+            ends[0] = chips_step(total, chips - 1, after(ends[1], buffer))
         return buffer
 
     tables, vectors = unpacked(total_sum(packed, between), tables, vectors)

time: 681 us -> 668 us (0.981)
  starting transfers between devices: 85 us -> 74.7 us
    ppermute x6, waiting for transfers between devices: 10.9 us -> 28.5 us  [step_chips(): return lax.ppermute(array, 'blk', pairs)]
    ppermute x40, waiting for transfers between devices: 104 us -> 87.4 us  [swap(): lax.ppermute(array, axis, [(i, i ^ bit) for i in range(lax.axis_size(axis...]
    unnamed x277 -> x275, local copies, waits for them, and re-layouts: 35.9 us -> 35.9 us
  transfers between devices with their start and end apart: 52 -> 52, of which waited for: 18 -> 22; matrix products, arithmetic and copies ran while one was open for 28% -> 27% of each run, Pallas kernels for 15% -> 16%
where the time goes in v3:
time: 668 us; the launch traced here: 658 us
  waiting for transfers between devices  171 us (26%)
  Pallas kernels  130 us (19%)
  matrix products  95.2 us (14%)
  local copies, waits for them, and re-layouts  86.4 us (13%)
  other arithmetic  84.2 us (13%)
  starting transfers between devices  74.7 us (11%)
  between operations  16.8 us (3%)
    dot_general x21, matrix products, dot(): return lax.dot_general(a, b, dims, preferred_element_type=f32)  95.2 us
    ppermute x40, waiting for transfers between devices, swap(): lax.ppermute(array, axis, [(i, i ^ bit) for i in range(lax.axis_size(axis...  87.4 us
    all_to_all x2, waiting for transfers between devices, spread_rows(): got = lax.all_to_all(chunks, 'blk', 0, 0, tiled=True)  54.2 us
    ppermute x40, starting transfers between devices, swap(): lax.ppermute(array, axis, [(i, i ^ bit) for i in range(lax.axis_size(axis...  37.2 us
    unnamed x275, local copies, waits for them, and re-layouts  35.9 us
    ppermute x6, waiting for transfers between devices, step_chips(): return lax.ppermute(array, 'blk', pairs)  28.5 us
    pallas_call x1, Pallas kernels, feed_forward(): pl.pallas_call(feed_kernel, grid=(mates, steps), in_specs=[pl.BlockSpec((...  26.7 us
    pallas_call x4, Pallas kernels, dp_lay(): pl.pallas_call(lay_kernel, grid_spec=pltpu.PrefetchScalarGridSpec(num_sca...  20.5 us
  transfers between devices with their start and end apart: 52, of which 22 were waited for; matrix products, arithmetic and copies ran while one was open for 27% of the time, Pallas kernels for 16%

profile of v3, /device:TPU:0, one launch (start us, length us, event | category | flops | bytes accessed | tf_op | source)
XLA Modules:
  0.0 658.0 jit_solution(3565924676281757721)
XLA Ops:
  18.4 7.4 %merge.5 = (bf16[5632,256]{1,0:T(8,128)(2,1)S(1)}, f32[1,256]{1,0:T(1,128)S(1)}) custom-call(bf16[1,5632,256]{2,1,0:T(8,128)(2,1)} %bitcast.453, bf16[1,96,5632]{2,1,0:T(8,128)(2,1)S(1)} %fusion.46.a_ref, bf16[1,96,256]{2,1,0:T(8,128)(2,1)S(1)} %constant_dynamic-update-slice_fusion.40.b_ref, f32[1,256]{1,0:T(1,128)S(1)} %bitcast.420), custom_call_target="tpu_custom_call" | custom-call | flops 276824064 | bytes 5767168 | tf_op jit(solution)/shard_map/merge/pallas_call | solution.py:110
  27.6 8.0 %merge.4 = (bf16[2048,768]{1,0:T(8,128)(2,1)S(1)}, f32[1,768]{1,0:T(1,128)S(1)}) custom-call(bf16[3,2048,256]{2,1,0:T(8,128)(2,1)} %w_ref.1, bf16[3,96,2048]{2,1,0:T(8,128)(2,1)S(1)} %fusion.44.a_ref, bf16[3,96,256]{2,1,0:T(8,128)(2,1)S(1)} %constant_dynamic-update-slice_fusion.29.b_ref, f32[1,768]{1,0:T(1,128)S(1)} %reshape.496.m_ref), custom_call_target="tpu_custom_call" | custom-call | flops 301989888 | bytes 6291456 | tf_op jit(solution)/shard_map/merge/pallas_call | solution.py:110
  38.8 7.4 %merge_rows.1 = (bf16[2,2,704,2048]{3,2,1,0:T(8,128)(2,1)}, f32[2,704,1]{2,1,0:T(8,128)}) custom-call(bf16[2,704,2048]{2,1,0:T(8,128)(2,1)} %bitcast.449, bf16[2,96,2048]{2,1,0:T(8,128)(2,1)} %copy-done.61, bf16[2,96,704]{2,1,0:T(8,128)(2,1)} %copy-done.68, f32[2,704,1]{2,1,0:T(8,128)} %copy.76.m_ref), custom_call_target="tpu_custom_call" | custom-call | flops 553648128 | bytes 11534336 | tf_op jit(solution)/shard_map/merge_rows/pallas_call | solution.py:145
  51.3 6.4 all-to-all-start
  62.3 45.4 %all-to-all-done = bf16[8,256,256]{2,1,0:T(8,128)(2,1)S(1)} async-done(((bf16[8,256,256]{2,1,0:T(8,128)(2,1)}), bf16[8,256,256]{2,1,0:T(8,128)(2,1)S(1)}, u32[]{:S(2)}, u32[]{:S(2)}) %all-to-all-start) | async-done | bytes 1048608 | tf_op jit(solution)/shard_map/all_to_all | solution.py:744
  128.4 7.8 %collective-permute-done = bf16[1,128,2048]{2,1,0:T(8,128)(2,1)} collective-permute-done((bf16[1,128,2048]{2,1,0:T(8,128)(2,1)}, bf16[1,128,2048]{2,1,0:T(8,128)(2,1)}, u32[]{:S(2)}, u32[]{:S(2)}) %collective-permute-start) | collective-permute-done | bytes 524320 | tf_op jit(solution)/shard_map/ppermute | solution.py:49
  139.6 8.9 %all-to-all-done.1 = bf16[8,368,256]{2,1,0:T(8,128)(2,1)} async-done(((bf16[8,368,256]{2,1,0:T(8,128)(2,1)}), bf16[8,368,256]{2,1,0:T(8,128)(2,1)}, u32[]{:S(2)}, u32[]{:S(2)}) %all-to-all-start.1) | async-done | bytes 1507360 | tf_op jit(solution)/shard_map/all_to_all | solution.py:744
  154.3 10.5 %fusion.113.pre = f32[1792,768]{1,0:T(8,128)} fusion(bf16[1792,2048]{1,0:T(8,128)(2,1)} %all-gather.3.cloned.1.call-done.h_ref, bf16[2048,768]{1,0:T(8,128)(2,1)} %copy-done.2), kind=kOutput, calls=%fused_computation.425 | convolution fusion | flops 5637144576 | bytes 15990784 | tf_op jit(solution)/shard_map/dot_general | solution.py:32
  164.9 20.3 %attend.1 = (bf16[1792,256]{1,0:T(8,128)(2,1)S(1)}, bf16[1792,256]{1,0:T(8,128)(2,1)S(1)}, bf16[1792,256]{1,0:T(8,128)(2,1)S(1)}, bf16[1792,256]{1,0:T(8,128)(2,...) custom-call(f32[1792,768]{1,0:T(8,128)} %fusion.113.pre, f32[1792,128]{1,0:T(8,128)S(1)} %pad_maximum_fusion.8.cosine, ...), custom_call_target="tpu_custom_call" | custom-call | flops 1644167168 | bytes 13762560 | tf_op jit(solution)/shard_map/attend/pallas_call | solution.py:282
  206.1 6.3 fusion.7
  213.3 5.4 lay.4.into
  222.8 5.4 lay.5
  228.2 24.6 %collective-permute-done.8 = bf16[176,2048]{1,0:T(8,128)(2,1)} collective-permute-done((bf16[176,2048]{1,0:T(8,128)(2,1)}, bf16[176,2048]{1,0:T(8,128)(2,1)}, u32[]{:S(2)}, u32[]{:S(2)}) %collective-permute-start.8) | collective-permute-done | bytes 720928 | tf_op jit(solution)/shard_map/ppermute | solution.py:49
  257.7 5.6 fusion.30
  266.7 8.4 %collective-permute-done.10 = bf16[1,88,2048]{2,1,0:T(8,128)(2,1)S(1)} collective-permute-done((bf16[1,88,2048]{2,1,0:T(8,128)(2,1)S(1)}, bf16[1,88,2048]{2,1,0:T(8,128)(2,1)S(1)}, u32[]{:S(2)}, u32[]{:S(2)}) %collective-permute-start.10) | collective-permute-done | bytes 360480 | tf_op jit(solution)/shard_map/ppermute | solution.py:49
  284.6 16.1 %collective-permute-done.16 = bf16[224,2048]{1,0:T(8,128)(2,1)S(1)} collective-permute-done((bf16[224,2048]{1,0:T(8,128)(2,1)S(1)}, bf16[224,2048]{1,0:T(8,128)(2,1)S(1)}, u32[]{:S(2)}, u32[]{:S(2)}) %collective-permute-start.16) | collective-permute-done | bytes 917536 | tf_op jit(solution)/shard_map/ppermute | solution.py:49
  305.1 4.9 lay.6.into
  316.7 4.8 lay.7
  327.7 26.7 %feed_forward.1 = (bf16[1408,896]{1,0:T(8,128)(2,1)}, bf16[2,2,704,896]{3,2,1,0:T(8,128)(2,1)}, f32[2,2,704,1]{3,2,1,0:T(8,128)}) custom-call(bf16[2,2,704,2048]{3,2,1,0:T(8,128)(2,1)} %bitcast.425, bf16[1408,2048]{1,0:T(8,128)(2,1)} %all-gather.5.cloned.1.call-done.down_ref, bf16[896,2048]{1,0:T(8,128)(2,1)} %pad_maximum_fusion.h_ref, ...), custom_call_target="tpu_custom_call" | custom-call | flops 15502147584 | bytes 24641536 | tf_op jit(solution)/shard_map/feed_forward/pallas_call | solution.py:376
  354.4 15.4 %convolution_convert_fusion = bf16[896,2048]{1,0:T(8,128)(2,1)S(1)} fusion(bf16[2816,896]{1,0:T(8,128)(2,1)} %bitcast.441, bf16[2816,2048]{1,0:T(8,128)(2,1)} %bitcast.426), kind=kOutput, calls=%fused_computation.4 | convolution fusion | flops 10336600064 | bytes 20250624 | tf_op jit(solution)/shard_map/dot_general | solution.py:32
  383.8 8.9 %convolution_convert_fusion.1 = bf16[896,2048]{1,0:T(8,128)(2,1)S(1)} fusion(bf16[1408,896]{1,0:T(8,128)(2,1)S(1)} %copy-done.37, bf16[1408,2048]{1,0:T(8,128)(2,1)} %all-gather.5.cloned.1.call-done.down_ref), kind=kOutput, calls=%fused_computation.5 | convolution fusion | flops 5169217536 | bytes 11960320 | tf_op jit(solution)/shard_map/dot_general | solution.py:32
  399.2 5.9 collective-permute-done.20
  421.9 7.0 %fusion.2 = f32[32,2816]{1,0:T(8,128)} fusion(bf16[2816,896]{1,0:T(8,128)(2,1)} %bitcast.442, bf16[896,2048]{1,0:T(8,128)(2,1)} %pad_maximum_fusion.h_ref, bf16[32,2048]{1,0:T(8,128)(2,1)S(1)} %bitcast.470, f32[32,2816]{1,0:T(8,128)S(1)} %convolution_bitcast_fusion, f32[2816]{0:T(1024)S(1)} %get-tuple-element.294, f32[2816]{0:T(1024)S(1)} %get-tuple-element.295, ...), kind=kOutput, calls=%fused_computation.9 | convolution fusion | flops 280662016 | bytes 9616416 | tf_op jit(solution)/shard_map/dot_general | solution.py:32
  448.5 17.7 %attend_back.1 = (bf16[1792,768]{1,0:T(8,128)(2,1)}, f32[8,768]{1,0:T(8,128)S(1)}) custom-call(bf16[1792,256]{1,0:T(8,128)(2,1)S(1)} %copy-done.7, bf16[1792,256]{1,0:T(8,128)(2,1)S(1)} %copy-done.9, bf16[1792,256]{1,0:T(8,128)(2,1)S(1)} %copy-done.11, f32[1792,768]{1,0:T(8,128)} %fusion.113.pre, f32[1792,128]{1,0:T(8,128)S(1)} %pad_maximum_fusion.8.cosine, ...), custom_call_target="tpu_custom_call" | custom-call | flops 4110417920 | bytes 18350080 | tf_op jit(solution)/shard_map/attend_back/pallas_call | solution.py:319
  469.3 19.4 %back_qkv.1 = (bf16[4,224,2048]{2,1,0:T(8,128)(2,1)}, bf16[4,224,2048]{2,1,0:T(8,128)(2,1)}, f32[48,2048]{1,0:T(8,128)}, f32[48,768]{1,0:T(8,128)}, f32[1,2048]{1,0:T(1,128)}, /*index=5*/f32[1,768]{1,0:T(1,128)}) custom-call(s32[1]{0:T(128)} %bitcast.130.core, bf16[1792,768]{1,0:T(8,128)(2,1)} %get-tuple-element.157.g_ref, ...), custom_call_target="tpu_custom_call" | custom-call | flops 8455716864 | bytes 29360128 | tf_op jit(solution)/shard_map/back_qkv/pallas_call | solution.py:459
  497.4 5.1 add_convert_fusion
  513.7 6.5 constant_dynamic-update-slice_fusion.69
  527.9 6.5 fusion.114
  555.1 5.3 collective-permute-start.28
  567.4 12.6 %collective-permute-done.28 = bf16[224,2048]{1,0:T(8,128)(2,1)} collective-permute-done((bf16[224,2048]{1,0:T(8,128)(2,1)}, bf16[224,2048]{1,0:T(8,128)(2,1)}, u32[]{:S(2)}, u32[]{:S(2)}) %collective-permute-start.28) | collective-permute-done | bytes 917536 | tf_op jit(solution)/shard_map/ppermute | solution.py:529
  603.7 4.7 collective-permute-done.38
  625.2 10.7 %collective-permute-done.40 = bf16[224,2048]{1,0:T(8,128)(2,1)S(1)} collective-permute-done((bf16[224,2048]{1,0:T(8,128)(2,1)S(1)}, bf16[224,2048]{1,0:T(8,128)(2,1)S(1)}, u32[]{:S(2)}, u32[]{:S(2)}) %collective-permute-start.40) | collective-permute-done | bytes 917536 | tf_op jit(solution)/shard_map/ppermute | solution.py:529
  (629 shorter events, 285.1 us)
Async XLA Ops:
  7.3 144.1 %all-gather.3.cloned.1.call-start = ((), (), s32[]{:S(2)}) async-start(), calls=%async_computation.4 | async-start | bytes 8257536 | tf_op jit(solution)/shard_map/all_gather | solution.py:703
  51.3 56.3 %all-to-all-start = ((bf16[8,256,256]{2,1,0:T(8,128)(2,1)}), bf16[8,256,256]{2,1,0:T(8,128)(2,1)S(1)}, u32[]{:S(2)}, u32[]{:S(2)}) async-start(bf16[8,256,256]{2,1,0:T(8,128)(2,1)} %bitcast.29), calls=%async_computation | async-start | bytes 2097152 | tf_op jit(solution)/shard_map/all_to_all | solution.py:744
  107.6 40.9 %all-to-all-start.1 = ((bf16[8,368,256]{2,1,0:T(8,128)(2,1)}), bf16[8,368,256]{2,1,0:T(8,128)(2,1)}, u32[]{:S(2)}, u32[]{:S(2)}) async-start(bf16[8,368,256]{2,1,0:T(8,128)(2,1)} %pad_maximum_fusion.4), calls=%async_computation.1 | async-start | bytes 3014656 | tf_op jit(solution)/shard_map/all_to_all | solution.py:744
  151.3 38.3 %collective-permute-start.4 = (bf16[176,2048]{1,0:T(8,128)(2,1)}, bf16[176,2048]{1,0:T(8,128)(2,1)}, u32[]{:S(2)}, u32[]{:S(2)}) collective-permute-start(bf16[176,2048]{1,0:T(8,128)(2,1)} %get-tuple-element.120), channel_id=1, source_target_pairs={{0,4},{1,5},{2,6},{3,7},{4,0},{5,1},{6,2},{7,3},{8,12},{9,13},{10,... | collective-permute-start | bytes 2162696 | tf_op jit(solution)/shard_map/ppermute | solution.py:49
  151.3 35.1 %collective-permute-start.2 = (bf16[2,128,2048]{2,1,0:T(8,128)(2,1)}, bf16[2,128,2048]{2,1,0:T(8,128)(2,1)S(1)}, u32[]{:S(2)}, u32[]{:S(2)}) collective-permute-start(bf16[2,128,2048]{2,1,0:T(8,128)(2,1)} %pad_maximum_fusion.6), channel_id=1, source_target_pairs={{0,16},{8,24},{16,0},{24,8},{1,17},{9,25},{17,1},{25,9},{2,18},{10... | collective-permute-start | bytes 3145736 | tf_op jit(solution)/shard_map/ppermute | solution.py:49
  152.8 35.7 %collective-permute-start.3 = (bf16[2,128,2048]{2,1,0:T(8,128)(2,1)S(1)}, bf16[2,128,2048]{2,1,0:T(8,128)(2,1)S(1)}, u32[]{:S(2)}, u32[]{:S(2)}) collective-permute-start(bf16[2,128,2048]{2,1,0:T(8,128)(2,1)S(1)} %pad_maximum_fusion.7), channel_id=1, source_target_pairs={{0,8},{8,0},{16,24},{24,16},{1,9},{9,1},{17,25},{25,17},{2,10},{10... | collective-permute-start | bytes 3145736 | tf_op jit(solution)/shard_map/ppermute | solution.py:49
  189.7 33.2 %collective-permute-start.5 = (bf16[8,128,2048]{2,1,0:T(8,128)(2,1)}, bf16[8,128,2048]{2,1,0:T(8,128)(2,1)}, u32[]{:S(2)}, u32[]{:S(2)}) collective-permute-start(bf16[8,128,2048]{2,1,0:T(8,128)(2,1)} %constant_dynamic-update-slice_fusion.46.one.two), channel_id=1, source_target_pairs={{0,1},{1,0},{2,3},{3,2},{4,5},{5,4},{6,7},{7,6},{8,9},{9,8},{10,11... | collective-permute-start | bytes 12582920 | tf_op jit(solution)/shard_map/ppermute | solution.py:49
  193.7 59.1 %all-to-all-start.2 = ((bf16[8,224,256]{2,1,0:T(8,128)(2,1)}), bf16[8,224,256]{2,1,0:T(8,128)(2,1)S(1)}, u32[]{:S(2)}, u32[]{:S(2)}) async-start(bf16[8,224,256]{2,1,0:T(8,128)(2,1)} %bitcast.37), calls=%async_computation.2 | async-start | bytes 1835008 | tf_op jit(solution)/shard_map/all_to_all | solution.py:809
  198.1 129.6 %all-gather.5.cloned.1.call-start = ((), (), s32[]{:S(2)}) async-start(), calls=%async_computation.5 | async-start | bytes 7208960 | tf_op jit(solution)/shard_map/all_gather | solution.py:795
  202.6 18.2 %collective-permute-start.6 = (bf16[1,88,2048]{2,1,0:T(8,128)(2,1)}, bf16[1,88,2048]{2,1,0:T(8,128)(2,1)}, u32[]{:S(2)}, u32[]{:S(2)}) collective-permute-start(bf16[1,88,2048]{2,1,0:T(8,128)(2,1)} %get-tuple-element.266), channel_id=1, source_target_pairs={{0,8},{8,0},{16,24},{24,16},{1,9},{9,1},{17,25},{25,17},{2,10},{10... | collective-permute-start | bytes 1081352 | tf_op jit(solution)/shard_map/ppermute | solution.py:49
  203.2 49.7 %collective-permute-start.8 = (bf16[176,2048]{1,0:T(8,128)(2,1)}, bf16[176,2048]{1,0:T(8,128)(2,1)}, u32[]{:S(2)}, u32[]{:S(2)}) collective-permute-start(bf16[176,2048]{1,0:T(8,128)(2,1)} %get-tuple-element.126), channel_id=1, source_target_pairs={{0,4},{1,5},{2,6},{3,7},{4,0},{5,1},{6,2},{7,3},{8,12},{9,13},{10,... | collective-permute-start | bytes 2162696 | tf_op jit(solution)/shard_map/ppermute | solution.py:49
  256.6 18.5 %collective-permute-start.10 = (bf16[1,88,2048]{2,1,0:T(8,128)(2,1)S(1)}, bf16[1,88,2048]{2,1,0:T(8,128)(2,1)S(1)}, u32[]{:S(2)}, u32[]{:S(2)}) collective-permute-start(bf16[1,88,2048]{2,1,0:T(8,128)(2,1)S(1)} %get-tuple-element.263), channel_id=1, source_target_pairs={{0,16},{8,24},{16,0},{24,8},{1,17},{9,25},{17,1},{25,9},{2,18},{10... | collective-permute-start | bytes 1081352 | tf_op jit(solution)/shard_map/ppermute | solution.py:49
  257.1 18.9 %collective-permute-start.9 = (bf16[1,88,2048]{2,1,0:T(8,128)(2,1)S(1)}, bf16[1,88,2048]{2,1,0:T(8,128)(2,1)S(1)}, u32[]{:S(2)}, u32[]{:S(2)}) collective-permute-start(bf16[1,88,2048]{2,1,0:T(8,128)(2,1)S(1)} %get-tuple-element.264), channel_id=1, source_target_pairs={{0,8},{8,0},{16,24},{24,16},{1,9},{9,1},{17,25},{25,17},{2,10},{10... | collective-permute-start | bytes 1081352 | tf_op jit(solution)/shard_map/ppermute | solution.py:49
  257.7 21.5 %collective-permute-start.11 = (bf16[224,2048]{1,0:T(8,128)(2,1)}, bf16[224,2048]{1,0:T(8,128)(2,1)S(1)}, u32[]{:S(2)}, u32[]{:S(2)}) collective-permute-start(bf16[224,2048]{1,0:T(8,128)(2,1)} %fusion.27), channel_id=1, source_target_pairs={{0,2},{1,3},{2,0},{3,1},{4,6},{5,7},{6,4},{7,5},{8,10},{9,11},{10,... | collective-permute-start | bytes 2752520 | tf_op jit(solution)/shard_map/ppermute | solution.py:49
  280.3 20.4 %collective-permute-start.16 = (bf16[224,2048]{1,0:T(8,128)(2,1)S(1)}, bf16[224,2048]{1,0:T(8,128)(2,1)S(1)}, u32[]{:S(2)}, u32[]{:S(2)}) collective-permute-start(bf16[224,2048]{1,0:T(8,128)(2,1)S(1)} %get-tuple-element.131), channel_id=1, source_target_pairs={{0,2},{1,3},{2,0},{3,1},{4,6},{5,7},{6,4},{7,5},{8,10},{9,11},{10,... | collective-permute-start | bytes 2752520 | tf_op jit(solution)/shard_map/ppermute | solution.py:49
  280.6 21.5 %collective-permute-start.14 = (bf16[2,88,2048]{2,1,0:T(8,128)(2,1)S(1)}, bf16[2,88,2048]{2,1,0:T(8,128)(2,1)S(1)}, u32[]{:S(2)}, u32[]{:S(2)}) collective-permute-start(bf16[2,88,2048]{2,1,0:T(8,128)(2,1)S(1)} %copy-done.54), channel_id=1, source_target_pairs={{0,16},{8,24},{16,0},{24,8},{1,17},{9,25},{17,1},{25,9},{2,18},{10... | collective-permute-start | bytes 2162696 | tf_op jit(solution)/shard_map/ppermute | solution.py:49
  282.1 21.2 %collective-permute-start.15 = (bf16[2,88,2048]{2,1,0:T(8,128)(2,1)S(1)}, bf16[2,88,2048]{2,1,0:T(8,128)(2,1)S(1)}, u32[]{:S(2)}, u32[]{:S(2)}) collective-permute-start(bf16[2,88,2048]{2,1,0:T(8,128)(2,1)S(1)} %copy-done.53), channel_id=1, source_target_pairs={{0,8},{8,0},{16,24},{24,16},{1,9},{9,1},{17,25},{25,17},{2,10},{10... | collective-permute-start | bytes 2162696 | tf_op jit(solution)/shard_map/ppermute | solution.py:49
  283.6 29.3 %collective-permute-start.12 = (bf16[2,88,2048]{2,1,0:T(8,128)(2,1)}, bf16[2,88,2048]{2,1,0:T(8,128)(2,1)}, u32[]{:S(2)}, u32[]{:S(2)}) collective-permute-start(bf16[2,88,2048]{2,1,0:T(8,128)(2,1)} %pad_maximum_fusion.12), channel_id=1, source_target_pairs={{0,16},{8,24},{16,0},{24,8},{1,17},{9,25},{17,1},{25,9},{2,18},{10... | collective-permute-start | bytes 2162696 | tf_op jit(solution)/shard_map/ppermute | solution.py:49
  284.1 29.5 %collective-permute-start.13 = (bf16[2,88,2048]{2,1,0:T(8,128)(2,1)}, bf16[2,88,2048]{2,1,0:T(8,128)(2,1)}, u32[]{:S(2)}, u32[]{:S(2)}) collective-permute-start(bf16[2,88,2048]{2,1,0:T(8,128)(2,1)} %pad_maximum_fusion.13), channel_id=1, source_target_pairs={{0,8},{8,0},{16,24},{24,16},{1,9},{9,1},{17,25},{25,17},{2,10},{10... | collective-permute-start | bytes 2162696 | tf_op jit(solution)/shard_map/ppermute | solution.py:49
  300.7 20.8 %collective-permute-start.18 = (bf16[448,2048]{1,0:T(8,128)(2,1)}, bf16[448,2048]{1,0:T(8,128)(2,1)}, u32[]{:S(2)}, u32[]{:S(2)}) collective-permute-start(bf16[448,2048]{1,0:T(8,128)(2,1)} %constant_dynamic-update-slice_fusion.50), channel_id=1, source_target_pairs={{0,1},{1,0},{2,3},{3,2},{4,5},{5,4},{6,7},{7,6},{8,9},{9,8},{10,11... | collective-permute-start | bytes 5505032 | tf_op jit(solution)/shard_map/ppermute | solution.py:49
  302.1 22.4 %collective-permute-start.17 = (bf16[448,2048]{1,0:T(8,128)(2,1)}, bf16[448,2048]{1,0:T(8,128)(2,1)}, u32[]{:S(2)}, u32[]{:S(2)}) collective-permute-start(bf16[448,2048]{1,0:T(8,128)(2,1)} %pad_maximum_fusion.3), channel_id=1, source_target_pairs={{0,1},{1,0},{2,3},{3,2},{4,5},{5,4},{6,7},{7,6},{8,9},{9,8},{10,11... | collective-permute-start | bytes 5505032 | tf_op jit(solution)/shard_map/ppermute | solution.py:49
  382.3 22.8 %collective-permute-start.20 = (bf16[224,2048]{1,0:T(8,128)(2,1)S(1)}, bf16[224,2048]{1,0:T(8,128)(2,1)S(1)}, u32[]{:S(2)}, u32[]{:S(2)}) collective-permute-start(bf16[224,2048]{1,0:T(8,128)(2,1)S(1)} %slice.503), channel_id=1, source_target_pairs={{0,2},{1,3},{2,0},{3,1},{4,6},{5,7},{6,4},{7,5},{8,10},{9,11},{10,... | collective-permute-start | bytes 2752520 | tf_op jit(solution)/shard_map/ppermute | solution.py:49
  415.2 19.6 %collective-permute-start.21 = (bf16[448,2048]{1,0:T(8,128)(2,1)}, bf16[448,2048]{1,0:T(8,128)(2,1)}, u32[]{:S(2)}, u32[]{:S(2)}) collective-permute-start(bf16[448,2048]{1,0:T(8,128)(2,1)} %slice.308), channel_id=1, source_target_pairs={{0,1},{1,0},{2,3},{3,2},{4,5},{5,4},{6,7},{7,6},{8,9},{9,8},{10,11... | collective-permute-start | bytes 5505032 | tf_op jit(solution)/shard_map/ppermute | solution.py:49
  416.1 28.9 %all-to-all-start.3 = ((bf16[8,224,256]{2,1,0:T(8,128)(2,1)}), bf16[8,224,256]{2,1,0:T(8,128)(2,1)S(1)}, u32[]{:S(2)}, u32[]{:S(2)}) async-start(bf16[8,224,256]{2,1,0:T(8,128)(2,1)} %bitcast.451), calls=%async_computation.3 | async-start | bytes 1835008 | tf_op jit(solution)/shard_map/all_to_all | solution.py:876
  438.8 27.4 %collective-permute-start.22 = (bf16[224,2048]{1,0:T(8,128)(2,1)}, bf16[224,2048]{1,0:T(8,128)(2,1)}, u32[]{:S(2)}, u32[]{:S(2)}) collective-permute-start(bf16[224,2048]{1,0:T(8,128)(2,1)} %slice.502), channel_id=1, source_target_pairs={{0,2},{1,3},{2,0},{3,1},{4,6},{5,7},{6,4},{7,5},{8,10},{9,11},{10,... | collective-permute-start | bytes 2752520 | tf_op jit(solution)/shard_map/ppermute | solution.py:49
  469.2 28.2 %collective-permute-start.24 = (f32[2048]{0:T(1024)S(1)}, f32[2048]{0:T(1024)S(1)}, u32[]{:S(2)}, u32[]{:S(2)}) collective-permute-start(f32[2048]{0:T(1024)S(1)} %get-tuple-element.304), channel_id=1, source_target_pairs={{0,1},{1,0},{2,3},{3,2},{4,5},{5,4},{6,7},{7,6},{8,9},{9,8},{10,11... | collective-permute-start | bytes 24584 | tf_op jit(solution)/shard_map/ppermute | solution.py:49
  504.3 23.6 %collective-permute-start.25 = (bf16[224,2048]{1,0:T(8,128)(2,1)}, bf16[224,2048]{1,0:T(8,128)(2,1)}, u32[]{:S(2)}, u32[]{:S(2)}) collective-permute-start(bf16[224,2048]{1,0:T(8,128)(2,1)} %get-tuple-element.163), channel_id=1, source_target_pairs={{0,2},{1,3},{8,10},{9,11},{16,18},{17,19},{24,26},{25,27}} | collective-permute-start | bytes 2752520 | tf_op jit(solution)/shard_map/ppermute | solution.py:529
  508.9 18.9 %collective-permute-start.26 = (bf16[224,2048]{1,0:T(8,128)(2,1)}, bf16[224,2048]{1,0:T(8,128)(2,1)}, u32[]{:S(2)}, u32[]{:S(2)}) collective-permute-start(bf16[224,2048]{1,0:T(8,128)(2,1)} %get-tuple-element.164), channel_id=1, source_target_pairs={{6,4},{7,5},{14,12},{15,13},{22,20},{23,21},{30,28},{31,29}} | collective-permute-start | bytes 2752520 | tf_op jit(solution)/shard_map/ppermute | solution.py:529
  555.1 24.9 %collective-permute-start.28 = (bf16[224,2048]{1,0:T(8,128)(2,1)}, bf16[224,2048]{1,0:T(8,128)(2,1)}, u32[]{:S(2)}, u32[]{:S(2)}) collective-permute-start(bf16[224,2048]{1,0:T(8,128)(2,1)} %get-tuple-element.174), channel_id=1, source_target_pairs={{0,2},{1,3},{2,4},{3,5},{8,10},{9,11},{10,12},{11,13},{16,18},{17,... | collective-permute-start | bytes 2752520 | tf_op jit(solution)/shard_map/ppermute | solution.py:529
  560.4 19.6 %collective-permute-start.29 = (bf16[224,2048]{1,0:T(8,128)(2,1)}, bf16[224,2048]{1,0:T(8,128)(2,1)}, u32[]{:S(2)}, u32[]{:S(2)}) collective-permute-start(bf16[224,2048]{1,0:T(8,128)(2,1)} %get-tuple-element.175), channel_id=1, source_target_pairs={{4,2},{5,3},{6,4},{7,5},{12,10},{13,11},{14,12},{15,13},{20,18},{2... | collective-permute-start | bytes 2752520 | tf_op jit(solution)/shard_map/ppermute | solution.py:529
  615.0 20.9 %collective-permute-start.40 = (bf16[224,2048]{1,0:T(8,128)(2,1)S(1)}, bf16[224,2048]{1,0:T(8,128)(2,1)S(1)}, u32[]{:S(2)}, u32[]{:S(2)}) collective-permute-start(bf16[224,2048]{1,0:T(8,128)(2,1)S(1)} %get-tuple-element.192), channel_id=1, source_target_pairs={{0,2},{1,3},{2,4},{3,5},{4,6},{5,7},{8,10},{9,11},{10,12},{11,13},... | collective-permute-start | bytes 2752520 | tf_op jit(solution)/shard_map/ppermute | solution.py:529
  618.7 21.4 %collective-permute-start.41 = (bf16[224,2048]{1,0:T(8,128)(2,1)S(1)}, bf16[224,2048]{1,0:T(8,128)(2,1)S(1)}, u32[]{:S(2)}, u32[]{:S(2)}) collective-permute-start(bf16[224,2048]{1,0:T(8,128)(2,1)S(1)} %get-tuple-element.193), channel_id=1, source_target_pairs={{2,0},{3,1},{4,2},{5,3},{6,4},{7,5},{10,8},{11,9},{12,10},{13,11},... | collective-permute-start | bytes 2752520 | tf_op jit(solution)/shard_map/ppermute | solution.py:529
  (138 other events, 1528.2 us)
Sparse Core Ops, SparseCore 0:
  11.5 98.3 all-gather.2
  200.8 74.8 all-gather.4

commit v4 on v3

--- a/solution.py
+++ b/solution.py
@@ -349,7 +349,18 @@
     )(q, k, v, triple, cosine, sine, begin, grad_att, mixed_t, lse)
 
 
-def feed_kernel(gu_ref, down_ref, h_ref, d_ref, acts_out, g_out, gm_out):
+def feed_kernel(
+    gu_ref, down_ref, h_pair, h_other, d_pair, d_other, acts_out, g_out, gm_out, h_ref, d_ref
+):
+    half = h_pair.shape[0]
+
+    @pl.when((pl.program_id(0) == 0) & (pl.program_id(1) == 0))
+    def _():
+        h_ref[:half] = h_pair[...]
+        h_ref[half:] = h_other[...]
+        d_ref[:half] = d_pair[...]
+        d_ref[half:] = d_other[...]
+
     h = h_ref[...]
     gate = dot(gu_ref[0, 0], h, NT)
     upward = dot(gu_ref[0, 1], h, NT)
@@ -366,31 +377,38 @@
 
 
 def feed_forward(gu, down, h, d, mates):
-    rows, width = h.shape
+    rows, width = 2 * h[0].shape[0], h[0].shape[1]
     hidden = down.shape[0] // mates
     unit = hidden // max(1, hidden // 352)
     steps = hidden // unit
     flat = lambda k, j: (k * steps + j, 0)
     deep = lambda k, j: (k, 0, j, 0)
     whole = lambda k, j: (0, 0)
-    acts, g, gm = pl.pallas_call(
+    once = pl.BlockSpec((rows // 2, width), whole, pipeline_mode=pl.Buffered(1))
+    acts, g, gm, h_all, d_all = pl.pallas_call(
         feed_kernel,
         grid=(mates, steps),
         in_specs=[
             pl.BlockSpec((1, 2, unit, width), deep),
             pl.BlockSpec((unit, width), flat),
-            pl.BlockSpec((rows, width), whole),
-            pl.BlockSpec((rows, width), whole),
+            once,
+            once,
+            once,
+            once,
         ],
         out_specs=[
             pl.BlockSpec((unit, rows), flat),
             pl.BlockSpec((1, 2, unit, rows), deep),
             pl.BlockSpec((1, 2, unit, 1), deep),
+            pl.BlockSpec((rows, width), whole),
+            pl.BlockSpec((rows, width), whole),
         ],
         out_shape=[
             jax.ShapeDtypeStruct((mates * hidden, rows), bf16),
             jax.ShapeDtypeStruct((mates, 2, hidden, rows), bf16),
             jax.ShapeDtypeStruct((mates, 2, hidden, 1), f32),
+            jax.ShapeDtypeStruct((rows, width), bf16),
+            jax.ShapeDtypeStruct((rows, width), bf16),
         ],
         compiler_params=pltpu.CompilerParams(vmem_limit_bytes=58 * 2**20),
         cost_estimate=pl.CostEstimate(
@@ -399,8 +417,8 @@
             transcendentals=0,
         ),
         name="feed_forward",
-    )(gu.reshape(mates, 2, hidden, width), down, h, d)
-    return acts, g.reshape(2 * mates * hidden, rows), gm
+    )(gu.reshape(mates, 2, hidden, width), down, *h, *d)
+    return acts, g.reshape(2 * mates * hidden, rows), gm, h_all, d_all
 
 
 def back_kernel(
@@ -509,11 +527,6 @@
     return inverse * (scaled - unit * jnp.mean(scaled * unit, axis=-1, keepdims=True))
 
 
-def quad_gather(block):
-    pair = jnp.concatenate([block, swap(block, "blk", 2)], axis=0)
-    return jnp.concatenate([pair, swap(pair, "blk", 1)], axis=0)
-
-
 def quad_halve(parts):
     half = parts.shape[0] // 2
     return parts[:half].astype(f32) + swap(parts[half:], "blk", 1).astype(f32)
@@ -840,7 +853,7 @@
     xa_out = dot(a_out_low, attended_late, NT).astype(bf16)
     up_states = [dp_last(dp_steps(after(state, h_two), 1, -1)) for state in up_states]
     d_final_pair = after(d_final_pair, h_two)
-    d_final_all = jnp.concatenate([d_final_pair, swap(d_final_pair, "blk", 1)], axis=0)
+    d_final_parts = (d_final_pair, swap(d_final_pair, "blk", 1))
     for k_ in range(1, mates):
         gu = dp_lay(gate_states[k_ - 1], gu, (k_, 0))
         gu = dp_lay(up_states[k_ - 1], gu, (k_, 1))
@@ -849,8 +862,11 @@
     norms_out = norms[:, :wide].reshape(-1)
     norms_down = norms[:, wide + 2 * hidden : 2 * wide + 2 * hidden].reshape(-1)
 
-    h_two_all = after(quad_gather(h_two), xa_out, gu, down_rows)
-    acts, g_gu, gm_gu = feed_forward(gu, down_rows, h_two_all, d_final_all, mates)
+    h_two_pair = jnp.concatenate([h_two, swap(h_two, "blk", 2)], axis=0)
+    h_two_parts = after((h_two_pair, swap(h_two_pair, "blk", 1)), xa_out, gu, down_rows)
+    acts, g_gu, gm_gu, h_two_all, d_final_all = feed_forward(
+        gu, down_rows, h_two_parts, d_final_parts, mates
+    )
     dh_parts = dot(g_gu, gu, TN).astype(bf16)
     dh_half = quad_halve(dh_parts)
     dh_two = quad_finish(dh_half)

time: 668 us -> 664 us (level)
    unnamed x275 -> x267, local copies, waits for them, and re-layouts: 35.9 us -> 34 us
  transfers between devices with their start and end apart: 52 -> 52, of which waited for: 22 -> 24; matrix products, arithmetic and copies ran while one was open for 27% -> 26% of each run, Pallas kernels for 16% -> 16%
where the time goes in v4:
time: 664 us; the launch traced here: 654 us
  waiting for transfers between devices  174 us (26%)
  Pallas kernels  132 us (20%)
  matrix products  94.2 us (14%)
  local copies, waits for them, and re-layouts  82.2 us (12%)
  other arithmetic  79.8 us (12%)
  starting transfers between devices  75.1 us (11%)
  between operations  16.7 us (3%)
    dot_general x21, matrix products, dot(): return lax.dot_general(a, b, dims, preferred_element_type=f32)  94.2 us
    ppermute x40, waiting for transfers between devices, swap(): lax.ppermute(array, axis, [(i, i ^ bit) for i in range(lax.axis_size(axis...  91.5 us
    all_to_all x2, waiting for transfers between devices, spread_rows(): got = lax.all_to_all(chunks, 'blk', 0, 0, tiled=True)  54.1 us
    ppermute x40, starting transfers between devices, swap(): lax.ppermute(array, axis, [(i, i ^ bit) for i in range(lax.axis_size(axis...  37.2 us
    unnamed x267, local copies, waits for them, and re-layouts  34 us
    pallas_call x1, Pallas kernels, feed_forward(): pl.pallas_call(feed_kernel, grid=(mates, steps), in_specs=[pl.BlockSpec((...  29.5 us
    ppermute x6, waiting for transfers between devices, step_chips(): return lax.ppermute(array, 'blk', pairs)  28.7 us
    pallas_call x4, Pallas kernels, dp_lay(): pl.pallas_call(lay_kernel, grid_spec=pltpu.PrefetchScalarGridSpec(num_sca...  20.5 us
  transfers between devices with their start and end apart: 52, of which 24 were waited for; matrix products, arithmetic and copies ran while one was open for 26% of the time, Pallas kernels for 16%

profile of v4, /device:TPU:0, one launch (start us, length us, event | category | flops | bytes accessed | tf_op | source)
XLA Modules:
  0.0 654.5 jit_solution(11022276204990850591)
XLA Ops:
  18.4 7.4 %merge.5 = (bf16[5632,256]{1,0:T(8,128)(2,1)S(1)}, f32[1,256]{1,0:T(1,128)S(1)}) custom-call(bf16[1,5632,256]{2,1,0:T(8,128)(2,1)} %bitcast.453, bf16[1,96,5632]{2,1,0:T(8,128)(2,1)S(1)} %fusion.46.a_ref, bf16[1,96,256]{2,1,0:T(8,128)(2,1)S(1)} %constant_dynamic-update-slice_fusion.40.b_ref, f32[1,256]{1,0:T(1,128)S(1)} %bitcast.420), custom_call_target="tpu_custom_call" | custom-call | flops 276824064 | bytes 5767168 | tf_op jit(solution)/shard_map/merge/pallas_call | solution.py:110
  27.6 8.0 %merge.4 = (bf16[2048,768]{1,0:T(8,128)(2,1)S(1)}, f32[1,768]{1,0:T(1,128)S(1)}) custom-call(bf16[3,2048,256]{2,1,0:T(8,128)(2,1)} %w_ref.1, bf16[3,96,2048]{2,1,0:T(8,128)(2,1)S(1)} %fusion.44.a_ref, bf16[3,96,256]{2,1,0:T(8,128)(2,1)S(1)} %constant_dynamic-update-slice_fusion.29.b_ref, f32[1,768]{1,0:T(1,128)S(1)} %reshape.496.m_ref), custom_call_target="tpu_custom_call" | custom-call | flops 301989888 | bytes 6291456 | tf_op jit(solution)/shard_map/merge/pallas_call | solution.py:110
  38.9 7.4 %merge_rows.1 = (bf16[2,2,704,2048]{3,2,1,0:T(8,128)(2,1)}, f32[2,704,1]{2,1,0:T(8,128)}) custom-call(bf16[2,704,2048]{2,1,0:T(8,128)(2,1)} %bitcast.449, bf16[2,96,2048]{2,1,0:T(8,128)(2,1)} %copy-done.59, bf16[2,96,704]{2,1,0:T(8,128)(2,1)} %copy-done.66, f32[2,704,1]{2,1,0:T(8,128)} %copy.76.m_ref), custom_call_target="tpu_custom_call" | custom-call | flops 553648128 | bytes 11534336 | tf_op jit(solution)/shard_map/merge_rows/pallas_call | solution.py:145
  51.4 6.4 all-to-all-start
  62.3 45.4 %all-to-all-done = bf16[8,256,256]{2,1,0:T(8,128)(2,1)S(1)} async-done(((bf16[8,256,256]{2,1,0:T(8,128)(2,1)}), bf16[8,256,256]{2,1,0:T(8,128)(2,1)S(1)}, u32[]{:S(2)}, u32[]{:S(2)}) %all-to-all-start) | async-done | bytes 1048608 | tf_op jit(solution)/shard_map/all_to_all | solution.py:757
  128.5 7.6 %collective-permute-done = bf16[1,128,2048]{2,1,0:T(8,128)(2,1)} collective-permute-done((bf16[1,128,2048]{2,1,0:T(8,128)(2,1)}, bf16[1,128,2048]{2,1,0:T(8,128)(2,1)}, u32[]{:S(2)}, u32[]{:S(2)}) %collective-permute-start) | collective-permute-done | bytes 524320 | tf_op jit(solution)/shard_map/ppermute | solution.py:49
  139.7 8.7 %all-to-all-done.1 = bf16[8,368,256]{2,1,0:T(8,128)(2,1)} async-done(((bf16[8,368,256]{2,1,0:T(8,128)(2,1)}), bf16[8,368,256]{2,1,0:T(8,128)(2,1)}, u32[]{:S(2)}, u32[]{:S(2)}) %all-to-all-start.1) | async-done | bytes 1507360 | tf_op jit(solution)/shard_map/all_to_all | solution.py:757
  154.1 10.5 %fusion.113.pre = f32[1792,768]{1,0:T(8,128)} fusion(bf16[1792,2048]{1,0:T(8,128)(2,1)} %all-gather.3.cloned.1.call-done.h_ref, bf16[2048,768]{1,0:T(8,128)(2,1)} %copy-done.2), kind=kOutput, calls=%fused_computation.423 | convolution fusion | flops 5637144576 | bytes 15990784 | tf_op jit(solution)/shard_map/dot_general | solution.py:32
  164.6 20.1 %attend.1 = (bf16[1792,256]{1,0:T(8,128)(2,1)S(1)}, bf16[1792,256]{1,0:T(8,128)(2,1)S(1)}, bf16[1792,256]{1,0:T(8,128)(2,1)S(1)}, bf16[1792,256]{1,0:T(8,128)(2,...) custom-call(f32[1792,768]{1,0:T(8,128)} %fusion.113.pre, f32[1792,128]{1,0:T(8,128)S(1)} %pad_maximum_fusion.6.cosine, ...), custom_call_target="tpu_custom_call" | custom-call | flops 1644167168 | bytes 13762560 | tf_op jit(solution)/shard_map/attend/pallas_call | solution.py:282
  205.2 5.4 fusion.7
  211.6 5.4 lay.4.into
  224.3 5.5 lay.5
  229.8 23.5 %collective-permute-done.8 = bf16[176,2048]{1,0:T(8,128)(2,1)} collective-permute-done((bf16[176,2048]{1,0:T(8,128)(2,1)}, bf16[176,2048]{1,0:T(8,128)(2,1)}, u32[]{:S(2)}, u32[]{:S(2)}) %collective-permute-start.8) | collective-permute-done | bytes 720928 | tf_op jit(solution)/shard_map/ppermute | solution.py:49
  258.1 5.6 fusion.30
  267.1 5.9 collective-permute-done.10
  286.0 15.1 %collective-permute-done.16 = bf16[224,2048]{1,0:T(8,128)(2,1)S(1)} collective-permute-done((bf16[224,2048]{1,0:T(8,128)(2,1)S(1)}, bf16[224,2048]{1,0:T(8,128)(2,1)S(1)}, u32[]{:S(2)}, u32[]{:S(2)}) %collective-permute-start.16) | collective-permute-done | bytes 917536 | tf_op jit(solution)/shard_map/ppermute | solution.py:49
  305.4 4.8 lay.6.into
  317.1 4.8 lay.7
  321.9 29.5 %feed_forward.1 = (bf16[1408,896]{1,0:T(8,128)(2,1)}, bf16[2,2,704,896]{3,2,1,0:T(8,128)(2,1)}, f32[2,2,704,1]{3,2,1,0:T(8,128)}, bf16[896,2048]{1,0:T(8,128)(2,1)}, bf16[896,2048]{1,0:T(8,128)(2,1)}) custom-call(bf16[2,2,704,2048]{3,2,1,0:T(8,128)(2,1)} %bitcast.425, bf16[1408,2048]{1,0:T(8,128)(2,1)} %all-gather.5.cloned.1.call-done.down_ref, ...), custom_call_target="tpu_custom_call" | custom-call | flops 15502147584 | bytes 24641536 | tf_op jit(solution)/shard_map/feed_forward/pallas_call | solution.py:388
  351.4 15.5 %convolution_convert_fusion = bf16[896,2048]{1,0:T(8,128)(2,1)S(1)} fusion(bf16[2816,896]{1,0:T(8,128)(2,1)} %bitcast.441, bf16[2816,2048]{1,0:T(8,128)(2,1)} %bitcast.426), kind=kOutput, calls=%fused_computation.3 | convolution fusion | flops 10336600064 | bytes 20250624 | tf_op jit(solution)/shard_map/dot_general | solution.py:32
  380.4 8.9 %convolution_convert_fusion.1 = bf16[896,2048]{1,0:T(8,128)(2,1)S(1)} fusion(bf16[1408,896]{1,0:T(8,128)(2,1)S(1)} %copy-done.37, bf16[1408,2048]{1,0:T(8,128)(2,1)} %all-gather.5.cloned.1.call-done.down_ref), kind=kOutput, calls=%fused_computation.4 | convolution fusion | flops 5169217536 | bytes 11960320 | tf_op jit(solution)/shard_map/dot_general | solution.py:32
  395.8 5.9 collective-permute-done.20
  418.6 7.0 %fusion.2 = f32[32,2816]{1,0:T(8,128)} fusion(bf16[2816,896]{1,0:T(8,128)(2,1)} %bitcast.442, bf16[896,2048]{1,0:T(8,128)(2,1)} %get-tuple-element.185, bf16[32,2048]{1,0:T(8,128)(2,1)S(1)} %bitcast.470, f32[32,2816]{1,0:T(8,128)S(1)} %convolution_bitcast_fusion, f32[2816]{0:T(1024)S(1)} %get-tuple-element.300, f32[2816]{0:T(1024)S(1)} %get-tuple-element.301, ...), kind=kOutput, calls=%fused_computation.8 | convolution fusion | flops 280662016 | bytes 9616416 | tf_op jit(solution)/shard_map/dot_general | solution.py:32
  445.3 17.2 %attend_back.1 = (bf16[1792,768]{1,0:T(8,128)(2,1)}, f32[8,768]{1,0:T(8,128)S(1)}) custom-call(bf16[1792,256]{1,0:T(8,128)(2,1)S(1)} %copy-done.7, bf16[1792,256]{1,0:T(8,128)(2,1)S(1)} %copy-done.9, bf16[1792,256]{1,0:T(8,128)(2,1)S(1)} %copy-done.11, f32[1792,768]{1,0:T(8,128)} %fusion.113.pre, f32[1792,128]{1,0:T(8,128)S(1)} %pad_maximum_fusion.6.cosine, ...), custom_call_target="tpu_custom_call" | custom-call | flops 4110417920 | bytes 18350080 | tf_op jit(solution)/shard_map/attend_back/pallas_call | solution.py:319
  465.6 19.6 %back_qkv.1 = (bf16[4,224,2048]{2,1,0:T(8,128)(2,1)}, bf16[4,224,2048]{2,1,0:T(8,128)(2,1)}, f32[48,2048]{1,0:T(8,128)}, f32[48,768]{1,0:T(8,128)}, f32[1,2048]{1,0:T(1,128)}, /*index=5*/f32[1,768]{1,0:T(1,128)}) custom-call(s32[1]{0:T(128)} %bitcast.130.core, bf16[1792,768]{1,0:T(8,128)(2,1)} %get-tuple-element.162.g_ref, ...), custom_call_target="tpu_custom_call" | custom-call | flops 8455716864 | bytes 29360128 | tf_op jit(solution)/shard_map/back_qkv/pallas_call | solution.py:477
  493.8 5.1 add_convert_fusion
  510.0 6.5 constant_dynamic-update-slice_fusion.69
  524.4 6.5 fusion.114
  551.7 5.3 collective-permute-start.28
  563.9 12.6 %collective-permute-done.28 = bf16[224,2048]{1,0:T(8,128)(2,1)} collective-permute-done((bf16[224,2048]{1,0:T(8,128)(2,1)}, bf16[224,2048]{1,0:T(8,128)(2,1)}, u32[]{:S(2)}, u32[]{:S(2)}) %collective-permute-start.28) | collective-permute-done | bytes 917536 | tf_op jit(solution)/shard_map/ppermute | solution.py:542
  600.2 4.7 collective-permute-done.38
  621.7 10.7 %collective-permute-done.40 = bf16[224,2048]{1,0:T(8,128)(2,1)S(1)} collective-permute-done((bf16[224,2048]{1,0:T(8,128)(2,1)S(1)}, bf16[224,2048]{1,0:T(8,128)(2,1)S(1)}, u32[]{:S(2)}, u32[]{:S(2)}) %collective-permute-start.40) | collective-permute-done | bytes 917536 | tf_op jit(solution)/shard_map/ppermute | solution.py:542
  (619 shorter events, 285.2 us)
Async XLA Ops:
  7.3 143.9 %all-gather.3.cloned.1.call-start = ((), (), s32[]{:S(2)}) async-start(), calls=%async_computation.4 | async-start | bytes 8257536 | tf_op jit(solution)/shard_map/all_gather | solution.py:716
  51.4 56.3 %all-to-all-start = ((bf16[8,256,256]{2,1,0:T(8,128)(2,1)}), bf16[8,256,256]{2,1,0:T(8,128)(2,1)S(1)}, u32[]{:S(2)}, u32[]{:S(2)}) async-start(bf16[8,256,256]{2,1,0:T(8,128)(2,1)} %bitcast.29), calls=%async_computation | async-start | bytes 2097152 | tf_op jit(solution)/shard_map/all_to_all | solution.py:757
  107.6 40.7 %all-to-all-start.1 = ((bf16[8,368,256]{2,1,0:T(8,128)(2,1)}), bf16[8,368,256]{2,1,0:T(8,128)(2,1)}, u32[]{:S(2)}, u32[]{:S(2)}) async-start(bf16[8,368,256]{2,1,0:T(8,128)(2,1)} %pad_maximum_fusion.2), calls=%async_computation.1 | async-start | bytes 3014656 | tf_op jit(solution)/shard_map/all_to_all | solution.py:757
  111.9 209.9 %all-gather.5.cloned.1.call-start = ((), (), s32[]{:S(2)}) async-start(), calls=%async_computation.5 | async-start | bytes 7208960 | tf_op jit(solution)/shard_map/all_gather | solution.py:808
  151.1 38.1 %collective-permute-start.4 = (bf16[176,2048]{1,0:T(8,128)(2,1)}, bf16[176,2048]{1,0:T(8,128)(2,1)}, u32[]{:S(2)}, u32[]{:S(2)}) collective-permute-start(bf16[176,2048]{1,0:T(8,128)(2,1)} %get-tuple-element.123), channel_id=1, source_target_pairs={{0,4},{1,5},{2,6},{3,7},{4,0},{5,1},{6,2},{7,3},{8,12},{9,13},{10,... | collective-permute-start | bytes 2162696 | tf_op jit(solution)/shard_map/ppermute | solution.py:49
  151.1 34.8 %collective-permute-start.2 = (bf16[2,128,2048]{2,1,0:T(8,128)(2,1)}, bf16[2,128,2048]{2,1,0:T(8,128)(2,1)S(1)}, u32[]{:S(2)}, u32[]{:S(2)}) collective-permute-start(bf16[2,128,2048]{2,1,0:T(8,128)(2,1)} %pad_maximum_fusion.4), channel_id=1, source_target_pairs={{0,16},{8,24},{16,0},{24,8},{1,17},{9,25},{17,1},{25,9},{2,18},{10... | collective-permute-start | bytes 3145736 | tf_op jit(solution)/shard_map/ppermute | solution.py:49
  152.6 35.5 %collective-permute-start.3 = (bf16[2,128,2048]{2,1,0:T(8,128)(2,1)S(1)}, bf16[2,128,2048]{2,1,0:T(8,128)(2,1)S(1)}, u32[]{:S(2)}, u32[]{:S(2)}) collective-permute-start(bf16[2,128,2048]{2,1,0:T(8,128)(2,1)S(1)} %pad_maximum_fusion.5), channel_id=1, source_target_pairs={{0,8},{8,0},{16,24},{24,16},{1,9},{9,1},{17,25},{25,17},{2,10},{10... | collective-permute-start | bytes 3145736 | tf_op jit(solution)/shard_map/ppermute | solution.py:49
  189.2 35.1 %collective-permute-start.5 = (bf16[8,128,2048]{2,1,0:T(8,128)(2,1)}, bf16[8,128,2048]{2,1,0:T(8,128)(2,1)}, u32[]{:S(2)}, u32[]{:S(2)}) collective-permute-start(bf16[8,128,2048]{2,1,0:T(8,128)(2,1)} %constant_dynamic-update-slice_fusion.46.one.two), channel_id=1, source_target_pairs={{0,1},{1,0},{2,3},{3,2},{4,5},{5,4},{6,7},{7,6},{8,9},{9,8},{10,11... | collective-permute-start | bytes 12582920 | tf_op jit(solution)/shard_map/ppermute | solution.py:49
  194.0 59.3 %all-to-all-start.2 = ((bf16[8,224,256]{2,1,0:T(8,128)(2,1)}), bf16[8,224,256]{2,1,0:T(8,128)(2,1)S(1)}, u32[]{:S(2)}, u32[]{:S(2)}) async-start(bf16[8,224,256]{2,1,0:T(8,128)(2,1)} %bitcast.37), calls=%async_computation.2 | async-start | bytes 1835008 | tf_op jit(solution)/shard_map/all_to_all | solution.py:822
  201.3 18.9 %collective-permute-start.7 = (bf16[1,88,2048]{2,1,0:T(8,128)(2,1)}, bf16[1,88,2048]{2,1,0:T(8,128)(2,1)}, u32[]{:S(2)}, u32[]{:S(2)}) collective-permute-start(bf16[1,88,2048]{2,1,0:T(8,128)(2,1)} %get-tuple-element.271), channel_id=1, source_target_pairs={{0,16},{8,24},{16,0},{24,8},{1,17},{9,25},{17,1},{25,9},{2,18},{10... | collective-permute-start | bytes 1081352 | tf_op jit(solution)/shard_map/ppermute | solution.py:49
  201.8 20.5 %collective-permute-start.6 = (bf16[1,88,2048]{2,1,0:T(8,128)(2,1)}, bf16[1,88,2048]{2,1,0:T(8,128)(2,1)}, u32[]{:S(2)}, u32[]{:S(2)}) collective-permute-start(bf16[1,88,2048]{2,1,0:T(8,128)(2,1)} %get-tuple-element.272), channel_id=1, source_target_pairs={{0,8},{8,0},{16,24},{24,16},{1,9},{9,1},{17,25},{25,17},{2,10},{10... | collective-permute-start | bytes 1081352 | tf_op jit(solution)/shard_map/ppermute | solution.py:49
  202.2 51.0 %collective-permute-start.8 = (bf16[176,2048]{1,0:T(8,128)(2,1)}, bf16[176,2048]{1,0:T(8,128)(2,1)}, u32[]{:S(2)}, u32[]{:S(2)}) collective-permute-start(bf16[176,2048]{1,0:T(8,128)(2,1)} %get-tuple-element.129), channel_id=1, source_target_pairs={{0,4},{1,5},{2,6},{3,7},{4,0},{5,1},{6,2},{7,3},{8,12},{9,13},{10,... | collective-permute-start | bytes 2162696 | tf_op jit(solution)/shard_map/ppermute | solution.py:49
  258.1 21.5 %collective-permute-start.11 = (bf16[224,2048]{1,0:T(8,128)(2,1)}, bf16[224,2048]{1,0:T(8,128)(2,1)S(1)}, u32[]{:S(2)}, u32[]{:S(2)}) collective-permute-start(bf16[224,2048]{1,0:T(8,128)(2,1)} %fusion.27), channel_id=1, source_target_pairs={{0,2},{1,3},{2,0},{3,1},{4,6},{5,7},{6,4},{7,5},{8,10},{9,11},{10,... | collective-permute-start | bytes 2752520 | tf_op jit(solution)/shard_map/ppermute | solution.py:49
  280.7 20.4 %collective-permute-start.16 = (bf16[224,2048]{1,0:T(8,128)(2,1)S(1)}, bf16[224,2048]{1,0:T(8,128)(2,1)S(1)}, u32[]{:S(2)}, u32[]{:S(2)}) collective-permute-start(bf16[224,2048]{1,0:T(8,128)(2,1)S(1)} %get-tuple-element.134), channel_id=1, source_target_pairs={{0,2},{1,3},{2,0},{3,1},{4,6},{5,7},{6,4},{7,5},{8,10},{9,11},{10,... | collective-permute-start | bytes 2752520 | tf_op jit(solution)/shard_map/ppermute | solution.py:49
  281.0 21.2 %collective-permute-start.14 = (bf16[2,88,2048]{2,1,0:T(8,128)(2,1)S(1)}, bf16[2,88,2048]{2,1,0:T(8,128)(2,1)S(1)}, u32[]{:S(2)}, u32[]{:S(2)}) collective-permute-start(bf16[2,88,2048]{2,1,0:T(8,128)(2,1)S(1)} %copy-done.52), channel_id=1, source_target_pairs={{0,16},{8,24},{16,0},{24,8},{1,17},{9,25},{17,1},{25,9},{2,18},{10... | collective-permute-start | bytes 2162696 | tf_op jit(solution)/shard_map/ppermute | solution.py:49
  282.5 21.1 %collective-permute-start.15 = (bf16[2,88,2048]{2,1,0:T(8,128)(2,1)S(1)}, bf16[2,88,2048]{2,1,0:T(8,128)(2,1)S(1)}, u32[]{:S(2)}, u32[]{:S(2)}) collective-permute-start(bf16[2,88,2048]{2,1,0:T(8,128)(2,1)S(1)} %copy-done.51), channel_id=1, source_target_pairs={{0,8},{8,0},{16,24},{24,16},{1,9},{9,1},{17,25},{25,17},{2,10},{10... | collective-permute-start | bytes 2162696 | tf_op jit(solution)/shard_map/ppermute | solution.py:49
  284.0 28.7 %collective-permute-start.12 = (bf16[2,88,2048]{2,1,0:T(8,128)(2,1)}, bf16[2,88,2048]{2,1,0:T(8,128)(2,1)}, u32[]{:S(2)}, u32[]{:S(2)}) collective-permute-start(bf16[2,88,2048]{2,1,0:T(8,128)(2,1)} %pad_maximum_fusion.10), channel_id=1, source_target_pairs={{0,16},{8,24},{16,0},{24,8},{1,17},{9,25},{17,1},{25,9},{2,18},{10... | collective-permute-start | bytes 2162696 | tf_op jit(solution)/shard_map/ppermute | solution.py:49
  284.5 29.5 %collective-permute-start.13 = (bf16[2,88,2048]{2,1,0:T(8,128)(2,1)}, bf16[2,88,2048]{2,1,0:T(8,128)(2,1)}, u32[]{:S(2)}, u32[]{:S(2)}) collective-permute-start(bf16[2,88,2048]{2,1,0:T(8,128)(2,1)} %pad_maximum_fusion.11), channel_id=1, source_target_pairs={{0,8},{8,0},{16,24},{24,16},{1,9},{9,1},{17,25},{25,17},{2,10},{10... | collective-permute-start | bytes 2162696 | tf_op jit(solution)/shard_map/ppermute | solution.py:49
  301.1 20.8 %collective-permute-start.18 = (bf16[448,2048]{1,0:T(8,128)(2,1)}, bf16[448,2048]{1,0:T(8,128)(2,1)}, u32[]{:S(2)}, u32[]{:S(2)}) collective-permute-start(bf16[448,2048]{1,0:T(8,128)(2,1)} %constant_dynamic-update-slice_fusion.50.d_pair), channel_id=1, source_target_pairs={{0,1},{1,0},{2,3},{3,2},{4,5},{5,4},{6,7},{7,6},{8,9},{9,8},{10,11... | collective-permute-start | bytes 5505032 | tf_op jit(solution)/shard_map/ppermute | solution.py:49
  302.1 19.7 %collective-permute-start.17 = (bf16[448,2048]{1,0:T(8,128)(2,1)}, bf16[448,2048]{1,0:T(8,128)(2,1)}, u32[]{:S(2)}, u32[]{:S(2)}) collective-permute-start(bf16[448,2048]{1,0:T(8,128)(2,1)} %constant_dynamic-update-slice_fusion.52.h_pair), channel_id=1, source_target_pairs={{0,1},{1,0},{2,3},{3,2},{4,5},{5,4},{6,7},{7,6},{8,9},{9,8},{10,11... | collective-permute-start | bytes 5505032 | tf_op jit(solution)/shard_map/ppermute | solution.py:49
  378.9 22.8 %collective-permute-start.20 = (bf16[224,2048]{1,0:T(8,128)(2,1)S(1)}, bf16[224,2048]{1,0:T(8,128)(2,1)S(1)}, u32[]{:S(2)}, u32[]{:S(2)}) collective-permute-start(bf16[224,2048]{1,0:T(8,128)(2,1)S(1)} %slice.503), channel_id=1, source_target_pairs={{0,2},{1,3},{2,0},{3,1},{4,6},{5,7},{6,4},{7,5},{8,10},{9,11},{10,... | collective-permute-start | bytes 2752520 | tf_op jit(solution)/shard_map/ppermute | solution.py:49
  411.8 19.8 %collective-permute-start.21 = (bf16[448,2048]{1,0:T(8,128)(2,1)}, bf16[448,2048]{1,0:T(8,128)(2,1)}, u32[]{:S(2)}, u32[]{:S(2)}) collective-permute-start(bf16[448,2048]{1,0:T(8,128)(2,1)} %slice.308), channel_id=1, source_target_pairs={{0,1},{1,0},{2,3},{3,2},{4,5},{5,4},{6,7},{7,6},{8,9},{9,8},{10,11... | collective-permute-start | bytes 5505032 | tf_op jit(solution)/shard_map/ppermute | solution.py:49
  412.7 29.1 %all-to-all-start.3 = ((bf16[8,224,256]{2,1,0:T(8,128)(2,1)}), bf16[8,224,256]{2,1,0:T(8,128)(2,1)S(1)}, u32[]{:S(2)}, u32[]{:S(2)}) async-start(bf16[8,224,256]{2,1,0:T(8,128)(2,1)} %bitcast.451), calls=%async_computation.3 | async-start | bytes 1835008 | tf_op jit(solution)/shard_map/all_to_all | solution.py:892
  435.5 27.0 %collective-permute-start.22 = (bf16[224,2048]{1,0:T(8,128)(2,1)}, bf16[224,2048]{1,0:T(8,128)(2,1)}, u32[]{:S(2)}, u32[]{:S(2)}) collective-permute-start(bf16[224,2048]{1,0:T(8,128)(2,1)} %slice.502), channel_id=1, source_target_pairs={{0,2},{1,3},{2,0},{3,1},{4,6},{5,7},{6,4},{7,5},{8,10},{9,11},{10,... | collective-permute-start | bytes 2752520 | tf_op jit(solution)/shard_map/ppermute | solution.py:49
  465.4 28.4 %collective-permute-start.24 = (f32[2048]{0:T(1024)S(1)}, f32[2048]{0:T(1024)S(1)}, u32[]{:S(2)}, u32[]{:S(2)}) collective-permute-start(f32[2048]{0:T(1024)S(1)} %get-tuple-element.310), channel_id=1, source_target_pairs={{0,1},{1,0},{2,3},{3,2},{4,5},{5,4},{6,7},{7,6},{8,9},{9,8},{10,11... | collective-permute-start | bytes 24584 | tf_op jit(solution)/shard_map/ppermute | solution.py:49
  500.7 23.6 %collective-permute-start.25 = (bf16[224,2048]{1,0:T(8,128)(2,1)}, bf16[224,2048]{1,0:T(8,128)(2,1)}, u32[]{:S(2)}, u32[]{:S(2)}) collective-permute-start(bf16[224,2048]{1,0:T(8,128)(2,1)} %get-tuple-element.168), channel_id=1, source_target_pairs={{0,2},{1,3},{8,10},{9,11},{16,18},{17,19},{24,26},{25,27}} | collective-permute-start | bytes 2752520 | tf_op jit(solution)/shard_map/ppermute | solution.py:542
  505.4 18.9 %collective-permute-start.26 = (bf16[224,2048]{1,0:T(8,128)(2,1)}, bf16[224,2048]{1,0:T(8,128)(2,1)}, u32[]{:S(2)}, u32[]{:S(2)}) collective-permute-start(bf16[224,2048]{1,0:T(8,128)(2,1)} %get-tuple-element.169), channel_id=1, source_target_pairs={{6,4},{7,5},{14,12},{15,13},{22,20},{23,21},{30,28},{31,29}} | collective-permute-start | bytes 2752520 | tf_op jit(solution)/shard_map/ppermute | solution.py:542
  551.7 24.9 %collective-permute-start.28 = (bf16[224,2048]{1,0:T(8,128)(2,1)}, bf16[224,2048]{1,0:T(8,128)(2,1)}, u32[]{:S(2)}, u32[]{:S(2)}) collective-permute-start(bf16[224,2048]{1,0:T(8,128)(2,1)} %get-tuple-element.180), channel_id=1, source_target_pairs={{0,2},{1,3},{2,4},{3,5},{8,10},{9,11},{10,12},{11,13},{16,18},{17,... | collective-permute-start | bytes 2752520 | tf_op jit(solution)/shard_map/ppermute | solution.py:542
  557.0 19.6 %collective-permute-start.29 = (bf16[224,2048]{1,0:T(8,128)(2,1)}, bf16[224,2048]{1,0:T(8,128)(2,1)}, u32[]{:S(2)}, u32[]{:S(2)}) collective-permute-start(bf16[224,2048]{1,0:T(8,128)(2,1)} %get-tuple-element.181), channel_id=1, source_target_pairs={{4,2},{5,3},{6,4},{7,5},{12,10},{13,11},{14,12},{15,13},{20,18},{2... | collective-permute-start | bytes 2752520 | tf_op jit(solution)/shard_map/ppermute | solution.py:542
  611.5 20.9 %collective-permute-start.40 = (bf16[224,2048]{1,0:T(8,128)(2,1)S(1)}, bf16[224,2048]{1,0:T(8,128)(2,1)S(1)}, u32[]{:S(2)}, u32[]{:S(2)}) collective-permute-start(bf16[224,2048]{1,0:T(8,128)(2,1)S(1)} %get-tuple-element.198), channel_id=1, source_target_pairs={{0,2},{1,3},{2,4},{3,5},{4,6},{5,7},{8,10},{9,11},{10,12},{11,13},... | collective-permute-start | bytes 2752520 | tf_op jit(solution)/shard_map/ppermute | solution.py:542
  615.2 21.4 %collective-permute-start.41 = (bf16[224,2048]{1,0:T(8,128)(2,1)S(1)}, bf16[224,2048]{1,0:T(8,128)(2,1)S(1)}, u32[]{:S(2)}, u32[]{:S(2)}) collective-permute-start(bf16[224,2048]{1,0:T(8,128)(2,1)S(1)} %get-tuple-element.199), channel_id=1, source_target_pairs={{2,0},{3,1},{4,2},{5,3},{6,4},{7,5},{10,8},{11,9},{12,10},{13,11},... | collective-permute-start | bytes 2752520 | tf_op jit(solution)/shard_map/ppermute | solution.py:542
  621.5 18.0 %collective-permute-start.45 = (f32[16,22528]{1,0:T(8,128)S(1)}, f32[16,22528]{1,0:T(8,128)S(1)}, u32[]{:S(2)}, u32[]{:S(2)}) collective-permute-start(f32[16,22528]{1,0:T(8,128)S(1)} %constant_dynamic-update-slice_fusion.78), channel_id=1, source_target_pairs={{0,1},{1,0},{2,3},{3,2},{4,5},{5,4},{6,7},{7,6},{8,9},{9,8},{10,11... | collective-permute-start | bytes 4325384 | tf_op jit(solution)/shard_map/ppermute | solution.py:49
  (134 other events, 1608.0 us)
Sparse Core Ops, SparseCore 0:
  11.5 98.3 all-gather.2
  193.3 78.1 all-gather.4

commit v5 on v4

--- a/solution.py
+++ b/solution.py
@@ -847,7 +847,7 @@
     gate_states = [dp_last(dp_steps(state, 1, -1)) for state in gate_states]
     d_final_pair = jnp.concatenate([d_final_low, swap(d_final_low, "blk", 2)], axis=0)
     up_states = [dp_steps(dp_start(g), 0, 1) for g in up_parts]
-    h_two = after(h_two, up_states, d_final_pair)
+    h_two = after(h_two, up_states)
 
     attended_late = after(attended, h_two)
     xa_out = dot(a_out_low, attended_late, NT).astype(bf16)

time: 664 us -> 659 us (level)
    unnamed x267 -> x264, local copies, waits for them, and re-layouts: 34 us -> 31.5 us
  transfers between devices with their start and end apart: 52 -> 52, of which waited for: 24 -> 21; matrix products, arithmetic and copies ran while one was open for 26% -> 26% of each run, Pallas kernels for 16% -> 16%
where the time goes in v5:
time: 659 us; the launch traced here: 649 us
  waiting for transfers between devices  170 us (26%)
  Pallas kernels  132 us (20%)
  matrix products  93.8 us (14%)
  other arithmetic  83.2 us (13%)
  local copies, waits for them, and re-layouts  76.3 us (12%)
  starting transfers between devices  76 us (12%)
  between operations  16.8 us (3%)
    dot_general x21, matrix products, dot(): return lax.dot_general(a, b, dims, preferred_element_type=f32)  93.8 us
    ppermute x40, waiting for transfers between devices, swap(): lax.ppermute(array, axis, [(i, i ^ bit) for i in range(lax.axis_size(axis...  85.9 us
    all_to_all x2, waiting for transfers between devices, spread_rows(): got = lax.all_to_all(chunks, 'blk', 0, 0, tiled=True)  55.9 us
    ppermute x40, starting transfers between devices, swap(): lax.ppermute(array, axis, [(i, i ^ bit) for i in range(lax.axis_size(axis...  38.2 us
    unnamed x264, local copies, waits for them, and re-layouts  31.5 us
    pallas_call x1, Pallas kernels, feed_forward(): pl.pallas_call(feed_kernel, grid=(mates, steps), in_specs=[pl.BlockSpec((...  29.5 us
    ppermute x6, waiting for transfers between devices, step_chips(): return lax.ppermute(array, 'blk', pairs)  28.4 us
    pallas_call x4, Pallas kernels, dp_lay(): pl.pallas_call(lay_kernel, grid_spec=pltpu.PrefetchScalarGridSpec(num_sca...  20.5 us
  transfers between devices with their start and end apart: 52, of which 21 were waited for; matrix products, arithmetic and copies ran while one was open for 26% of the time, Pallas kernels for 16%

profile of v5, /device:TPU:0, one launch (start us, length us, event | category | flops | bytes accessed | tf_op | source)
XLA Modules:
  0.0 648.8 jit_solution(15807834604956766546)
XLA Ops:
  19.1 7.4 %merge.5 = (bf16[5632,256]{1,0:T(8,128)(2,1)S(1)}, f32[1,256]{1,0:T(1,128)S(1)}) custom-call(bf16[1,5632,256]{2,1,0:T(8,128)(2,1)} %bitcast.452, bf16[1,96,5632]{2,1,0:T(8,128)(2,1)S(1)} %fusion.46.a_ref, bf16[1,96,256]{2,1,0:T(8,128)(2,1)S(1)} %constant_dynamic-update-slice_fusion.40.b_ref, f32[1,256]{1,0:T(1,128)S(1)} %bitcast.420), custom_call_target="tpu_custom_call" | custom-call | flops 276824064 | bytes 5767168 | tf_op jit(solution)/shard_map/merge/pallas_call | solution.py:110
  28.4 8.0 %merge.4 = (bf16[2048,768]{1,0:T(8,128)(2,1)S(1)}, f32[1,768]{1,0:T(1,128)S(1)}) custom-call(bf16[3,2048,256]{2,1,0:T(8,128)(2,1)} %w_ref.1, bf16[3,96,2048]{2,1,0:T(8,128)(2,1)S(1)} %fusion.44.a_ref, bf16[3,96,256]{2,1,0:T(8,128)(2,1)S(1)} %constant_dynamic-update-slice_fusion.29.b_ref, f32[1,768]{1,0:T(1,128)S(1)} %reshape.496.m_ref), custom_call_target="tpu_custom_call" | custom-call | flops 301989888 | bytes 6291456 | tf_op jit(solution)/shard_map/merge/pallas_call | solution.py:110
  39.6 7.3 %merge_rows.1 = (bf16[2,2,704,2048]{3,2,1,0:T(8,128)(2,1)}, f32[2,704,1]{2,1,0:T(8,128)}) custom-call(bf16[2,704,2048]{2,1,0:T(8,128)(2,1)} %bitcast.449, bf16[2,96,2048]{2,1,0:T(8,128)(2,1)} %copy-done.56, bf16[2,96,704]{2,1,0:T(8,128)(2,1)} %copy-done.63, f32[2,704,1]{2,1,0:T(8,128)} %copy.76.m_ref), custom_call_target="tpu_custom_call" | custom-call | flops 553648128 | bytes 11534336 | tf_op jit(solution)/shard_map/merge_rows/pallas_call | solution.py:145
  52.1 6.4 all-to-all-start
  63.0 44.7 %all-to-all-done = bf16[8,256,256]{2,1,0:T(8,128)(2,1)S(1)} async-done(((bf16[8,256,256]{2,1,0:T(8,128)(2,1)}), bf16[8,256,256]{2,1,0:T(8,128)(2,1)S(1)}, u32[]{:S(2)}, u32[]{:S(2)}) %all-to-all-start) | async-done | bytes 1048608 | tf_op jit(solution)/shard_map/all_to_all | solution.py:757
  125.3 7.2 %collective-permute-done = bf16[1,128,2048]{2,1,0:T(8,128)(2,1)} collective-permute-done((bf16[1,128,2048]{2,1,0:T(8,128)(2,1)}, bf16[1,128,2048]{2,1,0:T(8,128)(2,1)}, u32[]{:S(2)}, u32[]{:S(2)}) %collective-permute-start) | collective-permute-done | bytes 524320 | tf_op jit(solution)/shard_map/ppermute | solution.py:49
  137.1 11.3 %all-to-all-done.1 = bf16[8,368,256]{2,1,0:T(8,128)(2,1)} async-done(((bf16[8,368,256]{2,1,0:T(8,128)(2,1)}), bf16[8,368,256]{2,1,0:T(8,128)(2,1)}, u32[]{:S(2)}, u32[]{:S(2)}) %all-to-all-start.1) | async-done | bytes 1507360 | tf_op jit(solution)/shard_map/all_to_all | solution.py:757
  154.0 10.5 %fusion.113.pre = f32[1792,768]{1,0:T(8,128)} fusion(bf16[1792,2048]{1,0:T(8,128)(2,1)} %all-gather.3.cloned.1.call-done.h_ref, bf16[2048,768]{1,0:T(8,128)(2,1)} %copy-done.2), kind=kOutput, calls=%fused_computation.422 | convolution fusion | flops 5637144576 | bytes 15990784 | tf_op jit(solution)/shard_map/dot_general | solution.py:32
  164.6 20.1 %attend.1 = (bf16[1792,256]{1,0:T(8,128)(2,1)S(1)}, bf16[1792,256]{1,0:T(8,128)(2,1)S(1)}, bf16[1792,256]{1,0:T(8,128)(2,1)S(1)}, bf16[1792,256]{1,0:T(8,128)(2,...) custom-call(f32[1792,768]{1,0:T(8,128)} %fusion.113.pre, f32[1792,128]{1,0:T(8,128)S(1)} %pad_maximum_fusion.7.cosine, ...), custom_call_target="tpu_custom_call" | custom-call | flops 1644167168 | bytes 13762560 | tf_op jit(solution)/shard_map/attend/pallas_call | solution.py:282
  205.5 5.4 fusion.7
  211.8 5.4 lay.4.into
  224.6 5.5 lay.5
  230.1 23.6 %collective-permute-done.8 = bf16[176,2048]{1,0:T(8,128)(2,1)} collective-permute-done((bf16[176,2048]{1,0:T(8,128)(2,1)}, bf16[176,2048]{1,0:T(8,128)(2,1)}, u32[]{:S(2)}, u32[]{:S(2)}) %collective-permute-start.8) | collective-permute-done | bytes 720928 | tf_op jit(solution)/shard_map/ppermute | solution.py:49
  257.6 5.6 fusion.30
  283.8 15.0 %collective-permute-done.15 = bf16[224,2048]{1,0:T(8,128)(2,1)S(1)} collective-permute-done((bf16[224,2048]{1,0:T(8,128)(2,1)S(1)}, bf16[224,2048]{1,0:T(8,128)(2,1)S(1)}, u32[]{:S(2)}, u32[]{:S(2)}) %collective-permute-start.15) | collective-permute-done | bytes 917536 | tf_op jit(solution)/shard_map/ppermute | solution.py:49
  302.9 4.8 lay.6.into
  310.9 4.8 lay.7
  315.7 29.5 %feed_forward.1 = (bf16[1408,896]{1,0:T(8,128)(2,1)}, bf16[2,2,704,896]{3,2,1,0:T(8,128)(2,1)}, f32[2,2,704,1]{3,2,1,0:T(8,128)}, bf16[896,2048]{1,0:T(8,128)(2,1)}, bf16[896,2048]{1,0:T(8,128)(2,1)}) custom-call(bf16[2,2,704,2048]{3,2,1,0:T(8,128)(2,1)} %bitcast.425, bf16[1408,2048]{1,0:T(8,128)(2,1)} %all-gather.5.cloned.1.call-done.down_ref, ...), custom_call_target="tpu_custom_call" | custom-call | flops 15502147584 | bytes 24641536 | tf_op jit(solution)/shard_map/feed_forward/pallas_call | solution.py:388
  345.2 15.5 %convolution_convert_fusion = bf16[896,2048]{1,0:T(8,128)(2,1)S(1)} fusion(bf16[2816,896]{1,0:T(8,128)(2,1)} %bitcast.441, bf16[2816,2048]{1,0:T(8,128)(2,1)} %bitcast.426), kind=kOutput, calls=%fused_computation.3 | convolution fusion | flops 10336600064 | bytes 20250624 | tf_op jit(solution)/shard_map/dot_general | solution.py:32
  373.5 8.4 %convolution_convert_fusion.1 = bf16[896,2048]{1,0:T(8,128)(2,1)S(1)} fusion(bf16[1408,896]{1,0:T(8,128)(2,1)S(1)} %copy-done.37, bf16[1408,2048]{1,0:T(8,128)(2,1)} %all-gather.5.cloned.1.call-done.down_ref), kind=kOutput, calls=%fused_computation.4 | convolution fusion | flops 5169217536 | bytes 11960320 | tf_op jit(solution)/shard_map/dot_general | solution.py:32
  388.4 7.6 %collective-permute-done.20 = bf16[224,2048]{1,0:T(8,128)(2,1)S(1)} collective-permute-done((bf16[224,2048]{1,0:T(8,128)(2,1)S(1)}, bf16[224,2048]{1,0:T(8,128)(2,1)S(1)}, u32[]{:S(2)}, u32[]{:S(2)}) %collective-permute-start.20) | collective-permute-done | bytes 917536 | tf_op jit(solution)/shard_map/ppermute | solution.py:49
  412.8 7.0 %fusion.2 = f32[32,2816]{1,0:T(8,128)} fusion(bf16[2816,896]{1,0:T(8,128)(2,1)} %bitcast.442, bf16[896,2048]{1,0:T(8,128)(2,1)} %get-tuple-element.185, bf16[32,2048]{1,0:T(8,128)(2,1)S(1)} %bitcast.469, f32[32,2816]{1,0:T(8,128)S(1)} %convolution_bitcast_fusion, f32[2816]{0:T(1024)S(1)} %get-tuple-element.300, f32[2816]{0:T(1024)S(1)} %get-tuple-element.301, ...), kind=kOutput, calls=%fused_computation.8 | convolution fusion | flops 280662016 | bytes 9616416 | tf_op jit(solution)/shard_map/dot_general | solution.py:32
  439.4 17.7 %attend_back.1 = (bf16[1792,768]{1,0:T(8,128)(2,1)}, f32[8,768]{1,0:T(8,128)S(1)}) custom-call(bf16[1792,256]{1,0:T(8,128)(2,1)S(1)} %copy-done.7, bf16[1792,256]{1,0:T(8,128)(2,1)S(1)} %copy-done.9, bf16[1792,256]{1,0:T(8,128)(2,1)S(1)} %copy-done.11, f32[1792,768]{1,0:T(8,128)} %fusion.113.pre, f32[1792,128]{1,0:T(8,128)S(1)} %pad_maximum_fusion.7.cosine, ...), custom_call_target="tpu_custom_call" | custom-call | flops 4110417920 | bytes 18350080 | tf_op jit(solution)/shard_map/attend_back/pallas_call | solution.py:319
  460.1 19.4 %back_qkv.1 = (bf16[4,224,2048]{2,1,0:T(8,128)(2,1)}, bf16[4,224,2048]{2,1,0:T(8,128)(2,1)}, f32[48,2048]{1,0:T(8,128)}, f32[48,768]{1,0:T(8,128)}, f32[1,2048]{1,0:T(1,128)}, /*index=5*/f32[1,768]{1,0:T(1,128)}) custom-call(s32[1]{0:T(128)} %bitcast.130.core, bf16[1792,768]{1,0:T(8,128)(2,1)} %get-tuple-element.162.g_ref, ...), custom_call_target="tpu_custom_call" | custom-call | flops 8455716864 | bytes 29360128 | tf_op jit(solution)/shard_map/back_qkv/pallas_call | solution.py:477
  488.2 5.1 add_convert_fusion
  504.5 6.5 constant_dynamic-update-slice_fusion.67
  518.7 6.5 %fusion.114 = f32[32,2048]{1,0:T(8,128)S(1)} fusion(bf16[32,2816]{1,0:T(8,128)(2,1)S(1)} %get-tuple-element.186, bf16[2816,2048]{1,0:T(8,128)(2,1)} %bitcast.427), kind=kOutput, calls=%fused_computation.423 | convolution fusion | flops 369098752 | bytes 11976704 | tf_op jit(solution)/shard_map/dot_general | solution.py:32
  545.9 5.3 collective-permute-start.28
  558.2 12.6 %collective-permute-done.28 = bf16[224,2048]{1,0:T(8,128)(2,1)} collective-permute-done((bf16[224,2048]{1,0:T(8,128)(2,1)}, bf16[224,2048]{1,0:T(8,128)(2,1)}, u32[]{:S(2)}, u32[]{:S(2)}) %collective-permute-start.28) | collective-permute-done | bytes 917536 | tf_op jit(solution)/shard_map/ppermute | solution.py:542
  594.5 4.7 collective-permute-done.38
  610.9 4.9 collective-permute-done.42
  616.1 10.6 %collective-permute-done.40 = bf16[224,2048]{1,0:T(8,128)(2,1)S(1)} collective-permute-done((bf16[224,2048]{1,0:T(8,128)(2,1)S(1)}, bf16[224,2048]{1,0:T(8,128)(2,1)S(1)}, u32[]{:S(2)}, u32[]{:S(2)}) %collective-permute-start.40) | collective-permute-done | bytes 917536 | tf_op jit(solution)/shard_map/ppermute | solution.py:542
  (616 shorter events, 277.7 us)
Async XLA Ops:
  7.2 143.9 %all-gather.3.cloned.1.call-start = ((), (), s32[]{:S(2)}) async-start(), calls=%async_computation.4 | async-start | bytes 8257536 | tf_op jit(solution)/shard_map/all_gather | solution.py:716
  52.1 55.6 %all-to-all-start = ((bf16[8,256,256]{2,1,0:T(8,128)(2,1)}), bf16[8,256,256]{2,1,0:T(8,128)(2,1)S(1)}, u32[]{:S(2)}, u32[]{:S(2)}) async-start(bf16[8,256,256]{2,1,0:T(8,128)(2,1)} %bitcast.29), calls=%async_computation | async-start | bytes 2097152 | tf_op jit(solution)/shard_map/all_to_all | solution.py:757
  107.6 40.7 %all-to-all-start.1 = ((bf16[8,368,256]{2,1,0:T(8,128)(2,1)}), bf16[8,368,256]{2,1,0:T(8,128)(2,1)}, u32[]{:S(2)}, u32[]{:S(2)}) async-start(bf16[8,368,256]{2,1,0:T(8,128)(2,1)} %pad_maximum_fusion.3), calls=%async_computation.1 | async-start | bytes 3014656 | tf_op jit(solution)/shard_map/all_to_all | solution.py:757
  111.9 203.7 %all-gather.5.cloned.1.call-start = ((), (), s32[]{:S(2)}) async-start(), calls=%async_computation.5 | async-start | bytes 7208960 | tf_op jit(solution)/shard_map/all_gather | solution.py:808
  151.1 38.0 %collective-permute-start.4 = (bf16[176,2048]{1,0:T(8,128)(2,1)}, bf16[176,2048]{1,0:T(8,128)(2,1)}, u32[]{:S(2)}, u32[]{:S(2)}) collective-permute-start(bf16[176,2048]{1,0:T(8,128)(2,1)} %get-tuple-element.123), channel_id=1, source_target_pairs={{0,4},{1,5},{2,6},{3,7},{4,0},{5,1},{6,2},{7,3},{8,12},{9,13},{10,... | collective-permute-start | bytes 2162696 | tf_op jit(solution)/shard_map/ppermute | solution.py:49
  151.1 34.7 %collective-permute-start.2 = (bf16[2,128,2048]{2,1,0:T(8,128)(2,1)}, bf16[2,128,2048]{2,1,0:T(8,128)(2,1)S(1)}, u32[]{:S(2)}, u32[]{:S(2)}) collective-permute-start(bf16[2,128,2048]{2,1,0:T(8,128)(2,1)} %pad_maximum_fusion.5), channel_id=1, source_target_pairs={{0,16},{8,24},{16,0},{24,8},{1,17},{9,25},{17,1},{25,9},{2,18},{10... | collective-permute-start | bytes 3145736 | tf_op jit(solution)/shard_map/ppermute | solution.py:49
  152.6 35.4 %collective-permute-start.3 = (bf16[2,128,2048]{2,1,0:T(8,128)(2,1)}, bf16[2,128,2048]{2,1,0:T(8,128)(2,1)S(1)}, u32[]{:S(2)}, u32[]{:S(2)}) collective-permute-start(bf16[2,128,2048]{2,1,0:T(8,128)(2,1)} %pad_maximum_fusion.6), channel_id=1, source_target_pairs={{0,8},{8,0},{16,24},{24,16},{1,9},{9,1},{17,25},{25,17},{2,10},{10... | collective-permute-start | bytes 3145736 | tf_op jit(solution)/shard_map/ppermute | solution.py:49
  189.1 35.5 %collective-permute-start.5 = (bf16[8,128,2048]{2,1,0:T(8,128)(2,1)}, bf16[8,128,2048]{2,1,0:T(8,128)(2,1)}, u32[]{:S(2)}, u32[]{:S(2)}) collective-permute-start(bf16[8,128,2048]{2,1,0:T(8,128)(2,1)} %constant_dynamic-update-slice_fusion.46.one.two), channel_id=1, source_target_pairs={{0,1},{1,0},{2,3},{3,2},{4,5},{5,4},{6,7},{7,6},{8,9},{9,8},{10,11... | collective-permute-start | bytes 12582920 | tf_op jit(solution)/shard_map/ppermute | solution.py:49
  194.1 59.5 %all-to-all-start.2 = ((bf16[8,224,256]{2,1,0:T(8,128)(2,1)}), bf16[8,224,256]{2,1,0:T(8,128)(2,1)}, u32[]{:S(2)}, u32[]{:S(2)}) async-start(bf16[8,224,256]{2,1,0:T(8,128)(2,1)} %bitcast.37), calls=%async_computation.2 | async-start | bytes 1835008 | tf_op jit(solution)/shard_map/all_to_all | solution.py:822
  201.4 19.1 %collective-permute-start.7 = (bf16[1,88,2048]{2,1,0:T(8,128)(2,1)}, bf16[1,88,2048]{2,1,0:T(8,128)(2,1)}, u32[]{:S(2)}, u32[]{:S(2)}) collective-permute-start(bf16[1,88,2048]{2,1,0:T(8,128)(2,1)} %get-tuple-element.271), channel_id=1, source_target_pairs={{0,16},{8,24},{16,0},{24,8},{1,17},{9,25},{17,1},{25,9},{2,18},{10... | collective-permute-start | bytes 1081352 | tf_op jit(solution)/shard_map/ppermute | solution.py:49
  202.0 20.5 %collective-permute-start.6 = (bf16[1,88,2048]{2,1,0:T(8,128)(2,1)}, bf16[1,88,2048]{2,1,0:T(8,128)(2,1)}, u32[]{:S(2)}, u32[]{:S(2)}) collective-permute-start(bf16[1,88,2048]{2,1,0:T(8,128)(2,1)} %get-tuple-element.272), channel_id=1, source_target_pairs={{0,8},{8,0},{16,24},{24,16},{1,9},{9,1},{17,25},{25,17},{2,10},{10... | collective-permute-start | bytes 1081352 | tf_op jit(solution)/shard_map/ppermute | solution.py:49
  202.6 51.1 %collective-permute-start.8 = (bf16[176,2048]{1,0:T(8,128)(2,1)}, bf16[176,2048]{1,0:T(8,128)(2,1)}, u32[]{:S(2)}, u32[]{:S(2)}) collective-permute-start(bf16[176,2048]{1,0:T(8,128)(2,1)} %get-tuple-element.129), channel_id=1, source_target_pairs={{0,4},{1,5},{2,6},{3,7},{4,0},{5,1},{6,2},{7,3},{8,12},{9,13},{10,... | collective-permute-start | bytes 2162696 | tf_op jit(solution)/shard_map/ppermute | solution.py:49
  257.6 23.3 %collective-permute-start.17 = (bf16[224,2048]{1,0:T(8,128)(2,1)S(1)}, bf16[224,2048]{1,0:T(8,128)(2,1)S(1)}, u32[]{:S(2)}, u32[]{:S(2)}) collective-permute-start(bf16[224,2048]{1,0:T(8,128)(2,1)S(1)} %fusion.27), channel_id=1, source_target_pairs={{0,2},{1,3},{2,0},{3,1},{4,6},{5,7},{6,4},{7,5},{8,10},{9,11},{10,... | collective-permute-start | bytes 2752520 | tf_op jit(solution)/shard_map/ppermute | solution.py:49
  271.9 26.9 %collective-permute-start.15 = (bf16[224,2048]{1,0:T(8,128)(2,1)S(1)}, bf16[224,2048]{1,0:T(8,128)(2,1)S(1)}, u32[]{:S(2)}, u32[]{:S(2)}) collective-permute-start(bf16[224,2048]{1,0:T(8,128)(2,1)S(1)} %get-tuple-element.133), channel_id=1, source_target_pairs={{0,2},{1,3},{2,0},{3,1},{4,6},{5,7},{6,4},{7,5},{8,10},{9,11},{10,... | collective-permute-start | bytes 2752520 | tf_op jit(solution)/shard_map/ppermute | solution.py:49
  273.4 26.4 %collective-permute-start.13 = (bf16[2,88,2048]{2,1,0:T(8,128)(2,1)S(1)}, bf16[2,88,2048]{2,1,0:T(8,128)(2,1)S(1)}, u32[]{:S(2)}, u32[]{:S(2)}) collective-permute-start(bf16[2,88,2048]{2,1,0:T(8,128)(2,1)S(1)} %copy-done.51), channel_id=1, source_target_pairs={{0,16},{8,24},{16,0},{24,8},{1,17},{9,25},{17,1},{25,9},{2,18},{10... | collective-permute-start | bytes 2162696 | tf_op jit(solution)/shard_map/ppermute | solution.py:49
  273.9 27.1 %collective-permute-start.14 = (bf16[2,88,2048]{2,1,0:T(8,128)(2,1)S(1)}, bf16[2,88,2048]{2,1,0:T(8,128)(2,1)S(1)}, u32[]{:S(2)}, u32[]{:S(2)}) collective-permute-start(bf16[2,88,2048]{2,1,0:T(8,128)(2,1)S(1)} %copy-done.50), channel_id=1, source_target_pairs={{0,8},{8,0},{16,24},{24,16},{1,9},{9,1},{17,25},{25,17},{2,10},{10... | collective-permute-start | bytes 2162696 | tf_op jit(solution)/shard_map/ppermute | solution.py:49
  275.4 32.4 %collective-permute-start.11 = (bf16[2,88,2048]{2,1,0:T(8,128)(2,1)}, bf16[2,88,2048]{2,1,0:T(8,128)(2,1)}, u32[]{:S(2)}, u32[]{:S(2)}) collective-permute-start(bf16[2,88,2048]{2,1,0:T(8,128)(2,1)} %pad_maximum_fusion.11), channel_id=1, source_target_pairs={{0,16},{8,24},{16,0},{24,8},{1,17},{9,25},{17,1},{25,9},{2,18},{10... | collective-permute-start | bytes 2162696 | tf_op jit(solution)/shard_map/ppermute | solution.py:49
  280.9 26.8 %collective-permute-start.12 = (bf16[2,88,2048]{2,1,0:T(8,128)(2,1)}, bf16[2,88,2048]{2,1,0:T(8,128)(2,1)}, u32[]{:S(2)}, u32[]{:S(2)}) collective-permute-start(bf16[2,88,2048]{2,1,0:T(8,128)(2,1)} %pad_maximum_fusion.12), channel_id=1, source_target_pairs={{0,8},{8,0},{16,24},{24,16},{1,9},{9,1},{17,25},{25,17},{2,10},{10... | collective-permute-start | bytes 2162696 | tf_op jit(solution)/shard_map/ppermute | solution.py:49
  373.2 22.8 %collective-permute-start.20 = (bf16[224,2048]{1,0:T(8,128)(2,1)S(1)}, bf16[224,2048]{1,0:T(8,128)(2,1)S(1)}, u32[]{:S(2)}, u32[]{:S(2)}) collective-permute-start(bf16[224,2048]{1,0:T(8,128)(2,1)S(1)} %slice.503), channel_id=1, source_target_pairs={{0,2},{1,3},{2,0},{3,1},{4,6},{5,7},{6,4},{7,5},{8,10},{9,11},{10,... | collective-permute-start | bytes 2752520 | tf_op jit(solution)/shard_map/ppermute | solution.py:49
  406.1 19.6 %collective-permute-start.21 = (bf16[448,2048]{1,0:T(8,128)(2,1)}, bf16[448,2048]{1,0:T(8,128)(2,1)}, u32[]{:S(2)}, u32[]{:S(2)}) collective-permute-start(bf16[448,2048]{1,0:T(8,128)(2,1)} %slice.308), channel_id=1, source_target_pairs={{0,1},{1,0},{2,3},{3,2},{4,5},{5,4},{6,7},{7,6},{8,9},{9,8},{10,11... | collective-permute-start | bytes 5505032 | tf_op jit(solution)/shard_map/ppermute | solution.py:49
  407.0 28.9 %all-to-all-start.3 = ((bf16[8,224,256]{2,1,0:T(8,128)(2,1)}), bf16[8,224,256]{2,1,0:T(8,128)(2,1)S(1)}, u32[]{:S(2)}, u32[]{:S(2)}) async-start(bf16[8,224,256]{2,1,0:T(8,128)(2,1)} %bitcast.451), calls=%async_computation.3 | async-start | bytes 1835008 | tf_op jit(solution)/shard_map/all_to_all | solution.py:892
  429.7 27.4 %collective-permute-start.22 = (bf16[224,2048]{1,0:T(8,128)(2,1)}, bf16[224,2048]{1,0:T(8,128)(2,1)}, u32[]{:S(2)}, u32[]{:S(2)}) collective-permute-start(bf16[224,2048]{1,0:T(8,128)(2,1)} %slice.502), channel_id=1, source_target_pairs={{0,2},{1,3},{2,0},{3,1},{4,6},{5,7},{6,4},{7,5},{8,10},{9,11},{10,... | collective-permute-start | bytes 2752520 | tf_op jit(solution)/shard_map/ppermute | solution.py:49
  460.0 28.2 %collective-permute-start.24 = (f32[2048]{0:T(1024)S(1)}, f32[2048]{0:T(1024)S(1)}, u32[]{:S(2)}, u32[]{:S(2)}) collective-permute-start(f32[2048]{0:T(1024)S(1)} %get-tuple-element.310), channel_id=1, source_target_pairs={{0,1},{1,0},{2,3},{3,2},{4,5},{5,4},{6,7},{7,6},{8,9},{9,8},{10,11... | collective-permute-start | bytes 24584 | tf_op jit(solution)/shard_map/ppermute | solution.py:49
  495.1 23.6 %collective-permute-start.25 = (bf16[224,2048]{1,0:T(8,128)(2,1)}, bf16[224,2048]{1,0:T(8,128)(2,1)}, u32[]{:S(2)}, u32[]{:S(2)}) collective-permute-start(bf16[224,2048]{1,0:T(8,128)(2,1)} %get-tuple-element.168), channel_id=1, source_target_pairs={{0,2},{1,3},{8,10},{9,11},{16,18},{17,19},{24,26},{25,27}} | collective-permute-start | bytes 2752520 | tf_op jit(solution)/shard_map/ppermute | solution.py:542
  499.8 18.9 %collective-permute-start.26 = (bf16[224,2048]{1,0:T(8,128)(2,1)}, bf16[224,2048]{1,0:T(8,128)(2,1)}, u32[]{:S(2)}, u32[]{:S(2)}) collective-permute-start(bf16[224,2048]{1,0:T(8,128)(2,1)} %get-tuple-element.169), channel_id=1, source_target_pairs={{6,4},{7,5},{14,12},{15,13},{22,20},{23,21},{30,28},{31,29}} | collective-permute-start | bytes 2752520 | tf_op jit(solution)/shard_map/ppermute | solution.py:542
  545.9 24.9 %collective-permute-start.28 = (bf16[224,2048]{1,0:T(8,128)(2,1)}, bf16[224,2048]{1,0:T(8,128)(2,1)}, u32[]{:S(2)}, u32[]{:S(2)}) collective-permute-start(bf16[224,2048]{1,0:T(8,128)(2,1)} %get-tuple-element.180), channel_id=1, source_target_pairs={{0,2},{1,3},{2,4},{3,5},{8,10},{9,11},{10,12},{11,13},{16,18},{17,... | collective-permute-start | bytes 2752520 | tf_op jit(solution)/shard_map/ppermute | solution.py:542
  551.3 19.6 %collective-permute-start.29 = (bf16[224,2048]{1,0:T(8,128)(2,1)}, bf16[224,2048]{1,0:T(8,128)(2,1)}, u32[]{:S(2)}, u32[]{:S(2)}) collective-permute-start(bf16[224,2048]{1,0:T(8,128)(2,1)} %get-tuple-element.181), channel_id=1, source_target_pairs={{4,2},{5,3},{6,4},{7,5},{12,10},{13,11},{14,12},{15,13},{20,18},{2... | collective-permute-start | bytes 2752520 | tf_op jit(solution)/shard_map/ppermute | solution.py:542
  556.2 17.7 %collective-permute-start.33 = (f32[16,5632]{1,0:T(8,128)S(1)}, f32[16,5632]{1,0:T(8,128)S(1)}, u32[]{:S(2)}, u32[]{:S(2)}) collective-permute-start(f32[16,5632]{1,0:T(8,128)S(1)} %get-tuple-element.260), channel_id=1, source_target_pairs={{0,24},{8,16},{16,8},{24,0},{1,25},{9,17},{17,9},{25,1},{2,26},{10... | collective-permute-start | bytes 1081352 | tf_op jit(solution)/shard_map/ppermute | solution.py:49
  557.7 17.7 %collective-permute-start.32 = (f32[16,5632]{1,0:T(8,128)S(1)}, f32[16,5632]{1,0:T(8,128)}, u32[]{:S(2)}, u32[]{:S(2)}) collective-permute-start(f32[16,5632]{1,0:T(8,128)S(1)} %get-tuple-element.261), channel_id=1, source_target_pairs={{0,16},{8,24},{16,0},{24,8},{1,17},{9,25},{17,1},{25,9},{2,18},{10... | collective-permute-start | bytes 1081352 | tf_op jit(solution)/shard_map/ppermute | solution.py:49
  605.8 20.9 %collective-permute-start.40 = (bf16[224,2048]{1,0:T(8,128)(2,1)S(1)}, bf16[224,2048]{1,0:T(8,128)(2,1)S(1)}, u32[]{:S(2)}, u32[]{:S(2)}) collective-permute-start(bf16[224,2048]{1,0:T(8,128)(2,1)S(1)} %get-tuple-element.198), channel_id=1, source_target_pairs={{0,2},{1,3},{2,4},{3,5},{4,6},{5,7},{8,10},{9,11},{10,12},{11,13},... | collective-permute-start | bytes 2752520 | tf_op jit(solution)/shard_map/ppermute | solution.py:542
  609.5 21.3 %collective-permute-start.41 = (bf16[224,2048]{1,0:T(8,128)(2,1)S(1)}, bf16[224,2048]{1,0:T(8,128)(2,1)S(1)}, u32[]{:S(2)}, u32[]{:S(2)}) collective-permute-start(bf16[224,2048]{1,0:T(8,128)(2,1)S(1)} %get-tuple-element.199), channel_id=1, source_target_pairs={{2,0},{3,1},{4,2},{5,3},{6,4},{7,5},{10,8},{11,9},{12,10},{13,11},... | collective-permute-start | bytes 2752520 | tf_op jit(solution)/shard_map/ppermute | solution.py:542
  615.9 17.9 %collective-permute-start.45 = (f32[16,22528]{1,0:T(8,128)S(1)}, f32[16,22528]{1,0:T(8,128)S(1)}, u32[]{:S(2)}, u32[]{:S(2)}) collective-permute-start(f32[16,22528]{1,0:T(8,128)S(1)} %constant_dynamic-update-slice_fusion.76), channel_id=1, source_target_pairs={{0,1},{1,0},{2,3},{3,2},{4,5},{5,4},{6,7},{7,6},{8,9},{9,8},{10,11... | collective-permute-start | bytes 4325384 | tf_op jit(solution)/shard_map/ppermute | solution.py:49
  (133 other events, 1610.4 us)
Sparse Core Ops, SparseCore 0:
  11.4 98.3 all-gather.2
  190.2 75.6 all-gather.4
